TPU v7x, 128 devices: a whole 4x4x4 slice. The times are simulated.
128 devices in a mesh: region: 16 (over y, x), slab: 8 (over z, core).
Axes of the slice: x: 4, y: 4, z: 4, core: 2. Of those that a mesh axis runs over, the one named last changes fastest.
Arguments:
- volume: bfloat16 [65536, 1024], P(('region', 'slab')), may hold values from -40 to 40
- patches: bfloat16 [65536, 1024], P(('region', 'slab')), may hold values from -6 to 6
- requests: int32 [128, 16, 1], P(('region', 'slab')), may hold values from 0 to 3
- lists: int32 [512, 4], P(('region', 'slab')), may hold values from 0 to 15, all different within a row
- counts: int32 [512], P(('region', 'slab')), may hold values from 1 to 4, 1536 in all
- w_query: bfloat16 [1024, 1024], replicated, may hold values from -0.1875 to 0.1875
- key_weight: bfloat16 [1024, 1024], replicated, may hold values from -0.1875 to 0.1875
- value_weight: bfloat16 [1024, 1024], replicated, may hold values from -0.1875 to 0.1875
- w_out: bfloat16 [1024, 1024], replicated, may hold values from -0.1875 to 0.1875
- cotangent: bfloat16 [65536, 1024], P(('region', 'slab')), may hold values from -6 to 6
Outputs:
- mixed: bfloat16 [65536, 1024], P(('region', 'slab'))
- grad_volume: bfloat16 [65536, 1024], P(('region', 'slab'))
- grad_patches: bfloat16 [65536, 1024], P(('region', 'slab'))
- grad_out_weight: float32 [1024, 1024], replicated
Inputs may be any that keep to these rules, and one draw needn't show every extreme that they name: `lists`: each row names 4 different received slots.
All inputs are finite; a program needn't handle non-finite values. No bound on the sum of `counts` on one device may be relied on, other than what follows from the above.
Results may differ from a plain program's by a relative error of at most 0.015.
The roundings to bfloat16 on the way count: a program that leaves them out, or rounds other values in their place, can miss the bound.
Values may be sent and summed in bfloat16 or wider, within the bound.
No kernel may reach another device: no remote copies, remote signals or barrier semaphores. Data moves between devices by JAX's collectives and lax.ppermute only.
A program may use at most 192 MiB of HBM per device.

v0:
```python
import jax
import jax.numpy as jnp
from jax import lax
from jax.sharding import PartitionSpec as P

HEADS = 16
BLOCK = 128


def per_device(
    volume, patches, requests, lists, counts, w_query, key_weight, value_weight, w_out, cotangent
):
    single_float = jnp.float32
    bf16 = jnp.bfloat16
    width = volume.shape[1]
    group_count_total = lists.shape[0]
    listed = lists.shape[1]
    per_group = volume.shape[0] // group_count_total
    head_dim = width // HEADS
    scale = head_dim ** (-0.5)
    owned_count = patches.shape[0] // BLOCK
    asked = lax.all_to_all(requests, "region", split_axis=1, concat_axis=0, tiled=True)
    asked = asked.reshape(asked.shape[0], asked.shape[2])
    peers = asked.shape[0]
    capacity = asked.shape[1]
    slot_count = peers * capacity
    outgoing = patches.reshape(owned_count, BLOCK, width)[asked]
    blocks = lax.all_to_all(outgoing, "region", split_axis=0, concat_axis=0, tiled=True)
    slot_keys = jnp.einsum(
        "pcnd,de->pcne", blocks, key_weight, preferred_element_type=single_float
    ).astype(bf16)
    slot_vals = jnp.einsum(
        "pcnd,de->pcne", blocks, value_weight, preferred_element_type=single_float
    ).astype(bf16)
    keys = slot_keys
    vals = slot_vals
    keys = keys.reshape(slot_count, BLOCK, width)
    vals = vals.reshape(slot_count, BLOCK, width)
    query = jnp.dot(volume, w_query, preferred_element_type=single_float).astype(bf16)
    query_heads = query.reshape(group_count_total, per_group, HEADS, head_dim)
    key_heads = keys[lists].reshape(group_count_total, listed * BLOCK, HEADS, head_dim)
    value_heads = vals[lists].reshape(group_count_total, listed * BLOCK, HEADS, head_dim)
    scores = (
        jnp.einsum("gqhd,gkhd->ghqk", query_heads, key_heads, preferred_element_type=single_float)
        * scale
    )
    position = jnp.arange(listed * BLOCK, dtype=jnp.int32) // BLOCK
    live = position[None, :] < counts[:, None]
    scores = jnp.where(live[:, None, None, :], scores, -1e30)
    top = jnp.max(scores, axis=-1, keepdims=True)
    expd = jnp.exp(scores - top)
    probs = expd / jnp.sum(expd, axis=-1, keepdims=True)
    probs_b = probs.astype(bf16)
    attended = jnp.einsum(
        "ghqk,gkhd->gqhd", probs_b, value_heads, preferred_element_type=single_float
    ).astype(bf16)
    flat = attended.reshape(group_count_total * per_group, width)
    mixed = jnp.dot(flat, w_out, preferred_element_type=single_float).astype(bf16)
    out_terms = jnp.einsum("td,te->de", flat, cotangent, preferred_element_type=single_float)
    grad_out_weight = lax.psum(out_terms, ("region", "slab"))
    grad_att = jnp.einsum(
        "te,de->td", cotangent, w_out, preferred_element_type=single_float
    ).astype(bf16)
    grad_att_heads = grad_att.reshape(group_count_total, per_group, HEADS, head_dim)
    grad_prob = jnp.einsum(
        "gqhd,gkhd->ghqk", grad_att_heads, value_heads, preferred_element_type=single_float
    )
    grad_score = (
        probs * (grad_prob - jnp.sum(probs * grad_prob, axis=-1, keepdims=True)) * scale
    ).astype(bf16)
    grad_query = jnp.einsum(
        "ghqk,gkhd->gqhd", grad_score, key_heads, preferred_element_type=single_float
    ).astype(bf16)
    grad_volume = jnp.einsum(
        "te,de->td",
        grad_query.reshape(group_count_total * per_group, width),
        w_query,
        preferred_element_type=single_float,
    ).astype(bf16)
    grad_key_list = jnp.einsum(
        "ghqk,gqhd->gkhd", grad_score, query_heads, preferred_element_type=single_float
    ).reshape(group_count_total * listed, BLOCK, width)
    grad_value_list = jnp.einsum(
        "ghqk,gqhd->gkhd", probs_b, grad_att_heads, preferred_element_type=single_float
    ).reshape(group_count_total * listed, BLOCK, width)
    flat_lists = lists.reshape(-1)
    slot_key_gradient = (
        jnp.zeros((slot_count, BLOCK, width), single_float)
        .at[flat_lists]
        .add(grad_key_list)
        .astype(bf16)
    )
    slot_value_gradient = (
        jnp.zeros((slot_count, BLOCK, width), single_float)
        .at[flat_lists]
        .add(grad_value_list)
        .astype(bf16)
    )
    slot_grads = jnp.einsum(
        "ipa,fa->ipf", slot_key_gradient, key_weight, preferred_element_type=single_float
    ) + jnp.einsum(
        "ipa,fa->ipf", slot_value_gradient, value_weight, preferred_element_type=single_float
    )
    returned = lax.all_to_all(
        slot_grads.reshape(peers, capacity, BLOCK, width),
        "region",
        split_axis=0,
        concat_axis=0,
        tiled=True,
    )
    block_grads = (
        jnp.zeros((owned_count, BLOCK, width), single_float)
        .at[asked.reshape(-1)]
        .add(returned.reshape(slot_count, BLOCK, width))
    )
    grad_patches = block_grads.reshape(owned_count * BLOCK, width).astype(bf16)
    return (mixed, grad_volume, grad_patches, grad_out_weight)


def solution(mesh):
    in_specs = (
        P(("region", "slab"), None),
        P(("region", "slab"), None),
        P(("region", "slab"), None, None),
        P(("region", "slab"), None),
        P(("region", "slab")),
        P(),
        P(),
        P(),
        P(),
        P(("region", "slab"), None),
    )
    out_specs = (
        P(("region", "slab"), None),
        P(("region", "slab"), None),
        P(("region", "slab"), None),
        P(),
    )
    return jax.shard_map(
        per_device, mesh=mesh, in_specs=in_specs, out_specs=out_specs, check_vma=False
    )
```

profile of v0, /device:TPU:1, one launch (start us, length us, event | category | flops | bytes accessed | tf_op | source)
XLA Modules:
  0.0 639.6 jit_solution(16628964600789055485)
XLA Ops:
  7.2 0.9 copy.76
  8.1 13.8 %all_to_all.19 = s32[1,16,1]{2,0,1:T(1,128)S(1)} all-to-all(s32[1,16,1]{2,0,1:T(1,128)S(1)} %copy.76), channel_id=1, replica_groups=mesh['region'=16,'slab'=8] {'region'}, dimensions={1} | all-to-all | bytes 128 | tf_op jit(solution)/shard_map/all_to_all | solution.py:22
  21.8 0.4 reduce
  22.3 4.1 gather_fusion
  26.3 4.5 all-to-all-start.1
  31.1 3.2 convolution_convert_fusion.3
  34.2 2.4 reshape.274
  36.6 3.5 copy.80
  40.1 3.2 convolution_convert_fusion.1
  43.3 2.4 reshape.276
  45.7 2.8 copy.85
  48.7 41.4 %all-to-all-done.1 = bf16[16,1,128,1024]{3,2,1,0:T(8,128)(2,1)} async-done(((bf16[16,1,128,1024]{3,2,1,0:T(8,128)(2,1)}), bf16[16,1,128,1024]{3,2,1,0:T(8,128)(2,1)}, u32[]{:S(2)}, u32[]{:S(2)}) %all-to-all-start.1) | async-done | bytes 4194336 | tf_op jit(solution)/shard_map/all_to_all | solution.py:28
  90.0 8.2 %fusion.35 = bf16[16,128,1024]{2,1,0:T(8,128)(2,1)} fusion(bf16[16,1,128,1024]{3,2,1,0:T(8,128)(2,1)} %all-to-all-done.1, bf16[1024,1024]{1,0:T(8,128)(2,1)S(1)} %copy-done), kind=kOutput, calls=%fused_computation.35 | convolution fusion | flops 4297064448 | bytes 10485760 | tf_op jit(solution)/shard_map/pcnd,de->pcne/dot_general | solution.py:32
  98.3 5.0 gather_fusion.1
  103.2 9.4 %fusion.38 = bf16[16,128,1024]{2,1,0:T(8,128)(2,1)} fusion(bf16[16,1,128,1024]{3,2,1,0:T(8,128)(2,1)} %all-to-all-done.1, bf16[1024,1024]{1,0:T(8,128)(2,1)} %param.16), kind=kOutput, calls=%fused_computation.36 | convolution fusion | flops 4297064448 | bytes 10485760 | tf_op jit(solution)/shard_map/pcnd,de->pcne/dot_general | solution.py:29
  112.6 5.0 gather_fusion.2
  117.6 12.0 %reshape.275 = bf16[4,512,16,64]{3,2,1,0:T(8,128)(2,1)} reshape(bf16[16,128,1024]{2,1,0:T(8,128)(2,1)} %gather_fusion.2) | data formatting | bytes 8388608 | tf_op jit(solution)/shard_map/reshape | solution.py:41
  129.6 9.8 %copy.81 = bf16[4,512,16,64]{1,3,2,0:T(8,128)(2,1)} copy(bf16[4,512,16,64]{3,2,1,0:T(8,128)(2,1)} %reshape.275) | data formatting | bytes 8388608 | tf_op jit(solution)/shard_map/reshape | solution.py:41
  139.4 11.6 %reshape.273 = bf16[4,512,16,64]{3,2,1,0:T(8,128)(2,1)} reshape(bf16[16,128,1024]{2,1,0:T(8,128)(2,1)} %gather_fusion.1) | data formatting | bytes 8388608 | tf_op jit(solution)/shard_map/reshape | solution.py:42
  150.9 9.7 %copy.82 = bf16[4,512,16,64]{1,3,2,0:T(8,128)(2,1)} copy(bf16[4,512,16,64]{3,2,1,0:T(8,128)(2,1)} %reshape.273) | data formatting | bytes 8388608 | tf_op jit(solution)/shard_map/reshape | solution.py:42
  160.7 10.3 %fusion.79 = f32[4,16,128,512]{3,2,1,0:T(8,128)} fusion(bf16[4,128,16,64]{1,3,2,0:T(8,128)(2,1)S(1)} %copy.85, bf16[4,512,16,64]{1,3,2,0:T(8,128)(2,1)} %copy.82), kind=kOutput, calls=%fused_computation.81 | convolution fusion | flops 536870912 | bytes 22020096 | tf_op jit(solution)/shard_map/gqhd,gkhd->ghqk/dot_general | solution.py:65
  171.0 10.8 %fusion.78 = (f32[4,16,128]{2,1,0:T(8,128)S(1)}, f32[4,16,128,512]{3,2,1,0:T(8,128)}) fusion(pred[4,512]{1,0:T(4,128)(4,1)S(1)} %broadcast_compare_fusion, bf16[4,128,16,64]{1,3,2,0:T(8,128)(2,1)} %copy.80, bf16[4,512,16,64]{1,3,2,0:T(8,128)(2,1)} %copy.81), kind=kOutput, calls=%fused_computation.80 | convolution fusion | flops 553648640 | bytes 22054912 | tf_op jit(solution)/shard_map/sub | solution.py:51
  181.8 9.9 %fusion.27 = f32[4,512,16,64]{1,3,2,0:T(8,128)} fusion(bf16[4,128,16,64]{1,3,2,0:T(8,128)(2,1)S(1)} %copy.85, f32[4,16,128,512]{3,2,1,0:T(8,128)} %get-tuple-element.5, f32[4,16,128]{2,1,0:T(8,128)S(1)} %get-tuple-element.4), kind=kOutput, calls=%fused_computation.33 | convolution fusion | flops 545259520 | bytes 26247168 | tf_op jit(solution)/shard_map/ghqk,gqhd->gkhd/dot_general | solution.py:83
  191.7 58.6 %fusion.30 = f32[4,512,16,64]{1,3,2,0:T(8,128)} fusion(bf16[4,128,16,64]{1,3,2,0:T(8,128)(2,1)} %copy.80, f32[4,16,128,512]{3,2,1,0:T(8,128)} %fusion.79, f32[4,16,128,512]{3,2,1,0:T(8,128)} %get-tuple-element.5, f32[4,16,128]{2,1,0:T(8,128)S(1)} %get-tuple-element.4), kind=kOutput, calls=%fused_computation.34 | convolution fusion | flops 566239744 | bytes 43024384 | tf_op jit(solution)/shard_map/ghqk,gqhd->gkhd/dot_general | solution.py:80
  250.3 14.7 %copy.97 = f32[4,512,16,64]{3,2,1,0:T(8,128)} copy(f32[4,512,16,64]{1,3,2,0:T(8,128)} %fusion.27) | data formatting | bytes 16777216 | tf_op jit(solution)/shard_map/reshape | solution.py:85
  265.0 14.5 %reshape.272 = f32[16,128,1024]{2,1,0:T(8,128)} reshape(f32[4,512,16,64]{3,2,1,0:T(8,128)} %copy.97) | data formatting | bytes 16777216 | tf_op jit(solution)/shard_map/reshape | solution.py:85
  279.4 4.3 broadcast.127.clone
  283.7 18.2 %scatter_fusion.1 = f32[16,128,1024]{2,1,0:T(8,128)} fusion(f32[16,128,1024]{2,1,0:T(8,128)} %broadcast.127.clone, s32[16]{0:T(128)S(1)} %fusion.71, f32[16,128,1024]{2,1,0:T(8,128)} %reshape.272), kind=kCustom, calls=%fused_computation.4 | custom fusion | flops 2097152 | bytes 25165888 | tf_op jit(solution)/shard_map/scatter-add | solution.py:96
  301.9 10.2 %fusion.19 = f32[16,128,1024]{2,1,0:T(8,128)} fusion(f32[16,128,1024]{2,1,0:T(8,128)} %scatter_fusion.1, bf16[1024,1024]{1,0:T(8,128)(2,1)S(1)} %copy-done), kind=kOutput, calls=%fused_computation.25 | convolution fusion | flops 4297064448 | bytes 18874368 | tf_op jit(solution)/shard_map/ipa,fa->ipf/dot_general | solution.py:101
  312.1 14.5 %copy.96 = f32[4,512,16,64]{3,2,1,0:T(8,128)} copy(f32[4,512,16,64]{1,3,2,0:T(8,128)} %fusion.30) | data formatting | bytes 16777216 | tf_op jit(solution)/shard_map/reshape | solution.py:82
  326.7 14.5 %reshape.271 = f32[16,128,1024]{2,1,0:T(8,128)} reshape(f32[4,512,16,64]{3,2,1,0:T(8,128)} %copy.96) | data formatting | bytes 16777216 | tf_op jit(solution)/shard_map/reshape | solution.py:82
  341.1 4.3 broadcast.127.clone.1
  345.4 18.3 %scatter_fusion = f32[16,128,1024]{2,1,0:T(8,128)} fusion(f32[16,128,1024]{2,1,0:T(8,128)} %broadcast.127.clone.1, s32[16]{0:T(128)S(1)} %fusion.71, f32[16,128,1024]{2,1,0:T(8,128)} %reshape.271), kind=kCustom, calls=%fused_computation.3 | custom fusion | flops 2097152 | bytes 25165888 | tf_op jit(solution)/shard_map/scatter-add | solution.py:90
  363.7 11.5 %add_bitcast_fusion = f32[16,1,128,1024]{3,2,1,0:T(8,128)} fusion(f32[16,128,1024]{2,1,0:T(8,128)} %fusion.19, f32[16,128,1024]{2,1,0:T(8,128)} %scatter_fusion, bf16[1024,1024]{1,0:T(8,128)(2,1)S(1)} %copy-done.6), kind=kOutput, calls=%fused_computation.14 | convolution fusion | flops 4299161600 | bytes 27262976 | tf_op jit(solution)/shard_map/ipa,fa->ipf/dot_general | solution.py:99
  375.2 4.7 all-to-all-start.2
  380.0 8.9 %fusion.56 = bf16[4,128,16,64]{1,3,2,0:T(8,128)(2,1)S(1)} fusion(bf16[4,512,16,64]{1,3,2,0:T(8,128)(2,1)} %copy.82, f32[4,16,128,512]{3,2,1,0:T(8,128)} %get-tuple-element.5, f32[4,16,128]{2,1,0:T(8,128)S(1)} %get-tuple-element.4), kind=kOutput, calls=%fused_computation.49 | convolution fusion | flops 545783808 | bytes 22052864 | tf_op jit(solution)/shard_map/ghqk,gkhd->gqhd/dot_general | solution.py:54
  388.9 0.9 copy.83
  389.8 3.3 fusion.61
  393.2 56.7 %fusion.53 = bf16[4,128,16,64]{1,3,2,0:T(8,128)(2,1)S(1)} fusion(bf16[4,512,16,64]{1,3,2,0:T(8,128)(2,1)} %copy.81, f32[4,16,128,512]{3,2,1,0:T(8,128)} %fusion.79, f32[4,16,128,512]{3,2,1,0:T(8,128)} %get-tuple-element.5, f32[4,16,128]{2,1,0:T(8,128)S(1)} %get-tuple-element.4), kind=kOutput, calls=%fused_computation.48 | convolution fusion | flops 566764032 | bytes 38830080 | tf_op jit(solution)/shard_map/ghqk,gkhd->gqhd/dot_general | solution.py:71
  449.9 0.9 copy.88
  450.8 3.8 convolution_convert_fusion.2
  454.6 3.9 convolution_convert_fusion
  458.5 45.5 %all-to-all-done.2 = f32[16,1,128,1024]{3,2,1,0:T(8,128)} async-done(((f32[16,1,128,1024]{3,2,1,0:T(8,128)}), f32[16,1,128,1024]{3,2,1,0:T(8,128)}, u32[]{:S(2)}, u32[]{:S(2)}) %all-to-all-start.2) | async-done | bytes 8388640 | tf_op jit(solution)/shard_map/all_to_all | solution.py:104
  504.0 1.6 broadcast_in_dim.19
  505.7 17.6 %scatter_fusion.2 = f32[4,128,1024]{2,1,0:T(8,128)} fusion(f32[4,128,1024]{2,1,0:T(8,128)} %broadcast_in_dim.19, s32[16]{0:T(128)S(1)} %fusion.70, f32[16,128,1024]{2,1,0:T(8,128)} %bitcast.14), kind=kCustom, calls=%fused_computation.5 | custom fusion | flops 2097152 | bytes 25165888 | tf_op jit(solution)/shard_map/scatter-add | solution.py:114
  523.3 2.7 convert_element_type.64
  526.0 101.8 %all-reduce.2.cloned.1.call-done = f32[1024,1024]{1,0:T(8,128)} async-done(((f32[1024,1024]{1,0:T(8,128)}), f32[1024,1024]{1,0:T(8,128)}) %all-reduce.2.cloned.1.call-update) | async-done | bytes 4194320 | tf_op jit(solution)/shard_map/psum | solution.py:60
  627.8 4.8 copy.126
  (28 shorter events, 0.4 us)
Async XLA Ops:
  7.2 82.9 %copy-start = (bf16[1024,1024]{1,0:T(8,128)(2,1)S(1)}, bf16[1024,1024]{1,0:T(8,128)(2,1)}, u32[]{:S(2)}) copy-start(bf16[1024,1024]{1,0:T(8,128)(2,1)} %param.17) | copy-start | bytes 6291460
  22.2 4.1 copy-start.4
  22.3 8.6 %copy-start.2 = (s32[4,4]{1,0:T(4,128)S(1)}, s32[4,4]{1,0:T(4,128)}, u32[]{:S(2)}) copy-start(s32[4,4]{1,0:T(4,128)} %param.13) | copy-start | bytes 196
  26.3 63.7 %all-to-all-start.1 = ((bf16[16,1,128,1024]{3,2,1,0:T(8,128)(2,1)}), bf16[16,1,128,1024]{3,2,1,0:T(8,128)(2,1)}, u32[]{:S(2)}, u32[]{:S(2)}) async-start(bf16[16,1,128,1024]{3,2,1,0:T(8,128)(2,1)} %bitcast.82), calls=%async_computation.1 | async-start | bytes 8388608 | tf_op jit(solution)/shard_map/all_to_all | solution.py:28
  40.1 8.5 %copy-start.3 = (s32[4]{0:T(128)S(1)}, s32[4]{0:T(128)}, u32[]{:S(2)}) copy-start(s32[4]{0:T(128)} %param.14) | copy-start | bytes 52
  345.4 18.3 %copy-start.6 = (bf16[1024,1024]{1,0:T(8,128)(2,1)S(1)}, bf16[1024,1024]{1,0:T(8,128)(2,1)}, u32[]{:S(2)}) copy-start(bf16[1024,1024]{1,0:T(8,128)(2,1)} %param.16) | copy-start | bytes 6291460
  375.2 128.9 %all-to-all-start.2 = ((f32[16,1,128,1024]{3,2,1,0:T(8,128)}), f32[16,1,128,1024]{3,2,1,0:T(8,128)}, u32[]{:S(2)}, u32[]{:S(2)}) async-start(f32[16,1,128,1024]{3,2,1,0:T(8,128)} %add_bitcast_fusion), calls=%async_computation.2 | async-start | bytes 16777216 | tf_op jit(solution)/shard_map/all_to_all | solution.py:104
  379.9 9.9 %copy-start.7 = (bf16[512,1024]{1,0:T(8,128)(2,1)S(1)}, bf16[512,1024]{1,0:T(8,128)(2,1)}, u32[]{:S(2)}) copy-start(bf16[512,1024]{1,0:T(8,128)(2,1)} %param.19) | copy-start | bytes 3145732
  379.9 247.8 %all-reduce.2.cloned.1.call-start = ((), (), s32[]{:S(2)}) async-start(), calls=%async_computation.3 | async-start | bytes 8388608 | tf_op jit(solution)/shard_map/psum | solution.py:60
  388.9 4.2 copy-start.5
  505.6 126.9 %copy-start.1 = (bf16[1024,1024]{1,0:T(8,128)(2,1)S(1)}, bf16[1024,1024]{1,0:T(8,128)(2,1)}, u32[]{:S(2)}) copy-start(bf16[1024,1024]{1,0:T(8,128)(2,1)} %param.17) | copy-start | bytes 6291460
Sparse Core Ops, SparseCore 0:
  393.3 234.4 all-reduce.1
where the time goes:
time: 652 us; the launch traced here: 640 us
  matrix products  212 us (33%)
  waiting for transfers between devices  189 us (29%)
  local copies, waits for them, and re-layouts  144 us (22%)
  other arithmetic  57.4 us (9%)
  between operations  14.5 us (2%)
  blocking collectives  13.8 us (2%)
  starting transfers between devices  9.32 us (1%)
    psum x1, waiting for transfers between devices, per_device(): grad_out_weight = lax.psum(out_terms, ('region', 'slab'))  102 us
    dot_general x1, matrix products, per_device(): jnp.einsum('ghqk,gqhd->gkhd', grad_score, query_heads, preferred_element_...  58.6 us
    dot_general x1, matrix products, per_device(): jnp.einsum('ghqk,gkhd->gqhd', grad_score, key_heads, preferred_element_ty...  56.7 us
    all_to_all x1, waiting for transfers between devices, per_device(): lax.all_to_all(slot_grads.reshape(peers, capacity, BLOCK, width), 'region...  45.5 us
    all_to_all x1, waiting for transfers between devices, per_device(): lax.all_to_all(outgoing, 'region', split_axis=0, concat_axis=0, tiled=True)  41.4 us
    reshape x2, local copies, waits for them, and re-layouts, per_device(): grad_value_list = jnp.einsum('ghqk,gqhd->gkhd', probs_b, grad_att_heads,...  29.1 us
    reshape x2, local copies, waits for them, and re-layouts, per_device(): grad_key_list = jnp.einsum('ghqk,gqhd->gkhd', grad_score, query_heads, pr...  29 us
    reshape x2, local copies, waits for them, and re-layouts, per_device(): keys[lists].reshape(group_count_total, listed * BLOCK, HEADS, head_dim)  21.8 us
  transfers between devices with their start and end apart: 3, of which 3 were waited for; matrix products, arithmetic and copies ran while one was open for 18% of the time, Pallas kernels for 0%

commit v1 on v0

v1 whole, which is shorter than its diff:
```python
import jax
import jax.numpy as jnp
from jax import lax
from jax.experimental import pallas as pl
from jax.experimental.pallas import tpu as pltpu
from jax.sharding import PartitionSpec as P

HEADS = 16
BLOCK = 128
QUAD = 4


def nt(a, b):
    return lax.dot_general(a, b, (((1,), (1,)), ((), ())), preferred_element_type=jnp.float32)


def nn(a, b):
    return lax.dot_general(a, b, (((1,), (0,)), ((), ())), preferred_element_type=jnp.float32)


def project_kernel(x_ref, wk_ref, wv_ref, k_ref, v_ref, kt_ref, vt_ref):
    bf16 = jnp.bfloat16
    x = x_ref[0]
    quads = k_ref.shape[1]
    wide = k_ref.shape[3]
    for w_ref, out_ref, out_t_ref in ((wk_ref, k_ref, kt_ref), (wv_ref, v_ref, vt_ref)):
        for quad in range(quads):
            y = nn(x, w_ref[:, quad * wide:(quad + 1) * wide])
            out_ref[0, quad] = y.astype(bf16)
            out_t_ref[0, quad] = y.T.astype(bf16)


def project(x, wk, wv):
    slots, rows, width = x.shape
    quads = HEADS // QUAD
    wide = width // quads
    bf16 = jnp.bfloat16
    flat = jax.ShapeDtypeStruct((slots, quads, rows, wide), bf16)
    turned = jax.ShapeDtypeStruct((slots, quads, wide, rows), bf16)
    return pl.pallas_call(
        project_kernel,
        grid=(slots,),
        in_specs=[
            pl.BlockSpec((1, rows, width), lambda i: (i, 0, 0)),
            pl.BlockSpec((width, width), lambda i: (0, 0)),
            pl.BlockSpec((width, width), lambda i: (0, 0)),
        ],
        out_specs=[
            pl.BlockSpec((1, quads, rows, wide), lambda i: (i, 0, 0, 0)),
            pl.BlockSpec((1, quads, rows, wide), lambda i: (i, 0, 0, 0)),
            pl.BlockSpec((1, quads, wide, rows), lambda i: (i, 0, 0, 0)),
            pl.BlockSpec((1, quads, wide, rows), lambda i: (i, 0, 0, 0)),
        ],
        out_shape=[flat, flat, turned, turned],
        compiler_params=pltpu.CompilerParams(vmem_limit_bytes=40 * 2**20),
        cost_estimate=pl.CostEstimate(
            flops=4 * slots * rows * width * width, bytes_accessed=slots * rows * width * 10, transcendentals=0
        ),
        name="project",
    )(x, wk, wv)


def attention_kernel(
    lists_ref, counts_ref, q_ref, ga_ref, k_ref, v_ref, kt_ref, vt_ref,
    att_ref, gq_ref, dkv_ref, acc_ref,
):
    bf16 = jnp.bfloat16
    f32 = jnp.float32
    slots, quads, rows, wide = k_ref.shape
    groups, listed = lists_ref.shape
    per_group = q_ref.shape[0] // groups
    width = quads * wide
    head_dim = wide // QUAD
    keys = listed * rows

    acc_ref[...] = jnp.zeros_like(acc_ref)
    lane = lax.broadcasted_iota(jnp.int32, (per_group, wide), 1) // head_dim
    key_block = lax.broadcasted_iota(jnp.int32, (keys, QUAD * per_group), 0) // rows

    def spread(x):
        zero = jnp.zeros_like(x)
        return jnp.concatenate([jnp.where(lane == h, x, zero) for h in range(QUAD)], axis=0)

    def gather_diag(y):
        parts = []
        for pair in range(QUAD // 2):
            top = y[2 * pair * head_dim:(2 * pair + 1) * head_dim, 2 * pair * per_group:(2 * pair + 1) * per_group]
            low = y[(2 * pair + 1) * head_dim:(2 * pair + 2) * head_dim, (2 * pair + 1) * per_group:(2 * pair + 2) * per_group]
            parts.append(jnp.concatenate([top, low], axis=0).T)
        return jnp.concatenate(parts, axis=1)

    def step(i, carry):
        g = i // quads
        c = i % quads
        slot = [lists_ref[g, j] for j in range(listed)]
        count = counts_ref[g]
        at_rows = pl.ds(pl.multiple_of(g * per_group, per_group), per_group)
        at_cols = pl.ds(pl.multiple_of(c * wide, wide), wide)
        k4 = jnp.concatenate([k_ref[s, c] for s in slot], axis=0)
        v4 = jnp.concatenate([v_ref[s, c] for s in slot], axis=0)
        kt4 = jnp.concatenate([kt_ref[s, c] for s in slot], axis=1)
        vt4 = jnp.concatenate([vt_ref[s, c] for s in slot], axis=1)
        q4 = spread(q_ref[at_rows, at_cols])
        g4 = spread(ga_ref[at_rows, at_cols])
        scores = nt(k4, q4)
        scores = jnp.where(key_block < count, scores, -1e30)
        top = jnp.max(scores, axis=0, keepdims=True)
        expd = jnp.exp(scores - top)
        total = jnp.sum(expd, axis=0, keepdims=True)
        probs = expd * (1.0 / total)
        grad_prob = nt(v4, g4)
        delta = jnp.sum(probs * grad_prob, axis=0, keepdims=True)
        grad_score = (probs * (grad_prob - delta)).astype(bf16)
        probs_b = probs.astype(bf16)
        att_ref[at_rows, at_cols] = gather_diag(nn(vt4, probs_b)).astype(bf16)
        gq_ref[at_rows, at_cols] = (gather_diag(nn(kt4, grad_score)) * head_dim ** -0.5).astype(bf16)
        grad_key = nn(grad_score, q4)
        grad_value = nn(probs_b, g4)
        for j in range(listed):
            s = slot[j]
            acc_ref[s, c] += grad_key[j * rows:(j + 1) * rows]
            acc_ref[s, quads + c] += grad_value[j * rows:(j + 1) * rows]
        return carry

    lax.fori_loop(0, groups * quads, step, 0)

    def finish(s, carry):
        for c in range(2 * quads):
            dkv_ref[s, :, c * wide:(c + 1) * wide] = acc_ref[s, c].astype(bf16)
        return carry

    lax.fori_loop(0, slots, finish, 0)


def attention(lists, counts, q, ga, k, v, kt, vt):
    slots, quads, rows, wide = k.shape
    width = quads * wide
    bf16 = jnp.bfloat16
    smem = pl.BlockSpec(memory_space=pltpu.SMEM)
    vmem = pl.BlockSpec(memory_space=pltpu.VMEM)
    scores = lists.shape[0] * HEADS * (q.shape[0] // lists.shape[0]) * lists.shape[1] * rows
    return pl.pallas_call(
        attention_kernel,
        in_specs=[smem, smem] + [vmem] * 6,
        out_specs=[vmem] * 3,
        out_shape=[
            jax.ShapeDtypeStruct(q.shape, bf16),
            jax.ShapeDtypeStruct(q.shape, bf16),
            jax.ShapeDtypeStruct((slots, rows, 2 * width), bf16),
        ],
        scratch_shapes=[pltpu.VMEM((slots, 2 * quads, rows, wide), jnp.float32)],
        compiler_params=pltpu.CompilerParams(vmem_limit_bytes=60 * 2**20),
        cost_estimate=pl.CostEstimate(
            flops=12 * scores * wide, bytes_accessed=30 * 2**20, transcendentals=scores
        ),
        name="attention",
    )(lists, counts, q, ga, k, v, kt, vt)


def per_device(
    volume, patches, requests, lists, counts, w_query, key_weight, value_weight, w_out, cotangent
):
    f32 = jnp.float32
    bf16 = jnp.bfloat16
    width = volume.shape[1]
    head_dim = width // HEADS
    owned = patches.shape[0] // BLOCK
    asked = lax.all_to_all(requests, "region", split_axis=1, concat_axis=0, tiled=True)
    asked = asked.reshape(-1)
    slots = asked.shape[0]
    outgoing = patches.reshape(owned, BLOCK, width)[asked]
    blocks = lax.all_to_all(outgoing, "region", split_axis=0, concat_axis=0, tiled=True)

    query = (jnp.dot(volume, w_query, preferred_element_type=f32).astype(bf16) * head_dim ** -0.5).astype(bf16)
    grad_att = nt(cotangent, w_out).astype(bf16)
    w_both = jnp.concatenate([key_weight, value_weight], axis=1)

    k, v, kt, vt = project(blocks, key_weight, value_weight)
    attended, grad_query, slot_grads = attention(lists, counts, query, grad_att, k, v, kt, vt)

    returning = nt(slot_grads.reshape(slots * BLOCK, 2 * width), w_both).astype(bf16)
    returned = lax.all_to_all(
        returning.reshape(slots, BLOCK, width), "region", split_axis=0, concat_axis=0, tiled=True
    )
    out_terms = lax.dot_general(attended, cotangent, (((0,), (0,)), ((), ())), preferred_element_type=f32)
    grad_out_weight = lax.psum(out_terms, ("region", "slab"))
    mixed = nn(attended, w_out).astype(bf16)
    grad_volume = nt(grad_query, w_query).astype(bf16)

    holds = (asked[None, :] == jnp.arange(owned, dtype=jnp.int32)[:, None]).astype(bf16)
    grad_patches = nn(holds, returned.reshape(slots, BLOCK * width)).astype(bf16)
    return mixed, grad_volume, grad_patches.reshape(owned * BLOCK, width), grad_out_weight


def solution(mesh):
    rows = P(("region", "slab"), None)
    in_specs = (
        rows, rows, P(("region", "slab"), None, None), rows, P(("region", "slab")),
        P(), P(), P(), P(), rows,
    )
    return jax.shard_map(
        per_device, mesh=mesh, in_specs=in_specs, out_specs=(rows, rows, rows, P()), check_vma=False
    )
```

time: 652 us -> 373 us (0.57); the launches traced: 640 us -> 372 us
  matrix products: 212 us -> 30.4 us
  local copies, waits for them, and re-layouts: 144 us -> 23.2 us
  other arithmetic: 57.4 us -> 0.39 us
  Pallas kernels: 0 us -> 51.7 us
  waiting for transfers between devices: 189 us -> 229 us
    dot_general x14 -> x7, matrix products: 201 us -> 30.4 us  [the longest x3 19 us: nt(): lax.dot_general(a, b, (((1,), (1,)), ((), ())), preferred_element_type=jn...]
    reshape x13 -> x1, local copies, waits for them, and re-layouts: 112 us -> 1.88 us  [per_device(): grad_patches.reshape(owned * BLOCK, width)]
    scatter-add x3 -> x0, other arithmetic: 54.1 us -> none  [the longest x1 18.3 us: per_device(): slot_key_gradient = jnp.zeros((slot_count, BLOCK, width), single_float).a...]
    pallas_call x0 -> x2, Pallas kernels: none -> 51.7 us  [the longest x1 35.3 us: attention(): pl.pallas_call(attention_kernel, in_specs=[smem, smem] + [vmem] * 6, out_...]
    psum x1, waiting for transfers between devices: 102 us -> 127 us  [per_device(): grad_out_weight = lax.psum(out_terms, ('region', 'slab'))]
    all_to_all x1, waiting for transfers between devices: 41.4 us -> 53 us  [per_device(): lax.all_to_all(outgoing, 'region', split_axis=0, concat_axis=0, tiled=True)]
    unnamed x18 -> x23, local copies, waits for them, and re-layouts: 5.71 us -> 17.3 us
    sub x1 -> x0, matrix products: 10.8 us -> none  [per_device(): expd = jnp.exp(scores - top)]
  transfers between devices with their start and end apart: 3 -> 3, of which waited for: 3 -> 3; matrix products, arithmetic and copies ran while one was open for 18% -> 6% of each run, Pallas kernels for 0% -> 0%
where the time goes in v1:
time: 373 us; the launch traced here: 372 us
  waiting for transfers between devices  229 us (61%)
  Pallas kernels  51.7 us (14%)
  matrix products  30.4 us (8%)
  local copies, waits for them, and re-layouts  23.2 us (6%)
  between operations  14.1 us (4%)
  blocking collectives  13.8 us (4%)
  starting transfers between devices  9.56 us (3%)
    psum x1, waiting for transfers between devices, per_device(): grad_out_weight = lax.psum(out_terms, ('region', 'slab'))  127 us
    all_to_all x1, waiting for transfers between devices, per_device(): lax.all_to_all(outgoing, 'region', split_axis=0, concat_axis=0, tiled=True)  53 us
    all_to_all x1, waiting for transfers between devices, per_device(): lax.all_to_all(returning.reshape(slots, BLOCK, width), 'region', split_ax...  49 us
    pallas_call x1, Pallas kernels, attention(): pl.pallas_call(attention_kernel, in_specs=[smem, smem] + [vmem] * 6, out_...  35.3 us
    dot_general x3, matrix products, nt(): lax.dot_general(a, b, (((1,), (1,)), ((), ())), preferred_element_type=jn...  19 us
    unnamed x23, local copies, waits for them, and re-layouts  17.3 us
    pallas_call x1, Pallas kernels, project(): pl.pallas_call(project_kernel, grid=(slots,), in_specs=[pl.BlockSpec((1,...  16.4 us
    all_to_all x1, blocking collectives, per_device(): lax.all_to_all(requests, 'region', split_axis=1, concat_axis=0, tiled=True)  13.8 us
  transfers between devices with their start and end apart: 3, of which 3 were waited for; matrix products, arithmetic and copies ran while one was open for 6% of the time, Pallas kernels for 0%

profile of v1, /device:TPU:1, one launch (start us, length us, event | category | flops | bytes accessed | tf_op | source)
XLA Modules:
  0.0 372.1 jit_solution(10005032270549252380)
XLA Ops:
  7.2 0.0 copy-start
  7.2 0.9 copy.15
  8.1 13.8 %all_to_all.19 = s32[1,16,1]{2,0,1:T(1,128)S(1)} all-to-all(s32[1,16,1]{2,0,1:T(1,128)S(1)} %copy.15), channel_id=1, replica_groups=mesh['region'=16,'slab'=8] {'region'}, dimensions={1} | all-to-all | bytes 128 | tf_op jit(solution)/shard_map/all_to_all | solution.py:168
  21.8 0.4 reduce
  22.2 4.1 %gather_fusion = bf16[16,128,1024]{2,1,0:T(8,128)(2,1)} fusion(bf16[4,128,1024]{2,1,0:T(8,128)(2,1)} %bitcast.22, s32[1024]{0:T(1024)S(1)} %pad_clamp_fusion), kind=kCustom, calls=%fused_computation | custom fusion | bytes 8388672 | tf_op jit(solution)/shard_map/gather | solution.py:171
  26.3 0.0 copy-start.8
  26.3 4.7 %all-to-all-start.1 = ((bf16[16,128,1024]{2,1,0:T(8,128)(2,1)}), bf16[16,128,1024]{2,1,0:T(8,128)(2,1)}, u32[]{:S(2)}, u32[]{:S(2)}) async-start(bf16[16,128,1024]{2,1,0:T(8,128)(2,1)} %gather_fusion), calls=%async_computation.1 | async-start | bytes 8388608 | tf_op jit(solution)/shard_map/all_to_all | solution.py:172
  31.0 0.0 copy-done.8
  31.0 0.0 copy-start.6
  31.0 3.9 %fusion.7.q_ref = bf16[512,1024]{1,0:T(8,128)(2,1)} fusion(bf16[512,1024]{1,0:T(8,128)(2,1)S(1)} %copy-done.8, bf16[1024,1024]{1,0:T(8,128)(2,1)} %param.15), kind=kOutput, calls=%fused_computation.11 | convolution fusion | flops 1074790400 | bytes 4194304 | tf_op jit(solution)/shard_map/dot_general | solution.py:174
  34.9 0.0 copy-done
  34.9 0.0 copy-done.6
  34.9 2.3 convolution_convert_fusion.3.ga_ref
  37.2 53.0 %all-to-all-done.1.x_ref = bf16[16,128,1024]{2,1,0:T(8,128)(2,1)} async-done(((bf16[16,128,1024]{2,1,0:T(8,128)(2,1)}), bf16[16,128,1024]{2,1,0:T(8,128)(2,1)}, u32[]{:S(2)}, u32[]{:S(2)}) %all-to-all-start.1) | async-done | bytes 4194336 | tf_op jit(solution)/shard_map/all_to_all | solution.py:172
  90.1 0.0 copy-start.1
  90.1 1.6 copy-done.1
  91.7 0.0 copy-start.2
  91.7 1.6 copy-done.2
  93.3 16.4 %project.1 = (bf16[16,4,128,256]{3,2,1,0:T(8,128)(2,1)S(1)}, bf16[16,4,128,256]{3,2,1,0:T(8,128)(2,1)S(1)}, bf16[16,4,256,128]{3,2,1,0:T(8,128)(2,1)}, bf16[16,4,256,128]{3,2,1,0:T(8,128)(2,1)}) custom-call(bf16[16,128,1024]{2,1,0:T(8,128)(2,1)} %all-to-all-done.1.x_ref, bf16[1024,1024]{1,0:T(8,128)(2,1)S(1)} %copy-done.1, bf16[1024,1024]{1,0:T(8,128)(2,1)S(1)} %copy-done.2), custom_call_target="tpu_custom_call" | custom-call | flops 8589934592 | bytes 20971520 | tf_op jit(solution)/shard_map/project/pallas_call | solution.py:40
  109.7 0.0 copy-start.3
  109.7 1.9 copy-done.3
  111.6 0.0 copy-start.4
  111.6 1.9 copy-done.4
  113.5 35.3 %attention.1 = (bf16[512,1024]{1,0:T(8,128)(2,1)}, bf16[512,1024]{1,0:T(8,128)(2,1)}, bf16[16,128,2048]{2,1,0:T(8,128)(2,1)}) custom-call(s32[4,4]{1,0:T(4,128)} %lists_ref.1, s32[4]{0:T(128)} %counts_ref.1, bf16[512,1024]{1,0:T(8,128)(2,1)} %fusion.7.q_ref, bf16[512,1024]{1,0:T(8,128)(2,1)} %convolution_convert_fusion.3.ga_ref, ...), custom_call_target="tpu_custom_call" | custom-call | flops 12884901888 | bytes 31457280 | tf_op jit(solution)/shard_map/attention/pallas_call | solution.py:142
  148.9 14.5 %fusion.4 = bf16[2048,1024]{1,0:T(8,128)(2,1)} fusion(bf16[2048,2048]{1,0:T(8,128)(2,1)} %bitcast.24, bf16[1024,1024]{1,0:T(8,128)(2,1)} %wv_ref.1, bf16[1024,1024]{1,0:T(8,128)(2,1)} %wk_ref.1), kind=kOutput, calls=%fused_computation.6 | convolution fusion | flops 8600420352 | bytes 16777216 | tf_op jit(solution)/shard_map/dot_general | solution.py:14
  163.4 0.0 copy-start.5
  163.4 4.7 %all-to-all-start.2 = ((bf16[16,128,1024]{2,1,0:T(8,128)(2,1)}), bf16[16,128,1024]{2,1,0:T(8,128)(2,1)}, u32[]{:S(2)}, u32[]{:S(2)}) async-start(bf16[16,128,1024]{2,1,0:T(8,128)(2,1)} %bitcast.23), calls=%async_computation.2 | async-start | bytes 8388608 | tf_op jit(solution)/shard_map/all_to_all | solution.py:182
  168.1 0.2 all-reduce.2.cloned.1.call-start
  168.3 0.0 copy-done.5
  168.3 4.5 %fusion.11 = f32[1024,1024]{1,0:T(8,128)} fusion(bf16[512,1024]{1,0:T(8,128)(2,1)S(1)} %copy-done.5, bf16[512,1024]{1,0:T(8,128)(2,1)} %param.19), kind=kOutput, calls=%fused_computation.18 | convolution fusion | flops 1073741824 | bytes 6291456 | tf_op jit(solution)/shard_map/dot_general | solution.py:185
  172.8 0.0 all-reduce.2.cloned.1.call-update
  172.8 0.0 copy-start.7
  172.8 0.0 copy-start.9
  172.8 2.2 convolution_convert_fusion.2
  175.1 0.0 copy-done.7
  175.1 0.0 copy-done.9
  175.1 2.3 convolution_convert_fusion.1
  177.3 49.0 %all-to-all-done.2 = bf16[16,128,1024]{2,1,0:T(8,128)(2,1)} async-done(((bf16[16,128,1024]{2,1,0:T(8,128)(2,1)}), bf16[16,128,1024]{2,1,0:T(8,128)(2,1)}, u32[]{:S(2)}, u32[]{:S(2)}) %all-to-all-start.2) | async-done | bytes 4194336 | tf_op jit(solution)/shard_map/all_to_all | solution.py:182
  226.4 4.5 %copy.16 = bf16[2,8,128,1024]{3,1,2,0:T(8,128)(2,1)S(1)} copy(bf16[2,8,128,1024]{3,2,1,0:T(8,128)(2,1)} %bitcast.5) | data formatting | bytes 8388608
  230.9 0.8 convolution_convert_fusion
  231.7 1.9 reshape.66
  233.5 126.9 %all-reduce.2.cloned.1.call-done = f32[1024,1024]{1,0:T(8,128)} async-done(((f32[1024,1024]{1,0:T(8,128)}), f32[1024,1024]{1,0:T(8,128)}) %all-reduce.2.cloned.1.call-update) | async-done | bytes 4194320 | tf_op jit(solution)/shard_map/psum | solution.py:186
  360.4 4.8 %copy.18 = f32[1024,1024]{1,0:T(8,128)} copy(f32[1024,1024]{1,0:T(8,128)} %all-reduce.2.cloned.1.call-done) | data formatting | bytes 8388608
  (2 shorter events, 0.0 us)
Async XLA Ops:
  7.2 27.7 %copy-start = (bf16[1024,1024]{1,0:T(8,128)(2,1)S(1)}, bf16[1024,1024]{1,0:T(8,128)(2,1)}, u32[]{:S(2)}) copy-start(bf16[1024,1024]{1,0:T(8,128)(2,1)} %param.18) | copy-start | bytes 6291460
  26.3 4.7 %copy-start.8 = (bf16[512,1024]{1,0:T(8,128)(2,1)S(1)}, bf16[512,1024]{1,0:T(8,128)(2,1)}, u32[]{:S(2)}) copy-start(bf16[512,1024]{1,0:T(8,128)(2,1)} %param.10) | copy-start | bytes 3145732
  26.3 63.8 %all-to-all-start.1 = ((bf16[16,128,1024]{2,1,0:T(8,128)(2,1)}), bf16[16,128,1024]{2,1,0:T(8,128)(2,1)}, u32[]{:S(2)}, u32[]{:S(2)}) async-start(bf16[16,128,1024]{2,1,0:T(8,128)(2,1)} %gather_fusion), calls=%async_computation.1 | async-start | bytes 8388608 | tf_op jit(solution)/shard_map/all_to_all | solution.py:172
  31.0 3.9 %copy-start.6 = (bf16[512,1024]{1,0:T(8,128)(2,1)S(1)}, bf16[512,1024]{1,0:T(8,128)(2,1)}, u32[]{:S(2)}) copy-start(bf16[512,1024]{1,0:T(8,128)(2,1)} %param.19) | copy-start | bytes 3145732
  90.1 1.6 copy-start.1
  91.7 1.6 copy-start.2
  109.7 1.9 copy-start.3
  111.6 1.9 copy-start.4
  163.4 4.9 %copy-start.5 = (bf16[512,1024]{1,0:T(8,128)(2,1)S(1)}, bf16[512,1024]{1,0:T(8,128)(2,1)}, u32[]{:S(2)}) copy-start(bf16[512,1024]{1,0:T(8,128)(2,1)} %get-tuple-element.15) | copy-start | bytes 3145732
  163.4 63.0 %all-to-all-start.2 = ((bf16[16,128,1024]{2,1,0:T(8,128)(2,1)}), bf16[16,128,1024]{2,1,0:T(8,128)(2,1)}, u32[]{:S(2)}, u32[]{:S(2)}) async-start(bf16[16,128,1024]{2,1,0:T(8,128)(2,1)} %bitcast.23), calls=%async_computation.2 | async-start | bytes 8388608 | tf_op jit(solution)/shard_map/all_to_all | solution.py:182
  168.1 192.4 %all-reduce.2.cloned.1.call-start = ((), (), s32[]{:S(2)}) async-start(), calls=%async_computation.3 | async-start | bytes 8388608 | tf_op jit(solution)/shard_map/psum | solution.py:186
  172.8 2.2 copy-start.7
  172.8 2.2 copy-start.9
Sparse Core Ops, SparseCore 0:
  173.8 186.5 all-reduce.1

commit v2 on v1

v2 whole, which is shorter than its diff:
```python
import jax
import jax.numpy as jnp
from jax import lax
from jax.experimental import pallas as pl
from jax.experimental.pallas import tpu as pltpu
from jax.sharding import PartitionSpec as P

HEADS = 16
BLOCK = 128
QUAD = 4
BATCH = 4
SIDE = 4
MIB = 2**20


def nt(a, b):
    return lax.dot_general(a, b, (((1,), (1,)), ((), ())), preferred_element_type=jnp.float32)


def nn(a, b):
    return lax.dot_general(a, b, (((1,), (0,)), ((), ())), preferred_element_type=jnp.float32)


def attention_kernel(
    lists_ref, counts_ref, q_hbm, ga_hbm, x_hbm, wk_hbm, wv_hbm,
    att_ref, gq_ref, ret_hbm,
    q_ref, ga_ref, x_ref, wk_ref, wv_ref, k_ref, v_ref, kt_ref, vt_ref, acc_ref,
    used_ref, order_ref, in_sems, out_sems,
):
    bf16 = jnp.bfloat16
    slots, quads, rows, wide = k_ref.shape
    groups, listed = lists_ref.shape
    per_group = q_ref.shape[0] // groups
    head_dim = wide // QUAD

    loads = [
        pltpu.make_async_copy(src, dst, in_sems.at[i])
        for i, (src, dst) in enumerate(
            ((x_hbm, x_ref), (wk_hbm, wk_ref), (wv_hbm, wv_ref), (q_hbm, q_ref), (ga_hbm, ga_ref))
        )
    ]
    for load in loads:
        load.start()

    for s in range(slots):
        used_ref[s] = 0
    for g in range(groups):
        for j in range(listed):
            s = lists_ref[g, j]
            used_ref[s] = used_ref[s] | (j < counts_ref[g]).astype(jnp.int32)
    n_used = jnp.int32(0)
    for s in range(slots):
        order_ref[n_used] = s
        n_used = n_used + used_ref[s]
    n = n_used
    for s in range(slots):
        order_ref[n] = s
        n = n + 1 - used_ref[s]
    batches = (n_used + BATCH - 1) // BATCH

    def clear(s, carry):
        acc_ref[s] = jnp.zeros(acc_ref.shape[1:], acc_ref.dtype)
        return carry

    lax.fori_loop(0, slots, clear, 0)

    for load in loads:
        load.wait()

    def project(b, carry):
        ids = [order_ref[b * BATCH + i] for i in range(BATCH)]
        x = jnp.concatenate([x_ref[s] for s in ids], axis=0)
        for w_ref, out_ref, out_t_ref in ((wk_ref, k_ref, kt_ref), (wv_ref, v_ref, vt_ref)):
            for quad in range(quads):
                y = nn(x, w_ref[:, quad * wide:(quad + 1) * wide]).astype(bf16)
                for i, s in enumerate(ids):
                    part = y[i * rows:(i + 1) * rows]
                    out_ref[s, quad] = part
                    out_t_ref[s, quad] = part.T
        return carry

    lax.fori_loop(0, batches, project, 0)

    lane = lax.broadcasted_iota(jnp.int32, (per_group, wide), 1) // head_dim

    def spread(x):
        zero = jnp.zeros_like(x)
        return jnp.concatenate([jnp.where(lane == h, x, zero) for h in range(QUAD)], axis=0)

    def gather_diag(y):
        parts = []
        for pair in range(QUAD // 2):
            blocks = []
            for h in (2 * pair, 2 * pair + 1):
                blocks.append(y[h * head_dim:(h + 1) * head_dim, h * per_group:(h + 1) * per_group])
            parts.append(jnp.concatenate(blocks, axis=0).T)
        return jnp.concatenate(parts, axis=1)

    def step(i, carry):
        g = i // quads
        c = i % quads
        count = counts_ref[g]
        slot = [lists_ref[g, 0]] + [
            jnp.where(j < count, lists_ref[g, j], lists_ref[g, 0]) for j in range(1, listed)
        ]
        at_rows = pl.ds(pl.multiple_of(g * per_group, per_group), per_group)
        at_cols = pl.ds(pl.multiple_of(c * wide, wide), wide)
        k4 = jnp.concatenate([k_ref[s, c] for s in slot], axis=0)
        v4 = jnp.concatenate([v_ref[s, c] for s in slot], axis=0)
        kt4 = jnp.concatenate([kt_ref[s, c] for s in slot], axis=1)
        vt4 = jnp.concatenate([vt_ref[s, c] for s in slot], axis=1)
        q4 = spread(q_ref[at_rows, at_cols])
        g4 = spread(ga_ref[at_rows, at_cols])
        scores = nt(k4, q4)
        limits = [jnp.where(j < count, 3e38, -1e30) for j in range(listed)]
        scores = jnp.concatenate(
            [jnp.minimum(scores[j * rows:(j + 1) * rows], limits[j]) for j in range(listed)], axis=0
        )
        top = jnp.max(scores, axis=0, keepdims=True)
        expd = jnp.exp(scores - top)
        total = jnp.sum(expd, axis=0, keepdims=True)
        probs = expd * (1.0 / total)
        grad_prob = nt(v4, g4)
        delta = jnp.sum(probs * grad_prob, axis=0, keepdims=True)
        grad_score = (probs * (grad_prob - delta)).astype(bf16)
        probs_b = probs.astype(bf16)
        att_ref[at_rows, at_cols] = gather_diag(nn(vt4, probs_b)).astype(bf16)
        gq_ref[at_rows, at_cols] = (gather_diag(nn(kt4, grad_score)) * head_dim ** -0.5).astype(bf16)
        grad_key = nn(grad_score, q4)
        grad_value = nn(probs_b, g4)
        for j in range(listed):
            s = slot[j]
            acc_ref[s, c] += grad_key[j * rows:(j + 1) * rows]
            acc_ref[s, quads + c] += grad_value[j * rows:(j + 1) * rows]
        return carry

    lax.fori_loop(0, groups * quads, step, 0)

    def send(i, s):
        return pltpu.make_async_copy(x_ref.at[s], ret_hbm.at[s], out_sems.at[i])

    def turn_back(b, carry):
        ids = [order_ref[b * BATCH + i] for i in range(BATCH)]
        grads = [
            jnp.concatenate(
                [
                    jnp.concatenate([acc_ref[s, at + c].astype(bf16) for c in range(quads)], axis=1)
                    for s in ids
                ],
                axis=0,
            )
            for at in (0, quads)
        ]
        for c in range(quads):
            out_rows = slice(c * wide, (c + 1) * wide)
            y = (nt(grads[0], wk_ref[out_rows]) + nt(grads[1], wv_ref[out_rows])).astype(bf16)
            for i, s in enumerate(ids):
                x_ref[s, :, out_rows] = y[i * rows:(i + 1) * rows]
        for i, s in enumerate(ids):
            send(b * BATCH + i, s).start()
        return carry

    lax.fori_loop(0, batches, turn_back, 0)

    def nothing(i, carry):
        s = order_ref[i]
        x_ref[s] = jnp.zeros(x_ref.shape[1:], x_ref.dtype)
        send(i, s).start()
        return carry

    lax.fori_loop(batches * BATCH, slots, nothing, 0)

    def arrive(i, carry):
        send(i, order_ref[i]).wait()
        return carry

    lax.fori_loop(0, slots, arrive, 0)


def attention(lists, counts, q, ga, x, wk, wv):
    bf16 = jnp.bfloat16
    slots, rows, width = x.shape
    quads = HEADS // QUAD
    wide = width // quads
    smem = pl.BlockSpec(memory_space=pltpu.SMEM)
    vmem = pl.BlockSpec(memory_space=pltpu.VMEM)
    hbm = pl.BlockSpec(memory_space=pl.ANY)
    scores = HEADS * q.shape[0] * lists.shape[1] * rows
    straight = pltpu.VMEM((slots, quads, rows, wide), bf16)
    turned = pltpu.VMEM((slots, quads, wide, rows), bf16)
    return pl.pallas_call(
        attention_kernel,
        in_specs=[smem, smem] + [hbm] * 5,
        out_specs=[vmem, vmem, hbm],
        out_shape=[
            jax.ShapeDtypeStruct(q.shape, bf16),
            jax.ShapeDtypeStruct(q.shape, bf16),
            jax.ShapeDtypeStruct(x.shape, bf16),
        ],
        scratch_shapes=[
            pltpu.VMEM(q.shape, bf16), pltpu.VMEM(q.shape, bf16), pltpu.VMEM(x.shape, bf16),
            pltpu.VMEM(wk.shape, bf16), pltpu.VMEM(wv.shape, bf16),
            straight, straight, turned, turned,
            pltpu.VMEM((slots, 2 * quads, rows, wide), jnp.float32),
            pltpu.SMEM((slots + 1,), jnp.int32),
            pltpu.SMEM((slots + 1,), jnp.int32),
            pltpu.SemaphoreType.DMA((5,)),
            pltpu.SemaphoreType.DMA((slots,)),
        ],
        compiler_params=pltpu.CompilerParams(vmem_limit_bytes=60 * MIB),
        cost_estimate=pl.CostEstimate(
            flops=12 * scores * wide + 8 * slots * rows * width * width,
            bytes_accessed=20 * MIB, transcendentals=scores,
        ),
        name="attention",
    )(lists, counts, q, ga, x, wk, wv)


def settle_kernel(asked_ref, x_ref, out_ref, acc_ref):
    acc_ref[...] = jnp.zeros_like(acc_ref)
    for p in range(x_ref.shape[0]):
        acc_ref[asked_ref[p]] += x_ref[p].astype(jnp.float32)
    out_ref[...] = acc_ref[...].astype(out_ref.dtype)


def settle(asked, x, owned):
    slots, rows, width = x.shape
    cut = 32
    return pl.pallas_call(
        settle_kernel,
        grid=(rows // cut,),
        in_specs=[
            pl.BlockSpec(memory_space=pltpu.SMEM),
            pl.BlockSpec((slots, cut, width), lambda i: (0, i, 0)),
        ],
        out_specs=pl.BlockSpec((owned, cut, width), lambda i: (0, i, 0)),
        out_shape=jax.ShapeDtypeStruct((owned, rows, width), jnp.bfloat16),
        scratch_shapes=[pltpu.VMEM((owned, cut, width), jnp.float32)],
        compiler_params=pltpu.CompilerParams(vmem_limit_bytes=16 * MIB),
        cost_estimate=pl.CostEstimate(flops=slots * rows * width, bytes_accessed=3 * slots * rows * width, transcendentals=0),
        name="settle",
    )(asked, x)


def pick(parts, index):
    start = [index.astype(jnp.uint32)] + [jnp.uint32(0)] * (parts.ndim - 1)
    return lax.dynamic_slice(parts, start, (1,) + parts.shape[1:])[0]


def sum_over_devices(terms):
    f32, bf16 = jnp.float32, jnp.bfloat16
    region, slab = (lax.axis_index(axis).astype(jnp.uint32) for axis in ("region", "slab"))
    x = region & (SIDE - 1)
    z, core = slab >> 1, slab & 1
    width = terms.shape[1]

    def along_z(a, by):
        return lax.ppermute(a, "slab", [(p * 2 + c, (p + by) % SIDE * 2 + c) for p in range(SIDE) for c in range(2)])

    def along_x(a, by):
        return lax.ppermute(a, "region", [(p * SIDE + i, p * SIDE + (i + by) % SIDE) for p in range(SIDE) for i in range(SIDE)])

    def along_y(a, by):
        return lax.ppermute(a, "region", [(i * SIDE + p, (i + by) % SIDE * SIDE + p) for p in range(SIDE) for i in range(SIDE)])

    def swap(a):
        return lax.ppermute(a, "slab", [(p * 2 + c, p * 2 + 1 - c) for p in range(SIDE) for c in range(2)])

    def scatter(a, move, place):
        parts = a.reshape(SIDE, a.shape[0] // SIDE, width)
        got = [move(pick(parts, (place + by) & (SIDE - 1)).astype(bf16), by).astype(f32) for by in range(1, SIDE)]
        return pick(parts, place) + (got[0] + got[1] + got[2])

    def gather(a, move, place):
        got = [a] + [move(a, by) for by in range(1, SIDE)]
        stacked = jnp.stack(got)
        parts = [pick(stacked, (place - i) & (SIDE - 1)) for i in range(SIDE)]
        return jnp.concatenate(parts, axis=0)

    halves = terms.reshape(2, terms.shape[0] // 2, width)
    part = pick(halves, core) + swap(pick(halves, 1 - core).astype(bf16)).astype(f32)
    part = scatter(part, along_z, z)
    part = scatter(part, along_x, x).astype(bf16)
    ring = [part.astype(f32)] + [along_y(part, by).astype(f32) for by in range(1, SIDE)]
    part = ((ring[0] + ring[2]) + (ring[1] + ring[3])).astype(bf16)
    part = gather(part, along_x, x)
    part = gather(part, along_z, z)
    other = swap(part)
    first, second = jnp.where(core == 0, part, other), jnp.where(core == 0, other, part)
    return jnp.concatenate([first, second], axis=0).astype(f32)


def per_device(
    volume, patches, requests, lists, counts, w_query, key_weight, value_weight, w_out, cotangent
):
    f32 = jnp.float32
    bf16 = jnp.bfloat16
    width = volume.shape[1]
    head_dim = width // HEADS
    owned = patches.shape[0] // BLOCK
    asked = lax.all_to_all(requests, "region", split_axis=1, concat_axis=0, tiled=True)
    asked = asked.reshape(-1)
    outgoing = patches.reshape(owned, BLOCK, width)[asked]
    blocks = lax.all_to_all(outgoing, "region", split_axis=0, concat_axis=0, tiled=True)

    query = (nn(volume, w_query).astype(bf16) * head_dim ** -0.5).astype(bf16)
    grad_att = nt(cotangent, w_out).astype(bf16)

    attended, grad_query, returning = attention(lists, counts, query, grad_att, blocks, key_weight, value_weight)

    returned = lax.all_to_all(returning, "region", split_axis=0, concat_axis=0, tiled=True)
    out_terms = lax.dot_general(attended, cotangent, (((0,), (0,)), ((), ())), preferred_element_type=f32)
    grad_out_weight = sum_over_devices(out_terms)
    mixed = nn(attended, w_out).astype(bf16)
    grad_volume = nt(grad_query, w_query).astype(bf16)
    grad_patches = settle(asked, returned, owned)
    return mixed, grad_volume, grad_patches.reshape(owned * BLOCK, width), grad_out_weight


def solution(mesh):
    rows = P(("region", "slab"), None)
    in_specs = (
        rows, rows, P(("region", "slab"), None, None), rows, P(("region", "slab")),
        P(), P(), P(), P(), rows,
    )
    return jax.shard_map(
        per_device, mesh=mesh, in_specs=in_specs, out_specs=(rows, rows, rows, P()), check_vma=False
    )
```

time: 373 us -> 256 us (0.69)
  waiting for transfers between devices: 229 us -> 120 us
  starting transfers between devices: 9.56 us -> 38.6 us
  matrix products: 30.4 us -> 14.9 us
  local copies, waits for them, and re-layouts: 23.2 us -> 8.7 us
  between operations: 14.1 us -> 0.84 us
  other arithmetic: 0.39 us -> 9.46 us
    psum x1 -> x0, waiting for transfers between devices: 127 us -> none  [per_device(): grad_out_weight = lax.psum(out_terms, ('region', 'slab'))]
    ppermute x0 -> x17, waiting for transfers between devices: none -> 67.4 us  [the longest x6 37.7 us: along_x(): lax.ppermute(a, 'region', [(p * SIDE + i, p * SIDE + (i + by) % SIDE) for...]
    all_to_all x1, waiting for transfers between devices: 49 us -> 0.01 us  [per_device(): lax.all_to_all(returning, 'region', split_axis=0, concat_axis=0, tiled=True)]
    ppermute x0 -> x17, starting transfers between devices: none -> 29.5 us  [the longest x6 16.1 us: along_z(): lax.ppermute(a, 'slab', [(p * 2 + c, (p + by) % SIDE * 2 + c) for p in ra...]
    dot_general x3 -> x2, matrix products: 19 us -> 4.55 us  [nt(): lax.dot_general(a, b, (((1,), (1,)), ((), ())), preferred_element_type=jn...]
    unnamed x23 -> x13, local copies, waits for them, and re-layouts: 17.3 us -> 4.23 us
    dot_general x2, matrix products: 2.98 us -> 7.82 us  [nn(): lax.dot_general(a, b, (((1,), (0,)), ((), ())), preferred_element_type=jn...]
    dot_general x1 -> x0, matrix products: 3.9 us -> none  [per_device(): jnp.dot(volume, w_query, preferred_element_type=f32).astype(bf16)]
  transfers between devices with their start and end apart: 3 -> 19, of which waited for: 3 -> 12; matrix products, arithmetic and copies ran while one was open for 6% -> 8% of each run, Pallas kernels for 0% -> 0%
where the time goes in v2:
time: 256 us; the launch traced here: 257 us
  waiting for transfers between devices  120 us (47%)
  Pallas kernels  50.5 us (20%)
  starting transfers between devices  38.6 us (15%)
  matrix products  14.9 us (6%)
  blocking collectives  13.8 us (5%)
  other arithmetic  9.46 us (4%)
  local copies, waits for them, and re-layouts  8.7 us (3%)
    all_to_all x1, waiting for transfers between devices, per_device(): lax.all_to_all(outgoing, 'region', split_axis=0, concat_axis=0, tiled=True)  52.6 us
    pallas_call x1, Pallas kernels, attention(): pl.pallas_call(attention_kernel, in_specs=[smem, smem] + [hbm] * 5, out_s...  46.1 us
    ppermute x6, waiting for transfers between devices, along_x(): lax.ppermute(a, 'region', [(p * SIDE + i, p * SIDE + (i + by) % SIDE) for...  37.7 us
    ppermute x6, waiting for transfers between devices, along_z(): lax.ppermute(a, 'slab', [(p * 2 + c, (p + by) % SIDE * 2 + c) for p in ra...  27 us
    ppermute x6, starting transfers between devices, along_z(): lax.ppermute(a, 'slab', [(p * 2 + c, (p + by) % SIDE * 2 + c) for p in ra...  16.1 us
    all_to_all x1, blocking collectives, per_device(): lax.all_to_all(requests, 'region', split_axis=1, concat_axis=0, tiled=True)  13.8 us
    dot_general x2, matrix products, nn(): lax.dot_general(a, b, (((1,), (0,)), ((), ())), preferred_element_type=jn...  7.82 us
    ppermute x6, starting transfers between devices, along_x(): lax.ppermute(a, 'region', [(p * SIDE + i, p * SIDE + (i + by) % SIDE) for...  7.76 us
  transfers between devices with their start and end apart: 19, of which 12 were waited for; matrix products, arithmetic and copies ran while one was open for 8% of the time, Pallas kernels for 0%

profile of v2, /device:TPU:1, one launch (start us, length us, event | category | flops | bytes accessed | tf_op | source)
XLA Modules:
  0.0 256.8 jit_solution(645433565038634843)
XLA Ops:
  0.6 0.9 copy.15
  1.5 13.8 %all_to_all.19 = s32[1,16,1]{2,0,1:T(1,128)S(1)} all-to-all(s32[1,16,1]{2,0,1:T(1,128)S(1)} %copy.15), channel_id=1, replica_groups=mesh['region'=16,'slab'=8] {'region'}, dimensions={1} | all-to-all | bytes 128 | tf_op jit(solution)/shard_map/all_to_all | solution.py:301
  15.3 0.4 reduce.asked_ref
  15.7 4.1 %gather_fusion = bf16[16,128,1024]{2,1,0:T(8,128)(2,1)} fusion(bf16[4,128,1024]{2,1,0:T(8,128)(2,1)} %bitcast.68, s32[1024]{0:T(1024)S(1)} %pad_clamp_fusion), kind=kCustom, calls=%fused_computation | custom fusion | bytes 8388672 | tf_op jit(solution)/shard_map/gather | solution.py:303
  19.8 4.6 %all-to-all-start.1 = ((bf16[16,128,1024]{2,1,0:T(8,128)(2,1)}), bf16[16,128,1024]{2,1,0:T(8,128)(2,1)}, u32[]{:S(2)}, u32[]{:S(2)}) async-start(bf16[16,128,1024]{2,1,0:T(8,128)(2,1)} %gather_fusion), calls=%async_computation.1 | async-start | bytes 8388608 | tf_op jit(solution)/shard_map/all_to_all | solution.py:304
  24.3 4.2 %fusion.q_hbm = bf16[512,1024]{1,0:T(8,128)(2,1)} fusion(bf16[512,1024]{1,0:T(8,128)(2,1)} %param.10, bf16[1024,1024]{1,0:T(8,128)(2,1)} %param.15), kind=kOutput, calls=%fused_computation.8 | convolution fusion | flops 1074790400 | bytes 4194304 | tf_op jit(solution)/shard_map/dot_general | solution.py:21
  28.6 2.3 convolution_convert_fusion.2.ga_hbm
  30.8 52.6 %all-to-all-done.1.x_hbm = bf16[16,128,1024]{2,1,0:T(8,128)(2,1)} async-done(((bf16[16,128,1024]{2,1,0:T(8,128)(2,1)}), bf16[16,128,1024]{2,1,0:T(8,128)(2,1)}, u32[]{:S(2)}, u32[]{:S(2)}) %all-to-all-start.1) | async-done | bytes 4194336 | tf_op jit(solution)/shard_map/all_to_all | solution.py:304
  83.5 46.1 %attention.1 = (bf16[512,1024]{1,0:T(8,128)(2,1)}, bf16[512,1024]{1,0:T(8,128)(2,1)}, bf16[16,128,1024]{2,1,0:T(8,128)(2,1)}) custom-call(s32[4,4]{1,0:T(4,128)} %lists_ref.1, s32[4]{0:T(128)} %counts_ref.1, bf16[512,1024]{1,0:T(8,128)(2,1)} %fusion.q_hbm, bf16[512,1024]{1,0:T(8,128)(2,1)} %convolution_convert_fusion.2.ga_hbm, ...), custom_call_target="tpu_custom_call" | custom-call | flops 30064771072 | bytes 20971520 | tf_op jit(solution)/shard_map/attention/pallas_call | solution.py:191
  129.6 2.5 fusion.11
  132.1 2.0 copy-done.1
  134.1 0.2 fusion.1
  134.4 4.6 %all-to-all-start.2 = ((bf16[16,128,1024]{2,1,0:T(8,128)(2,1)}), bf16[16,128,1024]{2,1,0:T(8,128)(2,1)}, u32[]{:S(2)}, u32[]{:S(2)}) async-start(bf16[16,128,1024]{2,1,0:T(8,128)(2,1)} %get-tuple-element.9), calls=%async_computation.2 | async-start | bytes 8388608 | tf_op jit(solution)/shard_map/all_to_all | solution.py:311
  138.9 2.2 bitcast_add_fusion
  141.2 1.3 copy-done.2
  142.5 0.1 fusion.2
  142.6 6.8 %collective-permute-start.3 = (bf16[128,1024]{1,0:T(8,128)(2,1)S(1)}, bf16[128,1024]{1,0:T(8,128)(2,1)S(1)}, u32[]{:S(2)}, u32[]{:S(2)}) collective-permute-start(bf16[128,1024]{1,0:T(8,128)(2,1)S(1)} %get-tuple-element.13), channel_id=1, source_target_pairs={{0,6},{1,7},{2,0},{3,1},{4,2},{5,3},{6,4},{7,5},{8,14},{9,15},{10,... | collective-permute-start | bytes 786440 | tf_op jit(solution)/shard_map/ppermute | solution.py:258
  149.4 0.7 collective-permute-start.1
  150.1 10.7 %collective-permute-done.3 = bf16[128,1024]{1,0:T(8,128)(2,1)S(1)} collective-permute-done((bf16[128,1024]{1,0:T(8,128)(2,1)S(1)}, bf16[128,1024]{1,0:T(8,128)(2,1)S(1)}, u32[]{:S(2)}, u32[]{:S(2)}) %collective-permute-start.3) | collective-permute-done | bytes 262176 | tf_op jit(solution)/shard_map/ppermute | solution.py:258
  160.7 3.6 %collective-permute-done.1 = bf16[128,1024]{1,0:T(8,128)(2,1)} collective-permute-done((bf16[128,1024]{1,0:T(8,128)(2,1)S(1)}, bf16[128,1024]{1,0:T(8,128)(2,1)}, u32[]{:S(2)}, u32[]{:S(2)}) %collective-permute-start.1) | collective-permute-done | bytes 262176 | tf_op jit(solution)/shard_map/ppermute | solution.py:258
  164.3 1.3 bitcast_add_fusion.1
  165.6 2.6 %collective-permute-start.6 = (bf16[32,1024]{1,0:T(8,128)(2,1)S(1)}, bf16[32,1024]{1,0:T(8,128)(2,1)S(1)}, u32[]{:S(2)}, u32[]{:S(2)}) collective-permute-start(bf16[32,1024]{1,0:T(8,128)(2,1)S(1)} %get-tuple-element.20), channel_id=1, source_target_pairs={{0,24},{8,0},{16,8},{24,16},{32,56},{40,32},{48,40},{56,48},{64,88... | collective-permute-start | bytes 196616 | tf_op jit(solution)/shard_map/ppermute | solution.py:261
  168.2 0.6 collective-permute-start.5
  168.8 0.6 collective-permute-start.4
  169.4 32.5 %collective-permute-done.6 = bf16[32,1024]{1,0:T(8,128)(2,1)S(1)} collective-permute-done((bf16[32,1024]{1,0:T(8,128)(2,1)S(1)}, bf16[32,1024]{1,0:T(8,128)(2,1)S(1)}, u32[]{:S(2)}, u32[]{:S(2)}) %collective-permute-start.6) | collective-permute-done | bytes 65568 | tf_op jit(solution)/shard_map/ppermute | solution.py:261
  201.9 0.8 collective-permute-done.5
  202.7 1.0 collective-permute-start.9
  203.7 0.5 collective-permute-start.8
  204.3 1.9 collective-permute-start.7
  206.2 1.9 collective-permute-done.8
  208.1 0.8 collective-permute-done.7
  208.9 3.3 %collective-permute-start.12 = (bf16[32,1024]{1,0:T(8,128)(2,1)S(1)}, bf16[32,1024]{1,0:T(8,128)(2,1)S(1)}, u32[]{:S(2)}, u32[]{:S(2)}) collective-permute-start(bf16[32,1024]{1,0:T(8,128)(2,1)S(1)} %add_convert_fusion), channel_id=1, source_target_pairs={{0,24},{8,0},{16,8},{24,16},{32,56},{40,32},{48,40},{56,48},{64,88... | collective-permute-start | bytes 196616 | tf_op jit(solution)/shard_map/ppermute | solution.py:261
  212.3 0.7 collective-permute-start.10
  212.9 1.2 collective-permute-done.12
  214.2 2.8 %collective-permute-done.11 = bf16[32,1024]{1,0:T(8,128)(2,1)S(1)} collective-permute-done((bf16[32,1024]{1,0:T(8,128)(2,1)S(1)}, bf16[32,1024]{1,0:T(8,128)(2,1)S(1)}, u32[]{:S(2)}, u32[]{:S(2)}) %collective-permute-start.11) | collective-permute-done | bytes 65568 | tf_op jit(solution)/shard_map/ppermute | solution.py:261
  217.0 0.3 collective-permute-done.10
  217.4 8.0 %collective-permute-start.15 = (bf16[128,1024]{1,0:T(8,128)(2,1)S(1)}, bf16[128,1024]{1,0:T(8,128)(2,1)S(1)}, u32[]{:S(2)}, u32[]{:S(2)}) collective-permute-start(bf16[128,1024]{1,0:T(8,128)(2,1)S(1)} %get-tuple-element.23), channel_id=1, source_target_pairs={{0,6},{1,7},{2,0},{3,1},{4,2},{5,3},{6,4},{7,5},{8,14},{9,15},{10,... | collective-permute-start | bytes 786440 | tf_op jit(solution)/shard_map/ppermute | solution.py:258
  225.4 0.7 collective-permute-start.13
  226.1 9.7 %collective-permute-done.15 = bf16[128,1024]{1,0:T(8,128)(2,1)S(1)} collective-permute-done((bf16[128,1024]{1,0:T(8,128)(2,1)S(1)}, bf16[128,1024]{1,0:T(8,128)(2,1)S(1)}, u32[]{:S(2)}, u32[]{:S(2)}) %collective-permute-start.15) | collective-permute-done | bytes 262176 | tf_op jit(solution)/shard_map/ppermute | solution.py:258
  235.8 3.1 %collective-permute-done.13 = bf16[128,1024]{1,0:T(8,128)(2,1)S(1)} collective-permute-done((bf16[128,1024]{1,0:T(8,128)(2,1)S(1)}, bf16[128,1024]{1,0:T(8,128)(2,1)S(1)}, u32[]{:S(2)}, u32[]{:S(2)}) %collective-permute-start.13) | collective-permute-done | bytes 262176 | tf_op jit(solution)/shard_map/ppermute | solution.py:258
  238.9 0.1 pad_maximum_fusion
  239.1 1.0 pad_maximum_fusion.1
  240.2 2.1 collective-permute-start.16
  242.3 3.6 %convolution_convert_fusion.1 = bf16[512,1024]{1,0:T(8,128)(2,1)} fusion(bf16[512,1024]{1,0:T(8,128)(2,1)} %get-tuple-element.7, bf16[1024,1024]{1,0:T(8,128)(2,1)S(1)} %copy-done), kind=kOutput, calls=%fused_computation.5 | convolution fusion | flops 1074266112 | bytes 4194304 | tf_op jit(solution)/shard_map/dot_general | solution.py:21
  245.9 2.3 convolution_convert_fusion
  248.1 1.8 broadcast_select_fusion.1
  249.9 2.4 maximum_convert_fusion
  252.4 4.4 %settle.1 = bf16[4,128,1024]{2,1,0:T(8,128)(2,1)} custom-call(s32[16]{0:T(128)S(1)} %reduce.asked_ref, bf16[16,128,1024]{2,1,0:T(8,128)(2,1)} %all-to-all-done.2.x_ref), custom_call_target="tpu_custom_call" | custom-call | flops 2097152 | bytes 6291456 | tf_op jit(solution)/shard_map/settle/pallas_call | solution.py:229
  (30 shorter events, 0.5 us)
Async XLA Ops:
  0.6 27.9 %copy-start = (bf16[1024,1024]{1,0:T(8,128)(2,1)S(1)}, bf16[1024,1024]{1,0:T(8,128)(2,1)}, u32[]{:S(2)}) copy-start(bf16[1024,1024]{1,0:T(8,128)(2,1)} %param.18) | copy-start | bytes 6291460
  19.8 63.7 %all-to-all-start.1 = ((bf16[16,128,1024]{2,1,0:T(8,128)(2,1)}), bf16[16,128,1024]{2,1,0:T(8,128)(2,1)}, u32[]{:S(2)}, u32[]{:S(2)}) async-start(bf16[16,128,1024]{2,1,0:T(8,128)(2,1)} %gather_fusion), calls=%async_computation.1 | async-start | bytes 8388608 | tf_op jit(solution)/shard_map/all_to_all | solution.py:304
  24.3 4.2 %copy-start.3 = (bf16[512,1024]{1,0:T(8,128)(2,1)S(1)}, bf16[512,1024]{1,0:T(8,128)(2,1)}, u32[]{:S(2)}) copy-start(bf16[512,1024]{1,0:T(8,128)(2,1)} %param.19) | copy-start | bytes 3145732
  132.1 2.0 copy-start.1
  134.3 4.7 %collective-permute-start = (bf16[512,1024]{1,0:T(8,128)(2,1)S(1)}, bf16[512,1024]{1,0:T(8,128)(2,1)}, u32[]{:S(2)}, u32[]{:S(2)}) collective-permute-start(bf16[512,1024]{1,0:T(8,128)(2,1)S(1)} %fusion.1), channel_id=1, source_target_pairs={{0,1},{1,0},{2,3},{3,2},{4,5},{5,4},{6,7},{7,6},{8,9},{9,8},{10,11... | collective-permute-start | bytes 3145736 | tf_op jit(solution)/shard_map/ppermute | solution.py:267
  134.4 118.0 %all-to-all-start.2 = ((bf16[16,128,1024]{2,1,0:T(8,128)(2,1)}), bf16[16,128,1024]{2,1,0:T(8,128)(2,1)}, u32[]{:S(2)}, u32[]{:S(2)}) async-start(bf16[16,128,1024]{2,1,0:T(8,128)(2,1)} %get-tuple-element.9), calls=%async_computation.2 | async-start | bytes 8388608 | tf_op jit(solution)/shard_map/all_to_all | solution.py:311
  141.2 1.3 copy-start.2
  142.6 18.1 %collective-permute-start.3 = (bf16[128,1024]{1,0:T(8,128)(2,1)S(1)}, bf16[128,1024]{1,0:T(8,128)(2,1)S(1)}, u32[]{:S(2)}, u32[]{:S(2)}) collective-permute-start(bf16[128,1024]{1,0:T(8,128)(2,1)S(1)} %get-tuple-element.13), channel_id=1, source_target_pairs={{0,6},{1,7},{2,0},{3,1},{4,2},{5,3},{6,4},{7,5},{8,14},{9,15},{10,... | collective-permute-start | bytes 786440 | tf_op jit(solution)/shard_map/ppermute | solution.py:258
  149.4 11.3 %collective-permute-start.2 = (bf16[128,1024]{1,0:T(8,128)(2,1)S(1)}, bf16[128,1024]{1,0:T(8,128)(2,1)S(1)}, u32[]{:S(2)}, u32[]{:S(2)}) collective-permute-start(bf16[128,1024]{1,0:T(8,128)(2,1)S(1)} %get-tuple-element.14), channel_id=1, source_target_pairs={{0,4},{1,5},{2,6},{3,7},{4,0},{5,1},{6,2},{7,3},{8,12},{9,13},{10,... | collective-permute-start | bytes 786440 | tf_op jit(solution)/shard_map/ppermute | solution.py:258
  149.4 14.9 %collective-permute-start.1 = (bf16[128,1024]{1,0:T(8,128)(2,1)S(1)}, bf16[128,1024]{1,0:T(8,128)(2,1)}, u32[]{:S(2)}, u32[]{:S(2)}) collective-permute-start(bf16[128,1024]{1,0:T(8,128)(2,1)S(1)} %get-tuple-element.12), channel_id=1, source_target_pairs={{0,2},{1,3},{2,4},{3,5},{4,6},{5,7},{6,0},{7,1},{8,10},{9,11},{10,... | collective-permute-start | bytes 786440 | tf_op jit(solution)/shard_map/ppermute | solution.py:258
  165.6 36.2 %collective-permute-start.6 = (bf16[32,1024]{1,0:T(8,128)(2,1)S(1)}, bf16[32,1024]{1,0:T(8,128)(2,1)S(1)}, u32[]{:S(2)}, u32[]{:S(2)}) collective-permute-start(bf16[32,1024]{1,0:T(8,128)(2,1)S(1)} %get-tuple-element.20), channel_id=1, source_target_pairs={{0,24},{8,0},{16,8},{24,16},{32,56},{40,32},{48,40},{56,48},{64,88... | collective-permute-start | bytes 196616 | tf_op jit(solution)/shard_map/ppermute | solution.py:261
  168.2 34.4 %collective-permute-start.5 = (bf16[32,1024]{1,0:T(8,128)(2,1)S(1)}, bf16[32,1024]{1,0:T(8,128)(2,1)S(1)}, u32[]{:S(2)}, u32[]{:S(2)}) collective-permute-start(bf16[32,1024]{1,0:T(8,128)(2,1)S(1)} %get-tuple-element.21), channel_id=1, source_target_pairs={{0,16},{8,24},{16,0},{24,8},{32,48},{40,56},{48,32},{56,40},{64,80... | collective-permute-start | bytes 196616 | tf_op jit(solution)/shard_map/ppermute | solution.py:261
  168.8 33.9 %collective-permute-start.4 = (bf16[32,1024]{1,0:T(8,128)(2,1)S(1)}, bf16[32,1024]{1,0:T(8,128)(2,1)S(1)}, u32[]{:S(2)}, u32[]{:S(2)}) collective-permute-start(bf16[32,1024]{1,0:T(8,128)(2,1)S(1)} %get-tuple-element.19), channel_id=1, source_target_pairs={{0,8},{8,16},{16,24},{24,0},{32,40},{40,48},{48,56},{56,32},{64,72... | collective-permute-start | bytes 196616 | tf_op jit(solution)/shard_map/ppermute | solution.py:261
  202.7 3.5 %collective-permute-start.9 = (bf16[32,1024]{1,0:T(8,128)(2,1)S(1)}, bf16[32,1024]{1,0:T(8,128)(2,1)S(1)}, u32[]{:S(2)}, u32[]{:S(2)}) collective-permute-start(bf16[32,1024]{1,0:T(8,128)(2,1)S(1)} %fusion.5), channel_id=1, source_target_pairs={{0,96},{32,0},{64,32},{96,64},{8,104},{40,8},{72,40},{104,72},{16,... | collective-permute-start | bytes 196616 | tf_op jit(solution)/shard_map/ppermute | solution.py:264
  203.7 4.3 %collective-permute-start.8 = (bf16[32,1024]{1,0:T(8,128)(2,1)S(1)}, bf16[32,1024]{1,0:T(8,128)(2,1)S(1)}, u32[]{:S(2)}, u32[]{:S(2)}) collective-permute-start(bf16[32,1024]{1,0:T(8,128)(2,1)S(1)} %fusion.5), channel_id=1, source_target_pairs={{0,32},{32,64},{64,96},{96,0},{8,40},{40,72},{72,104},{104,8},{16,... | collective-permute-start | bytes 196616 | tf_op jit(solution)/shard_map/ppermute | solution.py:264
  204.3 4.6 %collective-permute-start.7 = (bf16[32,1024]{1,0:T(8,128)(2,1)S(1)}, bf16[32,1024]{1,0:T(8,128)(2,1)S(1)}, u32[]{:S(2)}, u32[]{:S(2)}) collective-permute-start(bf16[32,1024]{1,0:T(8,128)(2,1)S(1)} %fusion.5), channel_id=1, source_target_pairs={{0,64},{32,96},{64,0},{96,32},{8,72},{40,104},{72,8},{104,40},{16,... | collective-permute-start | bytes 196616 | tf_op jit(solution)/shard_map/ppermute | solution.py:264
  208.9 5.2 %collective-permute-start.12 = (bf16[32,1024]{1,0:T(8,128)(2,1)S(1)}, bf16[32,1024]{1,0:T(8,128)(2,1)S(1)}, u32[]{:S(2)}, u32[]{:S(2)}) collective-permute-start(bf16[32,1024]{1,0:T(8,128)(2,1)S(1)} %add_convert_fusion), channel_id=1, source_target_pairs={{0,24},{8,0},{16,8},{24,16},{32,56},{40,32},{48,40},{56,48},{64,88... | collective-permute-start | bytes 196616 | tf_op jit(solution)/shard_map/ppermute | solution.py:261
  212.3 4.7 %collective-permute-start.11 = (bf16[32,1024]{1,0:T(8,128)(2,1)S(1)}, bf16[32,1024]{1,0:T(8,128)(2,1)S(1)}, u32[]{:S(2)}, u32[]{:S(2)}) collective-permute-start(bf16[32,1024]{1,0:T(8,128)(2,1)S(1)} %add_convert_fusion), channel_id=1, source_target_pairs={{0,16},{8,24},{16,0},{24,8},{32,48},{40,56},{48,32},{56,40},{64,80... | collective-permute-start | bytes 196616 | tf_op jit(solution)/shard_map/ppermute | solution.py:261
  212.3 5.0 %collective-permute-start.10 = (bf16[32,1024]{1,0:T(8,128)(2,1)S(1)}, bf16[32,1024]{1,0:T(8,128)(2,1)S(1)}, u32[]{:S(2)}, u32[]{:S(2)}) collective-permute-start(bf16[32,1024]{1,0:T(8,128)(2,1)S(1)} %add_convert_fusion), channel_id=1, source_target_pairs={{0,8},{8,16},{16,24},{24,0},{32,40},{40,48},{48,56},{56,32},{64,72... | collective-permute-start | bytes 196616 | tf_op jit(solution)/shard_map/ppermute | solution.py:261
  217.4 18.3 %collective-permute-start.15 = (bf16[128,1024]{1,0:T(8,128)(2,1)S(1)}, bf16[128,1024]{1,0:T(8,128)(2,1)S(1)}, u32[]{:S(2)}, u32[]{:S(2)}) collective-permute-start(bf16[128,1024]{1,0:T(8,128)(2,1)S(1)} %get-tuple-element.23), channel_id=1, source_target_pairs={{0,6},{1,7},{2,0},{3,1},{4,2},{5,3},{6,4},{7,5},{8,14},{9,15},{10,... | collective-permute-start | bytes 786440 | tf_op jit(solution)/shard_map/ppermute | solution.py:258
  225.4 10.3 %collective-permute-start.14 = (bf16[128,1024]{1,0:T(8,128)(2,1)S(1)}, bf16[128,1024]{1,0:T(8,128)(2,1)S(1)}, u32[]{:S(2)}, u32[]{:S(2)}) collective-permute-start(bf16[128,1024]{1,0:T(8,128)(2,1)S(1)} %get-tuple-element.23), channel_id=1, source_target_pairs={{0,4},{1,5},{2,6},{3,7},{4,0},{5,1},{6,2},{7,3},{8,12},{9,13},{10,... | collective-permute-start | bytes 786440 | tf_op jit(solution)/shard_map/ppermute | solution.py:258
  225.4 13.5 %collective-permute-start.13 = (bf16[128,1024]{1,0:T(8,128)(2,1)S(1)}, bf16[128,1024]{1,0:T(8,128)(2,1)S(1)}, u32[]{:S(2)}, u32[]{:S(2)}) collective-permute-start(bf16[128,1024]{1,0:T(8,128)(2,1)S(1)} %get-tuple-element.23), channel_id=1, source_target_pairs={{0,2},{1,3},{2,4},{3,5},{4,6},{5,7},{6,0},{7,1},{8,10},{9,11},{10,... | collective-permute-start | bytes 786440 | tf_op jit(solution)/shard_map/ppermute | solution.py:258
  240.2 8.0 %collective-permute-start.16 = (bf16[512,1024]{1,0:T(8,128)(2,1)}, bf16[512,1024]{1,0:T(8,128)(2,1)}, u32[]{:S(2)}, u32[]{:S(2)}) collective-permute-start(bf16[512,1024]{1,0:T(8,128)(2,1)} %pad_maximum_fusion.1), channel_id=1, source_target_pairs={{0,1},{1,0},{2,3},{3,2},{4,5},{5,4},{6,7},{7,6},{8,9},{9,8},{10,11... | collective-permute-start | bytes 3145736 | tf_op jit(solution)/shard_map/ppermute | solution.py:267
  242.3 3.6 %copy-start.4 = (bf16[1024,1024]{1,0:T(8,128)(2,1)S(1)}, bf16[1024,1024]{1,0:T(8,128)(2,1)}, u32[]{:S(2)}) copy-start(bf16[1024,1024]{1,0:T(8,128)(2,1)} %param.15) | copy-start | bytes 6291460
  242.3 3.6 %copy-start.5 = (bf16[512,1024]{1,0:T(8,128)(2,1)S(1)}, bf16[512,1024]{1,0:T(8,128)(2,1)}, u32[]{:S(2)}) copy-start(bf16[512,1024]{1,0:T(8,128)(2,1)} %get-tuple-element.8) | copy-start | bytes 3145732

commit v3 on v2

--- a/solution.py
+++ b/solution.py
@@ -8,8 +8,9 @@
 HEADS = 16
 BLOCK = 128
 QUAD = 4
-BATCH = 4
+BATCH = 2
 SIDE = 4
+PIECES = 2
 MIB = 2**20
 
 
@@ -22,10 +23,10 @@
 
 
 def attention_kernel(
-    lists_ref, counts_ref, q_hbm, ga_hbm, x_hbm, wk_hbm, wv_hbm,
-    att_ref, gq_ref, ret_hbm,
-    q_ref, ga_ref, x_ref, wk_ref, wv_ref, k_ref, v_ref, kt_ref, vt_ref, acc_ref,
-    used_ref, order_ref, in_sems, out_sems,
+    lists_ref, counts_ref, core_ref, q_hbm, ga_hbm, cot_hbm, x_hbm, wk_hbm, wv_hbm,
+    att_ref, gq_ref, keep_ref, give_ref, ret0_hbm, ret1_hbm,
+    q_ref, ga_ref, cot_ref, att_t_ref, x_ref, wk_ref, wv_ref, k_ref, v_ref, kt_ref, vt_ref, acc_ref,
+    mask_ref, used_ref, order_ref, in_sems, out_sems,
 ):
     bf16 = jnp.bfloat16
     slots, quads, rows, wide = k_ref.shape
@@ -36,7 +37,7 @@
     loads = [
         pltpu.make_async_copy(src, dst, in_sems.at[i])
         for i, (src, dst) in enumerate(
-            ((x_hbm, x_ref), (wk_hbm, wk_ref), (wv_hbm, wv_ref), (q_hbm, q_ref), (ga_hbm, ga_ref))
+            ((x_hbm, x_ref), (wk_hbm, wk_ref), (wv_hbm, wv_ref), (q_hbm, q_ref), (ga_hbm, ga_ref), (cot_hbm, cot_ref))
         )
     ]
     for load in loads:
@@ -81,20 +82,18 @@
 
     lax.fori_loop(0, batches, project, 0)
 
-    lane = lax.broadcasted_iota(jnp.int32, (per_group, wide), 1) // head_dim
+    head_of_row = lax.broadcasted_iota(jnp.int32, mask_ref.shape, 0) // per_group
+    head_of_lane = lax.broadcasted_iota(jnp.int32, mask_ref.shape, 1) // head_dim
+    mask_ref[...] = (head_of_row == head_of_lane).astype(jnp.float32).astype(bf16)
 
     def spread(x):
-        zero = jnp.zeros_like(x)
-        return jnp.concatenate([jnp.where(lane == h, x, zero) for h in range(QUAD)], axis=0)
-
-    def gather_diag(y):
-        parts = []
-        for pair in range(QUAD // 2):
-            blocks = []
-            for h in (2 * pair, 2 * pair + 1):
-                blocks.append(y[h * head_dim:(h + 1) * head_dim, h * per_group:(h + 1) * per_group])
-            parts.append(jnp.concatenate(blocks, axis=0).T)
-        return jnp.concatenate(parts, axis=1)
+        return jnp.concatenate([x] * QUAD, axis=0) * mask_ref[...]
+
+    def diagonal(y):
+        blocks = [
+            y[h * head_dim:(h + 1) * head_dim, h * per_group:(h + 1) * per_group] for h in range(QUAD)
+        ]
+        return [jnp.concatenate(blocks[h:h + 2], axis=0) for h in range(0, QUAD, 2)]
 
     def step(i, carry):
         g = i // quads
@@ -124,8 +123,11 @@
         delta = jnp.sum(probs * grad_prob, axis=0, keepdims=True)
         grad_score = (probs * (grad_prob - delta)).astype(bf16)
         probs_b = probs.astype(bf16)
-        att_ref[at_rows, at_cols] = gather_diag(nn(vt4, probs_b)).astype(bf16)
-        gq_ref[at_rows, at_cols] = (gather_diag(nn(kt4, grad_score)) * head_dim ** -0.5).astype(bf16)
+        att_parts = diagonal(nn(vt4, probs_b))
+        att_ref[at_rows, at_cols] = jnp.concatenate([y.T for y in att_parts], axis=1).astype(bf16)
+        att_t_ref[at_cols, at_rows] = jnp.concatenate(att_parts, axis=0).astype(bf16)
+        gq_parts = diagonal(nn(kt4, grad_score) * head_dim ** -0.5)
+        gq_ref[at_rows, at_cols] = jnp.concatenate([y.T for y in gq_parts], axis=1).astype(bf16)
         grad_key = nn(grad_score, q4)
         grad_value = nn(probs_b, g4)
         for j in range(listed):
@@ -134,10 +136,14 @@
             acc_ref[s, quads + c] += grad_value[j * rows:(j + 1) * rows]
         return carry
 
-    lax.fori_loop(0, groups * quads, step, 0)
+    lax.fori_loop(0, groups * quads, step, 0, unroll=2)
 
     def send(i, s):
-        return pltpu.make_async_copy(x_ref.at[s], ret_hbm.at[s], out_sems.at[i])
+        cut = rows // PIECES
+        return [
+            pltpu.make_async_copy(x_ref.at[s, pl.ds(n * cut, cut)], ret.at[s], out_sems.at[i, n])
+            for n, ret in enumerate((ret0_hbm, ret1_hbm))
+        ]
 
     def turn_back(b, carry):
         ids = [order_ref[b * BATCH + i] for i in range(BATCH)]
@@ -157,7 +163,8 @@
             for i, s in enumerate(ids):
                 x_ref[s, :, out_rows] = y[i * rows:(i + 1) * rows]
         for i, s in enumerate(ids):
-            send(b * BATCH + i, s).start()
+            for copy in send(b * BATCH + i, s):
+                copy.start()
         return carry
 
     lax.fori_loop(0, batches, turn_back, 0)
@@ -165,19 +172,28 @@
     def nothing(i, carry):
         s = order_ref[i]
         x_ref[s] = jnp.zeros(x_ref.shape[1:], x_ref.dtype)
-        send(i, s).start()
+        for copy in send(i, s):
+            copy.start()
         return carry
 
     lax.fori_loop(batches * BATCH, slots, nothing, 0)
 
+    half = keep_ref.shape[0]
+    core = core_ref[0]
+    for out_ref, mine in ((keep_ref, core), (give_ref, 1 - core)):
+        for c in range(half // wide):
+            at = pl.ds(pl.multiple_of(mine * half + c * wide, wide), wide)
+            out_ref[c * wide:(c + 1) * wide, :] = nn(att_t_ref[at, :], cot_ref[...]).astype(out_ref.dtype)
+
     def arrive(i, carry):
-        send(i, order_ref[i]).wait()
+        for copy in send(i, order_ref[i]):
+            copy.wait()
         return carry
 
     lax.fori_loop(0, slots, arrive, 0)
 
 
-def attention(lists, counts, q, ga, x, wk, wv):
+def attention(lists, counts, core, q, ga, cot, x, wk, wv):
     bf16 = jnp.bfloat16
     slots, rows, width = x.shape
     quads = HEADS // QUAD
@@ -190,56 +206,62 @@
     turned = pltpu.VMEM((slots, quads, wide, rows), bf16)
     return pl.pallas_call(
         attention_kernel,
-        in_specs=[smem, smem] + [hbm] * 5,
-        out_specs=[vmem, vmem, hbm],
+        in_specs=[smem] * 3 + [hbm] * 6,
+        out_specs=[vmem] * 4 + [hbm] * PIECES,
         out_shape=[
             jax.ShapeDtypeStruct(q.shape, bf16),
             jax.ShapeDtypeStruct(q.shape, bf16),
-            jax.ShapeDtypeStruct(x.shape, bf16),
-        ],
+            jax.ShapeDtypeStruct((width // 2, width), jnp.float32),
+            jax.ShapeDtypeStruct((width // 2, width), bf16),
+        ] + [jax.ShapeDtypeStruct((slots, rows // PIECES, width), bf16)] * PIECES,
         scratch_shapes=[
-            pltpu.VMEM(q.shape, bf16), pltpu.VMEM(q.shape, bf16), pltpu.VMEM(x.shape, bf16),
+            pltpu.VMEM(q.shape, bf16), pltpu.VMEM(q.shape, bf16), pltpu.VMEM(q.shape, bf16),
+            pltpu.VMEM(q.shape[::-1], bf16), pltpu.VMEM(x.shape, bf16),
             pltpu.VMEM(wk.shape, bf16), pltpu.VMEM(wv.shape, bf16),
             straight, straight, turned, turned,
             pltpu.VMEM((slots, 2 * quads, rows, wide), jnp.float32),
+            pltpu.VMEM((QUAD * (q.shape[0] // lists.shape[0]), wide), bf16),
             pltpu.SMEM((slots + 1,), jnp.int32),
             pltpu.SMEM((slots + 1,), jnp.int32),
-            pltpu.SemaphoreType.DMA((5,)),
-            pltpu.SemaphoreType.DMA((slots,)),
+            pltpu.SemaphoreType.DMA((6,)),
+            pltpu.SemaphoreType.DMA((slots, PIECES)),
         ],
-        compiler_params=pltpu.CompilerParams(vmem_limit_bytes=60 * MIB),
+        compiler_params=pltpu.CompilerParams(vmem_limit_bytes=62 * MIB),
         cost_estimate=pl.CostEstimate(
             flops=12 * scores * wide + 8 * slots * rows * width * width,
             bytes_accessed=20 * MIB, transcendentals=scores,
         ),
         name="attention",
-    )(lists, counts, q, ga, x, wk, wv)
-
-
-def settle_kernel(asked_ref, x_ref, out_ref, acc_ref):
+    )(lists, counts, core, q, ga, cot, x, wk, wv)
+
+
+def settle_kernel(asked_ref, x_ref, *refs):
+    out_ref, acc_ref = refs[-2:]
     acc_ref[...] = jnp.zeros_like(acc_ref)
     for p in range(x_ref.shape[0]):
         acc_ref[asked_ref[p]] += x_ref[p].astype(jnp.float32)
     out_ref[...] = acc_ref[...].astype(out_ref.dtype)
 
 
-def settle(asked, x, owned):
+def settle(asked, x, owned, piece, earlier=()):
     slots, rows, width = x.shape
     cut = 32
+    first = piece * (rows // cut)
     return pl.pallas_call(
         settle_kernel,
         grid=(rows // cut,),
         in_specs=[
             pl.BlockSpec(memory_space=pltpu.SMEM),
             pl.BlockSpec((slots, cut, width), lambda i: (0, i, 0)),
-        ],
-        out_specs=pl.BlockSpec((owned, cut, width), lambda i: (0, i, 0)),
-        out_shape=jax.ShapeDtypeStruct((owned, rows, width), jnp.bfloat16),
+        ] + [pl.BlockSpec(memory_space=pl.ANY)] * len(earlier),
+        out_specs=pl.BlockSpec((owned, cut, width), lambda i: (0, first + i, 0)),
+        out_shape=jax.ShapeDtypeStruct((owned, rows * PIECES, width), jnp.bfloat16),
         scratch_shapes=[pltpu.VMEM((owned, cut, width), jnp.float32)],
+        input_output_aliases={2: 0} if earlier else {},
         compiler_params=pltpu.CompilerParams(vmem_limit_bytes=16 * MIB),
         cost_estimate=pl.CostEstimate(flops=slots * rows * width, bytes_accessed=3 * slots * rows * width, transcendentals=0),
         name="settle",
-    )(asked, x)
+    )(asked, x, *earlier)
 
 
 def pick(parts, index):
@@ -247,12 +269,16 @@
     return lax.dynamic_slice(parts, start, (1,) + parts.shape[1:])[0]
 
 
-def sum_over_devices(terms):
+def after(a, *others):
+    return lax.optimization_barrier((a,) + others)[0]
+
+
+def sum_over_devices(keep, give, first_piece, send_second, others):
     f32, bf16 = jnp.float32, jnp.bfloat16
     region, slab = (lax.axis_index(axis).astype(jnp.uint32) for axis in ("region", "slab"))
     x = region & (SIDE - 1)
     z, core = slab >> 1, slab & 1
-    width = terms.shape[1]
+    width = keep.shape[1]
 
     def along_z(a, by):
         return lax.ppermute(a, "slab", [(p * 2 + c, (p + by) % SIDE * 2 + c) for p in range(SIDE) for c in range(2)])
@@ -277,17 +303,18 @@
         parts = [pick(stacked, (place - i) & (SIDE - 1)) for i in range(SIDE)]
         return jnp.concatenate(parts, axis=0)
 
-    halves = terms.reshape(2, terms.shape[0] // 2, width)
-    part = pick(halves, core) + swap(pick(halves, 1 - core).astype(bf16)).astype(f32)
+    part = keep + swap(give).astype(f32)
     part = scatter(part, along_z, z)
-    part = scatter(part, along_x, x).astype(bf16)
+    part = after(scatter(part, along_x, x).astype(bf16), first_piece)
     ring = [part.astype(f32)] + [along_y(part, by).astype(f32) for by in range(1, SIDE)]
     part = ((ring[0] + ring[2]) + (ring[1] + ring[3])).astype(bf16)
     part = gather(part, along_x, x)
+    second_piece = send_second(part)
     part = gather(part, along_z, z)
+    part = after(part, second_piece, *others)
     other = swap(part)
     first, second = jnp.where(core == 0, part, other), jnp.where(core == 0, other, part)
-    return jnp.concatenate([first, second], axis=0).astype(f32)
+    return jnp.concatenate([first, second], axis=0).astype(f32), second_piece
 
 
 def per_device(
@@ -306,14 +333,23 @@
     query = (nn(volume, w_query).astype(bf16) * head_dim ** -0.5).astype(bf16)
     grad_att = nt(cotangent, w_out).astype(bf16)
 
-    attended, grad_query, returning = attention(lists, counts, query, grad_att, blocks, key_weight, value_weight)
-
-    returned = lax.all_to_all(returning, "region", split_axis=0, concat_axis=0, tiled=True)
-    out_terms = lax.dot_general(attended, cotangent, (((0,), (0,)), ((), ())), preferred_element_type=f32)
-    grad_out_weight = sum_over_devices(out_terms)
+    core = (lax.axis_index("slab") & 1).reshape(1)
+    attended, grad_query, keep, give, *pieces = attention(
+        lists, counts, core, query, grad_att, cotangent, blocks, key_weight, value_weight
+    )
+    returned = lax.all_to_all(pieces[0], "region", split_axis=0, concat_axis=0, tiled=True)
+
     mixed = nn(attended, w_out).astype(bf16)
     grad_volume = nt(grad_query, w_query).astype(bf16)
-    grad_patches = settle(asked, returned, owned)
+    patches_piece = settle(asked, returned, owned, 0)
+
+    def send_second(summed):
+        return lax.all_to_all(after(pieces[1], summed), "region", split_axis=0, concat_axis=0, tiled=True)
+
+    grad_out_weight, later = sum_over_devices(
+        keep, give, returned, send_second, (mixed, grad_volume, patches_piece)
+    )
+    grad_patches = settle(asked, later, owned, 1, (patches_piece,))
     return mixed, grad_volume, grad_patches.reshape(owned * BLOCK, width), grad_out_weight
 
 

time: 256 us -> 227 us (0.89); the launches traced: 257 us -> 224 us
  waiting for transfers between devices: 120 us -> 81.8 us
  starting transfers between devices: 38.6 us -> 58.6 us
  Pallas kernels: 50.5 us -> 44.4 us
  local copies, waits for them, and re-layouts: 8.7 us -> 5.71 us
  matrix products: 14.9 us -> 12.1 us
  other arithmetic: 9.46 us -> 6.73 us
    ppermute x6, waiting for transfers between devices: 37.7 us -> 9.18 us  [along_x(): lax.ppermute(a, 'region', [(p * SIDE + i, p * SIDE + (i + by) % SIDE) for...]
    ppermute x6, waiting for transfers between devices: 27 us -> 11.1 us  [along_z(): lax.ppermute(a, 'slab', [(p * 2 + c, (p + by) % SIDE * 2 + c) for p in ra...]
    ppermute x2, starting transfers between devices: 2.16 us -> 12.8 us  [swap(): lax.ppermute(a, 'slab', [(p * 2 + c, p * 2 + 1 - c) for p in range(SIDE)...]
    all_to_all x1 -> x2, starting transfers between devices: 4.56 us -> 11.8 us  [the longest x1 6.09 us: per_device(): lax.all_to_all(pieces[0], 'region', split_axis=0, concat_axis=0, tiled=True)]
    pallas_call x1, Pallas kernels: 46.1 us -> 39.3 us  [attention(): pl.pallas_call(attention_kernel, in_specs=[smem] * 3 + [hbm] * 6, out_spe...]
    all_to_all x1 -> x2, waiting for transfers between devices: 0.01 us -> 6.32 us  [the longest x1 6.32 us: send_second(): lax.all_to_all(after(pieces[1], summed), 'region', split_axis=0, concat_a...]
    dot_general x2, matrix products: 7.82 us -> 4.47 us  [nn(): lax.dot_general(a, b, (((1,), (0,)), ((), ())), preferred_element_type=jn...]
    dot_general x2, matrix products: 4.55 us -> 7.65 us  [nt(): lax.dot_general(a, b, (((1,), (1,)), ((), ())), preferred_element_type=jn...]
  transfers between devices with their start and end apart: 19 -> 20, of which waited for: 12 -> 11; matrix products, arithmetic and copies ran while one was open for 8% -> 7% of each run, Pallas kernels for 0% -> 2%
where the time goes in v3:
time: 227 us; the launch traced here: 224 us
  waiting for transfers between devices  81.8 us (36%)
  starting transfers between devices  58.6 us (26%)
  Pallas kernels  44.4 us (20%)
  blocking collectives  13.8 us (6%)
  matrix products  12.1 us (5%)
  other arithmetic  6.73 us (3%)
  local copies, waits for them, and re-layouts  5.71 us (3%)
    all_to_all x1, waiting for transfers between devices, per_device(): lax.all_to_all(outgoing, 'region', split_axis=0, concat_axis=0, tiled=True)  53.2 us
    pallas_call x1, Pallas kernels, attention(): pl.pallas_call(attention_kernel, in_specs=[smem] * 3 + [hbm] * 6, out_spe...  39.3 us
    ppermute x6, starting transfers between devices, along_z(): lax.ppermute(a, 'slab', [(p * 2 + c, (p + by) % SIDE * 2 + c) for p in ra...  16.9 us
    all_to_all x1, blocking collectives, per_device(): lax.all_to_all(requests, 'region', split_axis=1, concat_axis=0, tiled=True)  13.8 us
    ppermute x2, starting transfers between devices, swap(): lax.ppermute(a, 'slab', [(p * 2 + c, p * 2 + 1 - c) for p in range(SIDE)...  12.8 us
    ppermute x6, waiting for transfers between devices, along_z(): lax.ppermute(a, 'slab', [(p * 2 + c, (p + by) % SIDE * 2 + c) for p in ra...  11.1 us
    ppermute x6, waiting for transfers between devices, along_x(): lax.ppermute(a, 'region', [(p * SIDE + i, p * SIDE + (i + by) % SIDE) for...  9.18 us
    dot_general x2, matrix products, nt(): lax.dot_general(a, b, (((1,), (1,)), ((), ())), preferred_element_type=jn...  7.65 us
  transfers between devices with their start and end apart: 20, of which 11 were waited for; matrix products, arithmetic and copies ran while one was open for 7% of the time, Pallas kernels for 2%

profile of v3, /device:TPU:1, one launch (start us, length us, event | category | flops | bytes accessed | tf_op | source)
XLA Modules:
  0.0 224.0 jit_solution(15033750085332421015)
XLA Ops:
  0.6 0.8 copy.16
  1.5 13.8 %all_to_all.24 = s32[1,16,1]{2,0,1:T(1,128)S(1)} all-to-all(s32[1,16,1]{2,0,1:T(1,128)S(1)} %copy.16), channel_id=1, replica_groups=mesh['region'=16,'slab'=8] {'region'}, dimensions={1} | all-to-all | bytes 128 | tf_op jit(solution)/shard_map/all_to_all | solution.py:328
  15.2 0.4 reduce.asked_ref
  15.7 2.8 %gather_fusion = bf16[16,128,1024]{2,1,0:T(8,128)(2,1)} fusion(bf16[4,128,1024]{2,1,0:T(8,128)(2,1)S(1)} %bitcast.60, s32[1024]{0:T(1024)S(1)} %pad_clamp_fusion), kind=kCustom, calls=%fused_computation | custom fusion | bytes 8388672 | tf_op jit(solution)/shard_map/gather | solution.py:330
  18.5 4.7 %all-to-all-start.1 = ((bf16[16,128,1024]{2,1,0:T(8,128)(2,1)}), bf16[16,128,1024]{2,1,0:T(8,128)(2,1)}, u32[]{:S(2)}, u32[]{:S(2)}) async-start(bf16[16,128,1024]{2,1,0:T(8,128)(2,1)} %gather_fusion), calls=%async_computation.1 | async-start | bytes 8388608 | tf_op jit(solution)/shard_map/all_to_all | solution.py:331
  23.2 3.6 %convolution_convert_fusion.2.ga_hbm = bf16[512,1024]{1,0:T(8,128)(2,1)} fusion(bf16[512,1024]{1,0:T(8,128)(2,1)} %cot_hbm.1, bf16[1024,1024]{1,0:T(8,128)(2,1)S(1)} %copy-done.3), kind=kOutput, calls=%fused_computation.5 | convolution fusion | flops 1074266112 | bytes 4194304 | tf_op jit(solution)/shard_map/dot_general | solution.py:18
  26.9 2.2 fusion.q_hbm
  29.1 53.2 %all-to-all-done.1.x_hbm = bf16[16,128,1024]{2,1,0:T(8,128)(2,1)} async-done(((bf16[16,128,1024]{2,1,0:T(8,128)(2,1)}), bf16[16,128,1024]{2,1,0:T(8,128)(2,1)}, u32[]{:S(2)}, u32[]{:S(2)}) %all-to-all-start.1) | async-done | bytes 4194336 | tf_op jit(solution)/shard_map/all_to_all | solution.py:331
  82.3 39.3 %attention.1 = (bf16[512,1024]{1,0:T(8,128)(2,1)}, bf16[512,1024]{1,0:T(8,128)(2,1)}, f32[512,1024]{1,0:T(8,128)}, bf16[512,1024]{1,0:T(8,128)(2,1)}, bf16[16,64...) custom-call(s32[4,4]{1,0:T(4,128)} %lists_ref.1, s32[4]{0:T(128)} %counts_ref.1, s32[1]{0:T(128)} %bitcast.core_ref, ...), custom_call_target="tpu_custom_call" | custom-call | flops 30064771072 | bytes 20971520 | tf_op jit(solution)/shard_map/attention/pallas_call | solution.py:207
  121.7 5.6 %collective-permute-start = (bf16[512,1024]{1,0:T(8,128)(2,1)}, bf16[512,1024]{1,0:T(8,128)(2,1)S(1)}, u32[]{:S(2)}, u32[]{:S(2)}) collective-permute-start(bf16[512,1024]{1,0:T(8,128)(2,1)} %get-tuple-element.17), channel_id=1, source_target_pairs={{0,1},{1,0},{2,3},{3,2},{4,5},{5,4},{6,7},{7,6},{8,9},{9,8},{10,11... | collective-permute-start | bytes 3145736 | tf_op jit(solution)/shard_map/ppermute | solution.py:293
  127.3 6.1 %all-to-all-start.2 = ((bf16[16,64,1024]{2,1,0:T(8,128)(2,1)}), bf16[16,64,1024]{2,1,0:T(8,128)(2,1)}, u32[]{:S(2)}, u32[]{:S(2)}) async-start(bf16[16,64,1024]{2,1,0:T(8,128)(2,1)} %get-tuple-element.18), calls=%async_computation.2 | async-start | bytes 4194304 | tf_op jit(solution)/shard_map/all_to_all | solution.py:340
  133.4 1.0 copy-done.1
  134.4 2.1 convert_add_fusion
  136.5 0.9 fusion.1
  137.5 1.6 collective-permute-start.1
  139.1 4.8 %collective-permute-start.2 = (bf16[128,1024]{1,0:T(8,128)(2,1)}, bf16[128,1024]{1,0:T(8,128)(2,1)}, u32[]{:S(2)}, u32[]{:S(2)}) collective-permute-start(bf16[128,1024]{1,0:T(8,128)(2,1)} %get-tuple-element.26), channel_id=1, source_target_pairs={{0,4},{1,5},{2,6},{3,7},{4,0},{5,1},{6,2},{7,3},{8,12},{9,13},{10,... | collective-permute-start | bytes 786440 | tf_op jit(solution)/shard_map/ppermute | solution.py:284
  143.9 2.1 collective-permute-start.3
  146.0 0.6 collective-permute-done.1
  146.6 9.7 %collective-permute-done.2 = bf16[128,1024]{1,0:T(8,128)(2,1)} collective-permute-done((bf16[128,1024]{1,0:T(8,128)(2,1)}, bf16[128,1024]{1,0:T(8,128)(2,1)}, u32[]{:S(2)}, u32[]{:S(2)}) %collective-permute-start.2) | collective-permute-done | bytes 262176 | tf_op jit(solution)/shard_map/ppermute | solution.py:284
  156.3 1.3 bitcast_add_fusion
  157.6 1.0 collective-permute-start.4
  158.6 2.4 %collective-permute-start.5 = (bf16[32,1024]{1,0:T(8,128)(2,1)S(1)}, bf16[32,1024]{1,0:T(8,128)(2,1)S(1)}, u32[]{:S(2)}, u32[]{:S(2)}) collective-permute-start(bf16[32,1024]{1,0:T(8,128)(2,1)S(1)} %get-tuple-element.33), channel_id=1, source_target_pairs={{0,16},{8,24},{16,0},{24,8},{32,48},{40,56},{48,32},{56,40},{64,80... | collective-permute-start | bytes 196616 | tf_op jit(solution)/shard_map/ppermute | solution.py:287
  161.0 1.2 collective-permute-start.6
  162.2 0.3 collective-permute-done.4
  162.5 5.8 %collective-permute-done.5 = bf16[32,1024]{1,0:T(8,128)(2,1)S(1)} collective-permute-done((bf16[32,1024]{1,0:T(8,128)(2,1)S(1)}, bf16[32,1024]{1,0:T(8,128)(2,1)S(1)}, u32[]{:S(2)}, u32[]{:S(2)}) %collective-permute-start.5) | collective-permute-done | bytes 65568 | tf_op jit(solution)/shard_map/ppermute | solution.py:287
  168.4 2.3 %collective-permute-start.7 = (bf16[32,1024]{1,0:T(8,128)(2,1)S(1)}, bf16[32,1024]{1,0:T(8,128)(2,1)S(1)}, u32[]{:S(2)}, u32[]{:S(2)}) collective-permute-start(bf16[32,1024]{1,0:T(8,128)(2,1)S(1)} %fusion.4), channel_id=1, source_target_pairs={{0,64},{32,96},{64,0},{96,32},{8,72},{40,104},{72,8},{104,40},{16,... | collective-permute-start | bytes 196616 | tf_op jit(solution)/shard_map/ppermute | solution.py:290
  170.7 2.7 %collective-permute-start.9 = (bf16[32,1024]{1,0:T(8,128)(2,1)S(1)}, bf16[32,1024]{1,0:T(8,128)(2,1)S(1)}, u32[]{:S(2)}, u32[]{:S(2)}) collective-permute-start(bf16[32,1024]{1,0:T(8,128)(2,1)S(1)} %fusion.4), channel_id=1, source_target_pairs={{0,96},{32,0},{64,32},{96,64},{8,104},{40,8},{72,40},{104,72},{16,... | collective-permute-start | bytes 196616 | tf_op jit(solution)/shard_map/ppermute | solution.py:290
  173.3 2.0 collective-permute-done.8
  175.4 0.1 collective-permute-start.10
  175.4 2.6 %collective-permute-start.11 = (bf16[32,1024]{1,0:T(8,128)(2,1)S(1)}, bf16[32,1024]{1,0:T(8,128)(2,1)S(1)}, u32[]{:S(2)}, u32[]{:S(2)}) collective-permute-start(bf16[32,1024]{1,0:T(8,128)(2,1)S(1)} %add_convert_fusion), channel_id=1, source_target_pairs={{0,16},{8,24},{16,0},{24,8},{32,48},{40,56},{48,32},{56,40},{64,80... | collective-permute-start | bytes 196616 | tf_op jit(solution)/shard_map/ppermute | solution.py:287
  178.1 1.7 collective-permute-done.10
  179.8 0.7 collective-permute-done.11
  180.5 0.7 collective-permute-done.12
  181.3 5.7 %all-to-all-start.3 = ((bf16[16,64,1024]{2,1,0:T(8,128)(2,1)}), bf16[16,64,1024]{2,1,0:T(8,128)(2,1)}, u32[]{:S(2)}, u32[]{:S(2)}) async-start(bf16[16,64,1024]{2,1,0:T(8,128)(2,1)} %get-tuple-element.20), calls=%async_computation.3 | async-start | bytes 4194304 | tf_op jit(solution)/shard_map/all_to_all | solution.py:347
  187.1 4.0 %convolution_convert_fusion = bf16[512,1024]{1,0:T(8,128)(2,1)} fusion(bf16[512,1024]{1,0:T(8,128)(2,1)S(1)} %copy-done.7, bf16[1024,1024]{1,0:T(8,128)(2,1)} %param.15), kind=kOutput, calls=%fused_computation.3 | convolution fusion | flops 1074266112 | bytes 4194304 | tf_op jit(solution)/shard_map/dot_general | solution.py:18
  191.1 1.8 collective-permute-start.13
  192.9 4.6 %collective-permute-start.14 = (bf16[128,1024]{1,0:T(8,128)(2,1)S(1)}, bf16[128,1024]{1,0:T(8,128)(2,1)S(1)}, u32[]{:S(2)}, u32[]{:S(2)}) collective-permute-start(bf16[128,1024]{1,0:T(8,128)(2,1)S(1)} %get-tuple-element.35), channel_id=1, source_target_pairs={{0,4},{1,5},{2,6},{3,7},{4,0},{5,1},{6,2},{7,3},{8,12},{9,13},{10,... | collective-permute-start | bytes 786440 | tf_op jit(solution)/shard_map/ppermute | solution.py:284
  197.5 2.1 collective-permute-start.15
  199.5 2.2 convolution_convert_fusion.1
  201.8 2.5 %settle.2.refs_0_ = bf16[4,128,1024]{2,1,0:T(8,128)(2,1)} custom-call(s32[16]{0:T(128)S(1)} %reduce.asked_ref, bf16[16,64,1024]{2,1,0:T(8,128)(2,1)} %all-to-all-done.2.x_ref), custom_call_target="tpu_custom_call" | custom-call | flops 1048576 | bytes 3145728 | tf_op jit(solution)/shard_map/settle/pallas_call | solution.py:250
  204.3 0.8 collective-permute-done.14
  205.0 0.1 pad_maximum_fusion
  205.2 0.1 dynamic-slice_bitcast_fusion.3
  205.3 6.3 %all-to-all-done.3.x_ref = bf16[16,64,1024]{2,1,0:T(8,128)(2,1)} async-done(((bf16[16,64,1024]{2,1,0:T(8,128)(2,1)}), bf16[16,64,1024]{2,1,0:T(8,128)(2,1)}, u32[]{:S(2)}, u32[]{:S(2)}) %all-to-all-start.3) | async-done | bytes 2097184 | tf_op jit(solution)/shard_map/all_to_all | solution.py:347
  211.7 7.2 %collective-permute-start.16 = (bf16[512,1024]{1,0:T(8,128)(2,1)S(1)}, bf16[512,1024]{1,0:T(8,128)(2,1)S(1)}, u32[]{:S(2)}, u32[]{:S(2)}) collective-permute-start(bf16[512,1024]{1,0:T(8,128)(2,1)S(1)} %pad_maximum_fusion.1), channel_id=1, source_target_pairs={{0,1},{1,0},{2,3},{3,2},{4,5},{5,4},{6,7},{7,6},{8,9},{9,8},{10,11... | collective-permute-start | bytes 3145736 | tf_op jit(solution)/shard_map/ppermute | solution.py:293
  218.9 2.5 %settle.3 = bf16[4,128,1024]{2,1,0:T(8,128)(2,1)} custom-call(s32[16]{0:T(128)S(1)} %reduce.asked_ref, bf16[16,64,1024]{2,1,0:T(8,128)(2,1)} %all-to-all-done.3.x_ref, bf16[4,128,1024]{2,1,0:T(8,128)(2,1)} %settle.2.refs_0_), custom_call_target="tpu_custom_call", output_to_operand_aliasing={{}: (2, {})} | custom-call | flops 1048576 | bytes 3145728 | tf_op jit(solution)/shard_map/settle/pallas_call | solution.py:250
  221.4 0.1 broadcast_select_fusion.1
  221.5 2.4 %maximum_convert_fusion = f32[1024,1024]{1,0:T(8,128)} fusion(bf16[512,1024]{1,0:T(8,128)(2,1)S(1)} %get-tuple-element.23, bf16[512,1024]{1,0:T(8,128)(2,1)S(1)} %get-tuple-element.22), kind=kLoop, calls=%fused_computation.1 | loop fusion | flops 4194304 | bytes 6291456 | tf_op jit(solution)/shard_map/convert_element_type | solution.py:317
  (35 shorter events, 0.4 us)
Async XLA Ops:
  0.6 15.0 %copy-start = (bf16[512,1024]{1,0:T(8,128)(2,1)S(1)}, bf16[512,1024]{1,0:T(8,128)(2,1)}, u32[]{:S(2)}) copy-start(bf16[512,1024]{1,0:T(8,128)(2,1)} %param.11) | copy-start | bytes 3145732
  18.5 4.7 %copy-start.3 = (bf16[1024,1024]{1,0:T(8,128)(2,1)S(1)}, bf16[1024,1024]{1,0:T(8,128)(2,1)}, u32[]{:S(2)}) copy-start(bf16[1024,1024]{1,0:T(8,128)(2,1)} %param.18) | copy-start | bytes 6291460
  18.5 63.8 %all-to-all-start.1 = ((bf16[16,128,1024]{2,1,0:T(8,128)(2,1)}), bf16[16,128,1024]{2,1,0:T(8,128)(2,1)}, u32[]{:S(2)}, u32[]{:S(2)}) async-start(bf16[16,128,1024]{2,1,0:T(8,128)(2,1)} %gather_fusion), calls=%async_computation.1 | async-start | bytes 8388608 | tf_op jit(solution)/shard_map/all_to_all | solution.py:331
  23.2 3.7 %copy-start.2 = (bf16[1024,1024]{1,0:T(8,128)(2,1)S(1)}, bf16[1024,1024]{1,0:T(8,128)(2,1)}, u32[]{:S(2)}) copy-start(bf16[1024,1024]{1,0:T(8,128)(2,1)} %param.15) | copy-start | bytes 6291460
  23.2 3.7 %copy-start.5 = (bf16[512,1024]{1,0:T(8,128)(2,1)S(1)}, bf16[512,1024]{1,0:T(8,128)(2,1)}, u32[]{:S(2)}) copy-start(bf16[512,1024]{1,0:T(8,128)(2,1)} %param.10) | copy-start | bytes 3145732
  121.7 11.8 %collective-permute-start = (bf16[512,1024]{1,0:T(8,128)(2,1)}, bf16[512,1024]{1,0:T(8,128)(2,1)S(1)}, u32[]{:S(2)}, u32[]{:S(2)}) collective-permute-start(bf16[512,1024]{1,0:T(8,128)(2,1)} %get-tuple-element.17), channel_id=1, source_target_pairs={{0,1},{1,0},{2,3},{3,2},{4,5},{5,4},{6,7},{7,6},{8,9},{9,8},{10,11... | collective-permute-start | bytes 3145736 | tf_op jit(solution)/shard_map/ppermute | solution.py:293
  127.3 41.0 %all-to-all-start.2 = ((bf16[16,64,1024]{2,1,0:T(8,128)(2,1)}), bf16[16,64,1024]{2,1,0:T(8,128)(2,1)}, u32[]{:S(2)}, u32[]{:S(2)}) async-start(bf16[16,64,1024]{2,1,0:T(8,128)(2,1)} %get-tuple-element.18), calls=%async_computation.2 | async-start | bytes 4194304 | tf_op jit(solution)/shard_map/all_to_all | solution.py:340
  133.4 1.0 copy-start.1
  137.5 9.1 %collective-permute-start.1 = (bf16[128,1024]{1,0:T(8,128)(2,1)}, bf16[128,1024]{1,0:T(8,128)(2,1)}, u32[]{:S(2)}, u32[]{:S(2)}) collective-permute-start(bf16[128,1024]{1,0:T(8,128)(2,1)} %get-tuple-element.24), channel_id=1, source_target_pairs={{0,2},{1,3},{2,4},{3,5},{4,6},{5,7},{6,0},{7,1},{8,10},{9,11},{10,... | collective-permute-start | bytes 786440 | tf_op jit(solution)/shard_map/ppermute | solution.py:284
  139.1 17.2 %collective-permute-start.2 = (bf16[128,1024]{1,0:T(8,128)(2,1)}, bf16[128,1024]{1,0:T(8,128)(2,1)}, u32[]{:S(2)}, u32[]{:S(2)}) collective-permute-start(bf16[128,1024]{1,0:T(8,128)(2,1)} %get-tuple-element.26), channel_id=1, source_target_pairs={{0,4},{1,5},{2,6},{3,7},{4,0},{5,1},{6,2},{7,3},{8,12},{9,13},{10,... | collective-permute-start | bytes 786440 | tf_op jit(solution)/shard_map/ppermute | solution.py:284
  143.9 12.4 %collective-permute-start.3 = (bf16[128,1024]{1,0:T(8,128)(2,1)S(1)}, bf16[128,1024]{1,0:T(8,128)(2,1)}, u32[]{:S(2)}, u32[]{:S(2)}) collective-permute-start(bf16[128,1024]{1,0:T(8,128)(2,1)S(1)} %get-tuple-element.25), channel_id=1, source_target_pairs={{0,6},{1,7},{2,0},{3,1},{4,2},{5,3},{6,4},{7,5},{8,14},{9,15},{10,... | collective-permute-start | bytes 786440 | tf_op jit(solution)/shard_map/ppermute | solution.py:284
  157.6 5.0 %collective-permute-start.4 = (bf16[32,1024]{1,0:T(8,128)(2,1)S(1)}, bf16[32,1024]{1,0:T(8,128)(2,1)S(1)}, u32[]{:S(2)}, u32[]{:S(2)}) collective-permute-start(bf16[32,1024]{1,0:T(8,128)(2,1)S(1)} %get-tuple-element.31), channel_id=1, source_target_pairs={{0,8},{8,16},{16,24},{24,0},{32,40},{40,48},{48,56},{56,32},{64,72... | collective-permute-start | bytes 196616 | tf_op jit(solution)/shard_map/ppermute | solution.py:287
  158.6 9.7 %collective-permute-start.5 = (bf16[32,1024]{1,0:T(8,128)(2,1)S(1)}, bf16[32,1024]{1,0:T(8,128)(2,1)S(1)}, u32[]{:S(2)}, u32[]{:S(2)}) collective-permute-start(bf16[32,1024]{1,0:T(8,128)(2,1)S(1)} %get-tuple-element.33), channel_id=1, source_target_pairs={{0,16},{8,24},{16,0},{24,8},{32,48},{40,56},{48,32},{56,40},{64,80... | collective-permute-start | bytes 196616 | tf_op jit(solution)/shard_map/ppermute | solution.py:287
  161.0 7.3 %collective-permute-start.6 = (bf16[32,1024]{1,0:T(8,128)(2,1)S(1)}, bf16[32,1024]{1,0:T(8,128)(2,1)S(1)}, u32[]{:S(2)}, u32[]{:S(2)}) collective-permute-start(bf16[32,1024]{1,0:T(8,128)(2,1)S(1)} %get-tuple-element.32), channel_id=1, source_target_pairs={{0,24},{8,0},{16,8},{24,16},{32,56},{40,32},{48,40},{56,48},{64,88... | collective-permute-start | bytes 196616 | tf_op jit(solution)/shard_map/ppermute | solution.py:287
  168.4 5.0 %collective-permute-start.7 = (bf16[32,1024]{1,0:T(8,128)(2,1)S(1)}, bf16[32,1024]{1,0:T(8,128)(2,1)S(1)}, u32[]{:S(2)}, u32[]{:S(2)}) collective-permute-start(bf16[32,1024]{1,0:T(8,128)(2,1)S(1)} %fusion.4), channel_id=1, source_target_pairs={{0,64},{32,96},{64,0},{96,32},{8,72},{40,104},{72,8},{104,40},{16,... | collective-permute-start | bytes 196616 | tf_op jit(solution)/shard_map/ppermute | solution.py:290
  170.7 4.7 %collective-permute-start.8 = (bf16[32,1024]{1,0:T(8,128)(2,1)S(1)}, bf16[32,1024]{1,0:T(8,128)(2,1)S(1)}, u32[]{:S(2)}, u32[]{:S(2)}) collective-permute-start(bf16[32,1024]{1,0:T(8,128)(2,1)S(1)} %fusion.4), channel_id=1, source_target_pairs={{0,32},{32,64},{64,96},{96,0},{8,40},{40,72},{72,104},{104,8},{16,... | collective-permute-start | bytes 196616 | tf_op jit(solution)/shard_map/ppermute | solution.py:290
  170.7 4.7 %collective-permute-start.9 = (bf16[32,1024]{1,0:T(8,128)(2,1)S(1)}, bf16[32,1024]{1,0:T(8,128)(2,1)S(1)}, u32[]{:S(2)}, u32[]{:S(2)}) collective-permute-start(bf16[32,1024]{1,0:T(8,128)(2,1)S(1)} %fusion.4), channel_id=1, source_target_pairs={{0,96},{32,0},{64,32},{96,64},{8,104},{40,8},{72,40},{104,72},{16,... | collective-permute-start | bytes 196616 | tf_op jit(solution)/shard_map/ppermute | solution.py:290
  175.4 4.4 %collective-permute-start.10 = (bf16[32,1024]{1,0:T(8,128)(2,1)S(1)}, bf16[32,1024]{1,0:T(8,128)(2,1)S(1)}, u32[]{:S(2)}, u32[]{:S(2)}) collective-permute-start(bf16[32,1024]{1,0:T(8,128)(2,1)S(1)} %add_convert_fusion), channel_id=1, source_target_pairs={{0,8},{8,16},{16,24},{24,0},{32,40},{40,48},{48,56},{56,32},{64,72... | collective-permute-start | bytes 196616 | tf_op jit(solution)/shard_map/ppermute | solution.py:287
  175.4 5.0 %collective-permute-start.11 = (bf16[32,1024]{1,0:T(8,128)(2,1)S(1)}, bf16[32,1024]{1,0:T(8,128)(2,1)S(1)}, u32[]{:S(2)}, u32[]{:S(2)}) collective-permute-start(bf16[32,1024]{1,0:T(8,128)(2,1)S(1)} %add_convert_fusion), channel_id=1, source_target_pairs={{0,16},{8,24},{16,0},{24,8},{32,48},{40,56},{48,32},{56,40},{64,80... | collective-permute-start | bytes 196616 | tf_op jit(solution)/shard_map/ppermute | solution.py:287
  178.1 3.1 %collective-permute-start.12 = (bf16[32,1024]{1,0:T(8,128)(2,1)S(1)}, bf16[32,1024]{1,0:T(8,128)(2,1)S(1)}, u32[]{:S(2)}, u32[]{:S(2)}) collective-permute-start(bf16[32,1024]{1,0:T(8,128)(2,1)S(1)} %add_convert_fusion), channel_id=1, source_target_pairs={{0,24},{8,0},{16,8},{24,16},{32,56},{40,32},{48,40},{56,48},{64,88... | collective-permute-start | bytes 196616 | tf_op jit(solution)/shard_map/ppermute | solution.py:287
  181.3 5.7 %copy-start.7 = (bf16[512,1024]{1,0:T(8,128)(2,1)S(1)}, bf16[512,1024]{1,0:T(8,128)(2,1)}, u32[]{:S(2)}) copy-start(bf16[512,1024]{1,0:T(8,128)(2,1)} %get-tuple-element.14) | copy-start | bytes 3145732
  181.3 30.3 %all-to-all-start.3 = ((bf16[16,64,1024]{2,1,0:T(8,128)(2,1)}), bf16[16,64,1024]{2,1,0:T(8,128)(2,1)}, u32[]{:S(2)}, u32[]{:S(2)}) async-start(bf16[16,64,1024]{2,1,0:T(8,128)(2,1)} %get-tuple-element.20), calls=%async_computation.3 | async-start | bytes 4194304 | tf_op jit(solution)/shard_map/all_to_all | solution.py:347
  187.1 12.4 %copy-start.4 = (bf16[1024,1024]{1,0:T(8,128)(2,1)S(1)}, bf16[1024,1024]{1,0:T(8,128)(2,1)}, u32[]{:S(2)}) copy-start(bf16[1024,1024]{1,0:T(8,128)(2,1)} %param.18) | copy-start | bytes 6291460
  187.1 12.4 %copy-start.6 = (bf16[512,1024]{1,0:T(8,128)(2,1)S(1)}, bf16[512,1024]{1,0:T(8,128)(2,1)}, u32[]{:S(2)}) copy-start(bf16[512,1024]{1,0:T(8,128)(2,1)} %get-tuple-element.13) | copy-start | bytes 3145732
  191.1 13.2 %collective-permute-start.13 = (bf16[128,1024]{1,0:T(8,128)(2,1)S(1)}, bf16[128,1024]{1,0:T(8,128)(2,1)S(1)}, u32[]{:S(2)}, u32[]{:S(2)}) collective-permute-start(bf16[128,1024]{1,0:T(8,128)(2,1)S(1)} %get-tuple-element.35), channel_id=1, source_target_pairs={{0,2},{1,3},{2,4},{3,5},{4,6},{5,7},{6,0},{7,1},{8,10},{9,11},{10,... | collective-permute-start | bytes 786440 | tf_op jit(solution)/shard_map/ppermute | solution.py:284
  192.9 12.2 %collective-permute-start.14 = (bf16[128,1024]{1,0:T(8,128)(2,1)S(1)}, bf16[128,1024]{1,0:T(8,128)(2,1)S(1)}, u32[]{:S(2)}, u32[]{:S(2)}) collective-permute-start(bf16[128,1024]{1,0:T(8,128)(2,1)S(1)} %get-tuple-element.35), channel_id=1, source_target_pairs={{0,4},{1,5},{2,6},{3,7},{4,0},{5,1},{6,2},{7,3},{8,12},{9,13},{10,... | collective-permute-start | bytes 786440 | tf_op jit(solution)/shard_map/ppermute | solution.py:284
  197.5 7.6 %collective-permute-start.15 = (bf16[128,1024]{1,0:T(8,128)(2,1)S(1)}, bf16[128,1024]{1,0:T(8,128)(2,1)S(1)}, u32[]{:S(2)}, u32[]{:S(2)}) collective-permute-start(bf16[128,1024]{1,0:T(8,128)(2,1)S(1)} %get-tuple-element.35), channel_id=1, source_target_pairs={{0,6},{1,7},{2,0},{3,1},{4,2},{5,3},{6,4},{7,5},{8,14},{9,15},{10,... | collective-permute-start | bytes 786440 | tf_op jit(solution)/shard_map/ppermute | solution.py:284
  211.7 9.7 %collective-permute-start.16 = (bf16[512,1024]{1,0:T(8,128)(2,1)S(1)}, bf16[512,1024]{1,0:T(8,128)(2,1)S(1)}, u32[]{:S(2)}, u32[]{:S(2)}) collective-permute-start(bf16[512,1024]{1,0:T(8,128)(2,1)S(1)} %pad_maximum_fusion.1), channel_id=1, source_target_pairs={{0,1},{1,0},{2,3},{3,2},{4,5},{5,4},{6,7},{7,6},{8,9},{9,8},{10,11... | collective-permute-start | bytes 3145736 | tf_op jit(solution)/shard_map/ppermute | solution.py:293

commit v4 on v3

--- a/solution.py
+++ b/solution.py
@@ -24,9 +24,9 @@
 
 def attention_kernel(
     lists_ref, counts_ref, core_ref, q_hbm, ga_hbm, cot_hbm, x_hbm, wk_hbm, wv_hbm,
-    att_ref, gq_ref, keep_ref, give_ref, ret0_hbm, ret1_hbm,
-    q_ref, ga_ref, cot_ref, att_t_ref, x_ref, wk_ref, wv_ref, k_ref, v_ref, kt_ref, vt_ref, acc_ref,
-    mask_ref, used_ref, order_ref, in_sems, out_sems,
+    att_hbm, gq_hbm, keep_hbm, give_hbm, ret0_hbm, ret1_hbm,
+    att_ref, gq_ref, keep_ref, give_ref, q_ref, ga_ref, cot_ref, att_t_ref, x_ref, wk_ref, wv_ref, k_ref, v_ref, kt_ref, vt_ref, acc_ref,
+    mask_ref, used_ref, order_ref, in_sems, out_sems, result_sems,
 ):
     bf16 = jnp.bfloat16
     slots, quads, rows, wide = k_ref.shape
@@ -37,7 +37,7 @@
     loads = [
         pltpu.make_async_copy(src, dst, in_sems.at[i])
         for i, (src, dst) in enumerate(
-            ((x_hbm, x_ref), (wk_hbm, wk_ref), (wv_hbm, wv_ref), (q_hbm, q_ref), (ga_hbm, ga_ref), (cot_hbm, cot_ref))
+            ((wk_hbm, wk_ref), (x_hbm, x_ref), (wv_hbm, wv_ref), (q_hbm, q_ref), (ga_hbm, ga_ref), (cot_hbm, cot_ref))
         )
     ]
     for load in loads:
@@ -65,22 +65,27 @@
 
     lax.fori_loop(0, slots, clear, 0)
 
-    for load in loads:
-        load.wait()
-
-    def project(b, carry):
-        ids = [order_ref[b * BATCH + i] for i in range(BATCH)]
-        x = jnp.concatenate([x_ref[s] for s in ids], axis=0)
-        for w_ref, out_ref, out_t_ref in ((wk_ref, k_ref, kt_ref), (wv_ref, v_ref, vt_ref)):
+    def project(w_ref, out_ref, out_t_ref):
+        def batch(b, carry):
+            ids = [order_ref[b * BATCH + i] for i in range(BATCH)]
+            x = jnp.concatenate([x_ref[s] for s in ids], axis=0)
             for quad in range(quads):
                 y = nn(x, w_ref[:, quad * wide:(quad + 1) * wide]).astype(bf16)
                 for i, s in enumerate(ids):
                     part = y[i * rows:(i + 1) * rows]
                     out_ref[s, quad] = part
                     out_t_ref[s, quad] = part.T
-        return carry
-
-    lax.fori_loop(0, batches, project, 0)
+            return carry
+
+        lax.fori_loop(0, batches, batch, 0)
+
+    for load in loads[:2]:
+        load.wait()
+    project(wk_ref, k_ref, kt_ref)
+    loads[2].wait()
+    project(wv_ref, v_ref, vt_ref)
+    for load in loads[3:]:
+        load.wait()
 
     head_of_row = lax.broadcasted_iota(jnp.int32, mask_ref.shape, 0) // per_group
     head_of_lane = lax.broadcasted_iota(jnp.int32, mask_ref.shape, 1) // head_dim
@@ -117,17 +122,26 @@
         )
         top = jnp.max(scores, axis=0, keepdims=True)
         expd = jnp.exp(scores - top)
-        total = jnp.sum(expd, axis=0, keepdims=True)
-        probs = expd * (1.0 / total)
+        inverse = 1.0 / jnp.sum(expd, axis=0, keepdims=True)
         grad_prob = nt(v4, g4)
-        delta = jnp.sum(probs * grad_prob, axis=0, keepdims=True)
+        delta = jnp.sum(expd * grad_prob, axis=0, keepdims=True) * inverse
+        probs = expd * inverse
         grad_score = (probs * (grad_prob - delta)).astype(bf16)
         probs_b = probs.astype(bf16)
-        att_parts = diagonal(nn(vt4, probs_b))
+        def paired(wt, p):
+            blocks = []
+            for h in range(0, QUAD, 2):
+                y = nn(wt[h * head_dim:(h + 2) * head_dim], p[:, h * per_group:(h + 2) * per_group])
+                blocks.append(
+                    jnp.concatenate([y[:head_dim, :per_group], y[head_dim:, per_group:]], axis=0)
+                )
+            return blocks
+
+        att_parts = paired(vt4, probs_b)
         att_ref[at_rows, at_cols] = jnp.concatenate([y.T for y in att_parts], axis=1).astype(bf16)
         att_t_ref[at_cols, at_rows] = jnp.concatenate(att_parts, axis=0).astype(bf16)
-        gq_parts = diagonal(nn(kt4, grad_score) * head_dim ** -0.5)
-        gq_ref[at_rows, at_cols] = jnp.concatenate([y.T for y in gq_parts], axis=1).astype(bf16)
+        gq_parts = paired(kt4, grad_score)
+        gq_ref[at_rows, at_cols] = (jnp.concatenate([y.T for y in gq_parts], axis=1) * head_dim ** -0.5).astype(bf16)
         grad_key = nn(grad_score, q4)
         grad_value = nn(probs_b, g4)
         for j in range(listed):
@@ -136,7 +150,25 @@
             acc_ref[s, quads + c] += grad_value[j * rows:(j + 1) * rows]
         return carry
 
-    lax.fori_loop(0, groups * quads, step, 0, unroll=2)
+    lax.fori_loop(0, groups * quads, step, 0, unroll=4)
+
+    results = [
+        pltpu.make_async_copy(src, dst, result_sems.at[i])
+        for i, (src, dst) in enumerate(
+            ((att_ref, att_hbm), (gq_ref, gq_hbm), (keep_ref, keep_hbm), (give_ref, give_hbm))
+        )
+    ]
+    for result in results[:2]:
+        result.start()
+
+    half = keep_ref.shape[0]
+    core = core_ref[0]
+    for out_ref, mine in ((keep_ref, core), (give_ref, 1 - core)):
+        for c in range(half // wide):
+            at = pl.ds(pl.multiple_of(mine * half + c * wide, wide), wide)
+            out_ref[c * wide:(c + 1) * wide, :] = nn(att_t_ref[at, :], cot_ref[...]).astype(out_ref.dtype)
+    for result in results[2:]:
+        result.start()
 
     def send(i, s):
         cut = rows // PIECES
@@ -178,19 +210,14 @@
 
     lax.fori_loop(batches * BATCH, slots, nothing, 0)
 
-    half = keep_ref.shape[0]
-    core = core_ref[0]
-    for out_ref, mine in ((keep_ref, core), (give_ref, 1 - core)):
-        for c in range(half // wide):
-            at = pl.ds(pl.multiple_of(mine * half + c * wide, wide), wide)
-            out_ref[c * wide:(c + 1) * wide, :] = nn(att_t_ref[at, :], cot_ref[...]).astype(out_ref.dtype)
-
     def arrive(i, carry):
         for copy in send(i, order_ref[i]):
             copy.wait()
         return carry
 
     lax.fori_loop(0, slots, arrive, 0)
+    for result in results:
+        result.wait()
 
 
 def attention(lists, counts, core, q, ga, cot, x, wk, wv):
@@ -199,7 +226,6 @@
     quads = HEADS // QUAD
     wide = width // quads
     smem = pl.BlockSpec(memory_space=pltpu.SMEM)
-    vmem = pl.BlockSpec(memory_space=pltpu.VMEM)
     hbm = pl.BlockSpec(memory_space=pl.ANY)
     scores = HEADS * q.shape[0] * lists.shape[1] * rows
     straight = pltpu.VMEM((slots, quads, rows, wide), bf16)
@@ -207,7 +233,7 @@
     return pl.pallas_call(
         attention_kernel,
         in_specs=[smem] * 3 + [hbm] * 6,
-        out_specs=[vmem] * 4 + [hbm] * PIECES,
+        out_specs=[hbm] * (4 + PIECES),
         out_shape=[
             jax.ShapeDtypeStruct(q.shape, bf16),
             jax.ShapeDtypeStruct(q.shape, bf16),
@@ -215,6 +241,8 @@
             jax.ShapeDtypeStruct((width // 2, width), bf16),
         ] + [jax.ShapeDtypeStruct((slots, rows // PIECES, width), bf16)] * PIECES,
         scratch_shapes=[
+            pltpu.VMEM(q.shape, bf16), pltpu.VMEM(q.shape, bf16),
+            pltpu.VMEM((width // 2, width), jnp.float32), pltpu.VMEM((width // 2, width), bf16),
             pltpu.VMEM(q.shape, bf16), pltpu.VMEM(q.shape, bf16), pltpu.VMEM(q.shape, bf16),
             pltpu.VMEM(q.shape[::-1], bf16), pltpu.VMEM(x.shape, bf16),
             pltpu.VMEM(wk.shape, bf16), pltpu.VMEM(wv.shape, bf16),
@@ -225,6 +253,7 @@
             pltpu.SMEM((slots + 1,), jnp.int32),
             pltpu.SemaphoreType.DMA((6,)),
             pltpu.SemaphoreType.DMA((slots, PIECES)),
+            pltpu.SemaphoreType.DMA((4,)),
         ],
         compiler_params=pltpu.CompilerParams(vmem_limit_bytes=62 * MIB),
         cost_estimate=pl.CostEstimate(
@@ -325,8 +354,7 @@
     width = volume.shape[1]
     head_dim = width // HEADS
     owned = patches.shape[0] // BLOCK
-    asked = lax.all_to_all(requests, "region", split_axis=1, concat_axis=0, tiled=True)
-    asked = asked.reshape(-1)
+    asked = lax.all_to_all(requests.reshape(-1), "region", split_axis=0, concat_axis=0, tiled=True)
     outgoing = patches.reshape(owned, BLOCK, width)[asked]
     blocks = lax.all_to_all(outgoing, "region", split_axis=0, concat_axis=0, tiled=True)
 

time: 227 us -> 222 us (0.978)
  starting transfers between devices: 58.6 us -> 50.8 us
  waiting for transfers between devices: 81.8 us -> 87.2 us
    ppermute x6, starting transfers between devices: 16.9 us -> 11.2 us  [along_z(): lax.ppermute(a, 'slab', [(p * 2 + c, (p + by) % SIDE * 2 + c) for p in ra...]
    ppermute x2, starting transfers between devices: 12.8 us -> 7.61 us  [swap(): lax.ppermute(a, 'slab', [(p * 2 + c, p * 2 + 1 - c) for p in range(SIDE)...]
    all_to_all x1, starting transfers between devices: 6.09 us -> 9.12 us  [per_device(): lax.all_to_all(pieces[0], 'region', split_axis=0, concat_axis=0, tiled=True)]
  transfers between devices with their start and end apart: 20 -> 20, of which waited for: 11 -> 10; matrix products, arithmetic and copies ran while one was open for 7% -> 8% of each run, Pallas kernels for 2% -> 2%
where the time goes in v4:
time: 222 us; the launch traced here: 220 us
  waiting for transfers between devices  87.2 us (39%)
  starting transfers between devices  50.8 us (23%)
  Pallas kernels  42.5 us (19%)
  blocking collectives  13.8 us (6%)
  matrix products  12.1 us (5%)
  other arithmetic  6.73 us (3%)
  local copies, waits for them, and re-layouts  5.71 us (3%)
    all_to_all x1, waiting for transfers between devices, per_device(): lax.all_to_all(outgoing, 'region', split_axis=0, concat_axis=0, tiled=True)  53.2 us
    pallas_call x1, Pallas kernels, attention(): pl.pallas_call(attention_kernel, in_specs=[smem] * 3 + [hbm] * 6, out_spe...  37.5 us
    all_to_all x1, blocking collectives, per_device(): lax.all_to_all(requests.reshape(-1), 'region', split_axis=0, concat_axis=...  13.8 us
    ppermute x6, waiting for transfers between devices, along_z(): lax.ppermute(a, 'slab', [(p * 2 + c, (p + by) % SIDE * 2 + c) for p in ra...  13.3 us
    ppermute x6, starting transfers between devices, along_z(): lax.ppermute(a, 'slab', [(p * 2 + c, (p + by) % SIDE * 2 + c) for p in ra...  11.2 us
    ppermute x6, waiting for transfers between devices, along_x(): lax.ppermute(a, 'region', [(p * SIDE + i, p * SIDE + (i + by) % SIDE) for...  10.8 us
    all_to_all x1, starting transfers between devices, per_device(): lax.all_to_all(pieces[0], 'region', split_axis=0, concat_axis=0, tiled=True)  9.12 us
    all_to_all x1, waiting for transfers between devices, send_second(): lax.all_to_all(after(pieces[1], summed), 'region', split_axis=0, concat_a...  7.96 us
  transfers between devices with their start and end apart: 20, of which 10 were waited for; matrix products, arithmetic and copies ran while one was open for 8% of the time, Pallas kernels for 2%

profile of v4, /device:TPU:1, one launch (start us, length us, event | category | flops | bytes accessed | tf_op | source)
XLA Modules:
  0.0 219.8 jit_solution(9279978923573032401)
XLA Ops:
  0.6 0.8 copy.16
  1.5 13.8 %all_to_all.29 = s32[16,1,1]{2,1,0:T(1,128)S(1)} all-to-all(s32[16,1,1]{2,1,0:T(1,128)S(1)} %copy.16), channel_id=1, replica_groups=mesh['region'=16,'slab'=8] {'region'}, dimensions={0} | all-to-all | bytes 128 | tf_op jit(solution)/shard_map/all_to_all | solution.py:357
  15.2 0.4 reduce.asked_ref
  15.7 2.8 %gather_fusion = bf16[16,128,1024]{2,1,0:T(8,128)(2,1)} fusion(bf16[4,128,1024]{2,1,0:T(8,128)(2,1)S(1)} %bitcast.61, s32[1024]{0:T(1024)S(1)} %pad_clamp_fusion), kind=kCustom, calls=%fused_computation | custom fusion | bytes 8388672 | tf_op jit(solution)/shard_map/gather | solution.py:358
  18.5 4.7 %all-to-all-start.1 = ((bf16[16,128,1024]{2,1,0:T(8,128)(2,1)}), bf16[16,128,1024]{2,1,0:T(8,128)(2,1)}, u32[]{:S(2)}, u32[]{:S(2)}) async-start(bf16[16,128,1024]{2,1,0:T(8,128)(2,1)} %gather_fusion), calls=%async_computation.1 | async-start | bytes 8388608 | tf_op jit(solution)/shard_map/all_to_all | solution.py:359
  23.2 3.6 %convolution_convert_fusion.2.ga_hbm = bf16[512,1024]{1,0:T(8,128)(2,1)} fusion(bf16[512,1024]{1,0:T(8,128)(2,1)} %cot_hbm.1, bf16[1024,1024]{1,0:T(8,128)(2,1)S(1)} %copy-done.3), kind=kOutput, calls=%fused_computation.5 | convolution fusion | flops 1074266112 | bytes 4194304 | tf_op jit(solution)/shard_map/dot_general | solution.py:18
  26.9 2.2 %fusion.q_hbm = bf16[512,1024]{1,0:T(8,128)(2,1)} fusion(bf16[512,1024]{1,0:T(8,128)(2,1)S(1)} %copy-done.5, bf16[1024,1024]{1,0:T(8,128)(2,1)S(1)} %copy-done.2), kind=kOutput, calls=%fused_computation.7 | convolution fusion | flops 1074790400 | bytes 4194304 | tf_op jit(solution)/shard_map/dot_general | solution.py:22
  29.1 53.2 %all-to-all-done.1.x_hbm = bf16[16,128,1024]{2,1,0:T(8,128)(2,1)} async-done(((bf16[16,128,1024]{2,1,0:T(8,128)(2,1)}), bf16[16,128,1024]{2,1,0:T(8,128)(2,1)}, u32[]{:S(2)}, u32[]{:S(2)}) %all-to-all-start.1) | async-done | bytes 4194336 | tf_op jit(solution)/shard_map/all_to_all | solution.py:359
  82.3 37.5 %attention.1 = (bf16[512,1024]{1,0:T(8,128)(2,1)}, bf16[512,1024]{1,0:T(8,128)(2,1)}, f32[512,1024]{1,0:T(8,128)}, bf16[512,1024]{1,0:T(8,128)(2,1)}, bf16[16,64...) custom-call(s32[4,4]{1,0:T(4,128)} %lists_ref.1, s32[4]{0:T(128)} %counts_ref.1, s32[1]{0:T(128)} %bitcast.core_ref, ...), custom_call_target="tpu_custom_call" | custom-call | flops 30064771072 | bytes 20971520 | tf_op jit(solution)/shard_map/attention/pallas_call | solution.py:233
  119.8 0.3 collective-permute-start
  120.1 9.1 %all-to-all-start.2 = ((bf16[16,64,1024]{2,1,0:T(8,128)(2,1)}), bf16[16,64,1024]{2,1,0:T(8,128)(2,1)}, u32[]{:S(2)}, u32[]{:S(2)}) async-start(bf16[16,64,1024]{2,1,0:T(8,128)(2,1)} %get-tuple-element.18), calls=%async_computation.2 | async-start | bytes 4194304 | tf_op jit(solution)/shard_map/all_to_all | solution.py:368
  129.3 1.0 copy-done.1
  130.3 2.1 convert_add_fusion
  132.4 0.9 fusion.1
  133.3 2.6 %collective-permute-start.1 = (bf16[128,1024]{1,0:T(8,128)(2,1)}, bf16[128,1024]{1,0:T(8,128)(2,1)}, u32[]{:S(2)}, u32[]{:S(2)}) collective-permute-start(bf16[128,1024]{1,0:T(8,128)(2,1)} %get-tuple-element.24), channel_id=1, source_target_pairs={{0,2},{1,3},{2,4},{3,5},{4,6},{5,7},{6,0},{7,1},{8,10},{9,11},{10,... | collective-permute-start | bytes 786440 | tf_op jit(solution)/shard_map/ppermute | solution.py:313
  135.9 2.4 %collective-permute-start.2 = (bf16[128,1024]{1,0:T(8,128)(2,1)}, bf16[128,1024]{1,0:T(8,128)(2,1)}, u32[]{:S(2)}, u32[]{:S(2)}) collective-permute-start(bf16[128,1024]{1,0:T(8,128)(2,1)} %get-tuple-element.26), channel_id=1, source_target_pairs={{0,4},{1,5},{2,6},{3,7},{4,0},{5,1},{6,2},{7,3},{8,12},{9,13},{10,... | collective-permute-start | bytes 786440 | tf_op jit(solution)/shard_map/ppermute | solution.py:313
  138.3 0.5 collective-permute-start.3
  138.8 5.1 %collective-permute-done.1 = bf16[128,1024]{1,0:T(8,128)(2,1)} collective-permute-done((bf16[128,1024]{1,0:T(8,128)(2,1)}, bf16[128,1024]{1,0:T(8,128)(2,1)}, u32[]{:S(2)}, u32[]{:S(2)}) %collective-permute-start.1) | collective-permute-done | bytes 262176 | tf_op jit(solution)/shard_map/ppermute | solution.py:313
  143.9 6.5 %collective-permute-done.2 = bf16[128,1024]{1,0:T(8,128)(2,1)} collective-permute-done((bf16[128,1024]{1,0:T(8,128)(2,1)}, bf16[128,1024]{1,0:T(8,128)(2,1)}, u32[]{:S(2)}, u32[]{:S(2)}) %collective-permute-start.2) | collective-permute-done | bytes 262176 | tf_op jit(solution)/shard_map/ppermute | solution.py:313
  150.4 1.3 bitcast_add_fusion
  151.7 1.0 collective-permute-start.4
  152.7 2.4 %collective-permute-start.5 = (bf16[32,1024]{1,0:T(8,128)(2,1)S(1)}, bf16[32,1024]{1,0:T(8,128)(2,1)S(1)}, u32[]{:S(2)}, u32[]{:S(2)}) collective-permute-start(bf16[32,1024]{1,0:T(8,128)(2,1)S(1)} %get-tuple-element.33), channel_id=1, source_target_pairs={{0,16},{8,24},{16,0},{24,8},{32,48},{40,56},{48,32},{56,40},{64,80... | collective-permute-start | bytes 196616 | tf_op jit(solution)/shard_map/ppermute | solution.py:316
  155.1 1.2 collective-permute-start.6
  156.3 2.1 collective-permute-done.4
  158.4 5.8 %collective-permute-done.5 = bf16[32,1024]{1,0:T(8,128)(2,1)S(1)} collective-permute-done((bf16[32,1024]{1,0:T(8,128)(2,1)S(1)}, bf16[32,1024]{1,0:T(8,128)(2,1)S(1)}, u32[]{:S(2)}, u32[]{:S(2)}) %collective-permute-start.5) | collective-permute-done | bytes 65568 | tf_op jit(solution)/shard_map/ppermute | solution.py:316
  164.3 2.3 %collective-permute-start.7 = (bf16[32,1024]{1,0:T(8,128)(2,1)S(1)}, bf16[32,1024]{1,0:T(8,128)(2,1)S(1)}, u32[]{:S(2)}, u32[]{:S(2)}) collective-permute-start(bf16[32,1024]{1,0:T(8,128)(2,1)S(1)} %fusion.4), channel_id=1, source_target_pairs={{0,64},{32,96},{64,0},{96,32},{8,72},{40,104},{72,8},{104,40},{16,... | collective-permute-start | bytes 196616 | tf_op jit(solution)/shard_map/ppermute | solution.py:319
  166.6 2.7 %collective-permute-start.9 = (bf16[32,1024]{1,0:T(8,128)(2,1)S(1)}, bf16[32,1024]{1,0:T(8,128)(2,1)S(1)}, u32[]{:S(2)}, u32[]{:S(2)}) collective-permute-start(bf16[32,1024]{1,0:T(8,128)(2,1)S(1)} %fusion.4), channel_id=1, source_target_pairs={{0,96},{32,0},{64,32},{96,64},{8,104},{40,8},{72,40},{104,72},{16,... | collective-permute-start | bytes 196616 | tf_op jit(solution)/shard_map/ppermute | solution.py:319
  169.3 1.9 collective-permute-done.8
  171.2 0.1 collective-permute-start.10
  171.3 2.0 collective-permute-start.11
  173.3 0.6 collective-permute-start.12
  173.9 2.3 %collective-permute-done.10 = bf16[32,1024]{1,0:T(8,128)(2,1)S(1)} collective-permute-done((bf16[32,1024]{1,0:T(8,128)(2,1)S(1)}, bf16[32,1024]{1,0:T(8,128)(2,1)S(1)}, u32[]{:S(2)}, u32[]{:S(2)}) %collective-permute-start.10) | collective-permute-done | bytes 65568 | tf_op jit(solution)/shard_map/ppermute | solution.py:316
  176.3 0.6 collective-permute-done.12
  177.0 5.9 %all-to-all-start.3 = ((bf16[16,64,1024]{2,1,0:T(8,128)(2,1)}), bf16[16,64,1024]{2,1,0:T(8,128)(2,1)}, u32[]{:S(2)}, u32[]{:S(2)}) async-start(bf16[16,64,1024]{2,1,0:T(8,128)(2,1)} %get-tuple-element.20), calls=%async_computation.3 | async-start | bytes 4194304 | tf_op jit(solution)/shard_map/all_to_all | solution.py:375
  182.9 4.0 %convolution_convert_fusion = bf16[512,1024]{1,0:T(8,128)(2,1)} fusion(bf16[512,1024]{1,0:T(8,128)(2,1)S(1)} %copy-done.7, bf16[1024,1024]{1,0:T(8,128)(2,1)} %param.15), kind=kOutput, calls=%fused_computation.3 | convolution fusion | flops 1074266112 | bytes 4194304 | tf_op jit(solution)/shard_map/dot_general | solution.py:18
  186.9 3.3 %collective-permute-start.13 = (bf16[128,1024]{1,0:T(8,128)(2,1)S(1)}, bf16[128,1024]{1,0:T(8,128)(2,1)S(1)}, u32[]{:S(2)}, u32[]{:S(2)}) collective-permute-start(bf16[128,1024]{1,0:T(8,128)(2,1)S(1)} %get-tuple-element.35), channel_id=1, source_target_pairs={{0,2},{1,3},{2,4},{3,5},{4,6},{5,7},{6,0},{7,1},{8,10},{9,11},{10,... | collective-permute-start | bytes 786440 | tf_op jit(solution)/shard_map/ppermute | solution.py:313
  190.2 1.7 collective-permute-start.14
  191.9 0.7 collective-permute-start.15
  192.6 2.2 %convolution_convert_fusion.1 = bf16[512,1024]{1,0:T(8,128)(2,1)} fusion(bf16[512,1024]{1,0:T(8,128)(2,1)S(1)} %copy-done.6, bf16[1024,1024]{1,0:T(8,128)(2,1)S(1)} %copy-done.4), kind=kOutput, calls=%fused_computation.4 | convolution fusion | flops 1074266112 | bytes 4194304 | tf_op jit(solution)/shard_map/dot_general | solution.py:22
  194.9 2.5 %settle.2.refs_0_ = bf16[4,128,1024]{2,1,0:T(8,128)(2,1)} custom-call(s32[16]{0:T(128)S(1)} %reduce.asked_ref, bf16[16,64,1024]{2,1,0:T(8,128)(2,1)} %all-to-all-done.2.x_ref), custom_call_target="tpu_custom_call" | custom-call | flops 1048576 | bytes 3145728 | tf_op jit(solution)/shard_map/settle/pallas_call | solution.py:279
  197.4 1.8 collective-permute-done.14
  199.1 0.1 pad_maximum_fusion
  199.3 0.1 dynamic-slice_bitcast_fusion.3
  199.4 8.0 %all-to-all-done.3.x_ref = bf16[16,64,1024]{2,1,0:T(8,128)(2,1)} async-done(((bf16[16,64,1024]{2,1,0:T(8,128)(2,1)}), bf16[16,64,1024]{2,1,0:T(8,128)(2,1)}, u32[]{:S(2)}, u32[]{:S(2)}) %all-to-all-start.3) | async-done | bytes 2097184 | tf_op jit(solution)/shard_map/all_to_all | solution.py:375
  207.4 7.3 %collective-permute-start.16 = (bf16[512,1024]{1,0:T(8,128)(2,1)S(1)}, bf16[512,1024]{1,0:T(8,128)(2,1)S(1)}, u32[]{:S(2)}, u32[]{:S(2)}) collective-permute-start(bf16[512,1024]{1,0:T(8,128)(2,1)S(1)} %pad_maximum_fusion.1), channel_id=1, source_target_pairs={{0,1},{1,0},{2,3},{3,2},{4,5},{5,4},{6,7},{7,6},{8,9},{9,8},{10,11... | collective-permute-start | bytes 3145736 | tf_op jit(solution)/shard_map/ppermute | solution.py:322
  214.7 2.5 %settle.3 = bf16[4,128,1024]{2,1,0:T(8,128)(2,1)} custom-call(s32[16]{0:T(128)S(1)} %reduce.asked_ref, bf16[16,64,1024]{2,1,0:T(8,128)(2,1)} %all-to-all-done.3.x_ref, bf16[4,128,1024]{2,1,0:T(8,128)(2,1)} %settle.2.refs_0_), custom_call_target="tpu_custom_call", output_to_operand_aliasing={{}: (2, {})} | custom-call | flops 1048576 | bytes 3145728 | tf_op jit(solution)/shard_map/settle/pallas_call | solution.py:279
  217.2 0.1 broadcast_select_fusion.1
  217.3 2.4 %maximum_convert_fusion = f32[1024,1024]{1,0:T(8,128)} fusion(bf16[512,1024]{1,0:T(8,128)(2,1)S(1)} %get-tuple-element.23, bf16[512,1024]{1,0:T(8,128)(2,1)S(1)} %get-tuple-element.22), kind=kLoop, calls=%fused_computation.1 | loop fusion | flops 4194304 | bytes 6291456 | tf_op jit(solution)/shard_map/convert_element_type | solution.py:346
  (35 shorter events, 0.4 us)
Async XLA Ops:
  0.6 15.0 %copy-start = (bf16[512,1024]{1,0:T(8,128)(2,1)S(1)}, bf16[512,1024]{1,0:T(8,128)(2,1)}, u32[]{:S(2)}) copy-start(bf16[512,1024]{1,0:T(8,128)(2,1)} %param.11) | copy-start | bytes 3145732
  18.5 4.7 %copy-start.3 = (bf16[1024,1024]{1,0:T(8,128)(2,1)S(1)}, bf16[1024,1024]{1,0:T(8,128)(2,1)}, u32[]{:S(2)}) copy-start(bf16[1024,1024]{1,0:T(8,128)(2,1)} %param.18) | copy-start | bytes 6291460
  18.5 63.8 %all-to-all-start.1 = ((bf16[16,128,1024]{2,1,0:T(8,128)(2,1)}), bf16[16,128,1024]{2,1,0:T(8,128)(2,1)}, u32[]{:S(2)}, u32[]{:S(2)}) async-start(bf16[16,128,1024]{2,1,0:T(8,128)(2,1)} %gather_fusion), calls=%async_computation.1 | async-start | bytes 8388608 | tf_op jit(solution)/shard_map/all_to_all | solution.py:359
  23.2 3.7 %copy-start.2 = (bf16[1024,1024]{1,0:T(8,128)(2,1)S(1)}, bf16[1024,1024]{1,0:T(8,128)(2,1)}, u32[]{:S(2)}) copy-start(bf16[1024,1024]{1,0:T(8,128)(2,1)} %param.15) | copy-start | bytes 6291460
  23.2 3.7 %copy-start.5 = (bf16[512,1024]{1,0:T(8,128)(2,1)S(1)}, bf16[512,1024]{1,0:T(8,128)(2,1)}, u32[]{:S(2)}) copy-start(bf16[512,1024]{1,0:T(8,128)(2,1)} %param.10) | copy-start | bytes 3145732
  119.8 9.5 %collective-permute-start = (bf16[512,1024]{1,0:T(8,128)(2,1)}, bf16[512,1024]{1,0:T(8,128)(2,1)S(1)}, u32[]{:S(2)}, u32[]{:S(2)}) collective-permute-start(bf16[512,1024]{1,0:T(8,128)(2,1)} %get-tuple-element.17), channel_id=1, source_target_pairs={{0,1},{1,0},{2,3},{3,2},{4,5},{5,4},{6,7},{7,6},{8,9},{9,8},{10,11... | collective-permute-start | bytes 3145736 | tf_op jit(solution)/shard_map/ppermute | solution.py:322
  120.1 44.1 %all-to-all-start.2 = ((bf16[16,64,1024]{2,1,0:T(8,128)(2,1)}), bf16[16,64,1024]{2,1,0:T(8,128)(2,1)}, u32[]{:S(2)}, u32[]{:S(2)}) async-start(bf16[16,64,1024]{2,1,0:T(8,128)(2,1)} %get-tuple-element.18), calls=%async_computation.2 | async-start | bytes 4194304 | tf_op jit(solution)/shard_map/all_to_all | solution.py:368
  129.3 1.0 copy-start.1
  133.3 10.6 %collective-permute-start.1 = (bf16[128,1024]{1,0:T(8,128)(2,1)}, bf16[128,1024]{1,0:T(8,128)(2,1)}, u32[]{:S(2)}, u32[]{:S(2)}) collective-permute-start(bf16[128,1024]{1,0:T(8,128)(2,1)} %get-tuple-element.24), channel_id=1, source_target_pairs={{0,2},{1,3},{2,4},{3,5},{4,6},{5,7},{6,0},{7,1},{8,10},{9,11},{10,... | collective-permute-start | bytes 786440 | tf_op jit(solution)/shard_map/ppermute | solution.py:313
  135.9 14.4 %collective-permute-start.2 = (bf16[128,1024]{1,0:T(8,128)(2,1)}, bf16[128,1024]{1,0:T(8,128)(2,1)}, u32[]{:S(2)}, u32[]{:S(2)}) collective-permute-start(bf16[128,1024]{1,0:T(8,128)(2,1)} %get-tuple-element.26), channel_id=1, source_target_pairs={{0,4},{1,5},{2,6},{3,7},{4,0},{5,1},{6,2},{7,3},{8,12},{9,13},{10,... | collective-permute-start | bytes 786440 | tf_op jit(solution)/shard_map/ppermute | solution.py:313
  138.3 12.1 %collective-permute-start.3 = (bf16[128,1024]{1,0:T(8,128)(2,1)S(1)}, bf16[128,1024]{1,0:T(8,128)(2,1)}, u32[]{:S(2)}, u32[]{:S(2)}) collective-permute-start(bf16[128,1024]{1,0:T(8,128)(2,1)S(1)} %get-tuple-element.25), channel_id=1, source_target_pairs={{0,6},{1,7},{2,0},{3,1},{4,2},{5,3},{6,4},{7,5},{8,14},{9,15},{10,... | collective-permute-start | bytes 786440 | tf_op jit(solution)/shard_map/ppermute | solution.py:313
  151.7 6.7 %collective-permute-start.4 = (bf16[32,1024]{1,0:T(8,128)(2,1)S(1)}, bf16[32,1024]{1,0:T(8,128)(2,1)S(1)}, u32[]{:S(2)}, u32[]{:S(2)}) collective-permute-start(bf16[32,1024]{1,0:T(8,128)(2,1)S(1)} %get-tuple-element.31), channel_id=1, source_target_pairs={{0,8},{8,16},{16,24},{24,0},{32,40},{40,48},{48,56},{56,32},{64,72... | collective-permute-start | bytes 196616 | tf_op jit(solution)/shard_map/ppermute | solution.py:316
  152.7 11.5 %collective-permute-start.5 = (bf16[32,1024]{1,0:T(8,128)(2,1)S(1)}, bf16[32,1024]{1,0:T(8,128)(2,1)S(1)}, u32[]{:S(2)}, u32[]{:S(2)}) collective-permute-start(bf16[32,1024]{1,0:T(8,128)(2,1)S(1)} %get-tuple-element.33), channel_id=1, source_target_pairs={{0,16},{8,24},{16,0},{24,8},{32,48},{40,56},{48,32},{56,40},{64,80... | collective-permute-start | bytes 196616 | tf_op jit(solution)/shard_map/ppermute | solution.py:316
  155.1 9.1 %collective-permute-start.6 = (bf16[32,1024]{1,0:T(8,128)(2,1)S(1)}, bf16[32,1024]{1,0:T(8,128)(2,1)S(1)}, u32[]{:S(2)}, u32[]{:S(2)}) collective-permute-start(bf16[32,1024]{1,0:T(8,128)(2,1)S(1)} %get-tuple-element.32), channel_id=1, source_target_pairs={{0,24},{8,0},{16,8},{24,16},{32,56},{40,32},{48,40},{56,48},{64,88... | collective-permute-start | bytes 196616 | tf_op jit(solution)/shard_map/ppermute | solution.py:316
  164.3 5.0 %collective-permute-start.7 = (bf16[32,1024]{1,0:T(8,128)(2,1)S(1)}, bf16[32,1024]{1,0:T(8,128)(2,1)S(1)}, u32[]{:S(2)}, u32[]{:S(2)}) collective-permute-start(bf16[32,1024]{1,0:T(8,128)(2,1)S(1)} %fusion.4), channel_id=1, source_target_pairs={{0,64},{32,96},{64,0},{96,32},{8,72},{40,104},{72,8},{104,40},{16,... | collective-permute-start | bytes 196616 | tf_op jit(solution)/shard_map/ppermute | solution.py:319
  166.6 4.5 %collective-permute-start.8 = (bf16[32,1024]{1,0:T(8,128)(2,1)S(1)}, bf16[32,1024]{1,0:T(8,128)(2,1)S(1)}, u32[]{:S(2)}, u32[]{:S(2)}) collective-permute-start(bf16[32,1024]{1,0:T(8,128)(2,1)S(1)} %fusion.4), channel_id=1, source_target_pairs={{0,32},{32,64},{64,96},{96,0},{8,40},{40,72},{72,104},{104,8},{16,... | collective-permute-start | bytes 196616 | tf_op jit(solution)/shard_map/ppermute | solution.py:319
  166.6 4.5 %collective-permute-start.9 = (bf16[32,1024]{1,0:T(8,128)(2,1)S(1)}, bf16[32,1024]{1,0:T(8,128)(2,1)S(1)}, u32[]{:S(2)}, u32[]{:S(2)}) collective-permute-start(bf16[32,1024]{1,0:T(8,128)(2,1)S(1)} %fusion.4), channel_id=1, source_target_pairs={{0,96},{32,0},{64,32},{96,64},{8,104},{40,8},{72,40},{104,72},{16,... | collective-permute-start | bytes 196616 | tf_op jit(solution)/shard_map/ppermute | solution.py:319
  171.2 5.1 %collective-permute-start.10 = (bf16[32,1024]{1,0:T(8,128)(2,1)S(1)}, bf16[32,1024]{1,0:T(8,128)(2,1)S(1)}, u32[]{:S(2)}, u32[]{:S(2)}) collective-permute-start(bf16[32,1024]{1,0:T(8,128)(2,1)S(1)} %add_convert_fusion), channel_id=1, source_target_pairs={{0,8},{8,16},{16,24},{24,0},{32,40},{40,48},{48,56},{56,32},{64,72... | collective-permute-start | bytes 196616 | tf_op jit(solution)/shard_map/ppermute | solution.py:316
  171.3 5.0 %collective-permute-start.11 = (bf16[32,1024]{1,0:T(8,128)(2,1)S(1)}, bf16[32,1024]{1,0:T(8,128)(2,1)S(1)}, u32[]{:S(2)}, u32[]{:S(2)}) collective-permute-start(bf16[32,1024]{1,0:T(8,128)(2,1)S(1)} %add_convert_fusion), channel_id=1, source_target_pairs={{0,16},{8,24},{16,0},{24,8},{32,48},{40,56},{48,32},{56,40},{64,80... | collective-permute-start | bytes 196616 | tf_op jit(solution)/shard_map/ppermute | solution.py:316
  173.3 3.6 %collective-permute-start.12 = (bf16[32,1024]{1,0:T(8,128)(2,1)S(1)}, bf16[32,1024]{1,0:T(8,128)(2,1)S(1)}, u32[]{:S(2)}, u32[]{:S(2)}) collective-permute-start(bf16[32,1024]{1,0:T(8,128)(2,1)S(1)} %add_convert_fusion), channel_id=1, source_target_pairs={{0,24},{8,0},{16,8},{24,16},{32,56},{40,32},{48,40},{56,48},{64,88... | collective-permute-start | bytes 196616 | tf_op jit(solution)/shard_map/ppermute | solution.py:316
  177.0 5.9 %copy-start.7 = (bf16[512,1024]{1,0:T(8,128)(2,1)S(1)}, bf16[512,1024]{1,0:T(8,128)(2,1)}, u32[]{:S(2)}) copy-start(bf16[512,1024]{1,0:T(8,128)(2,1)} %get-tuple-element.14) | copy-start | bytes 3145732
  177.0 30.4 %all-to-all-start.3 = ((bf16[16,64,1024]{2,1,0:T(8,128)(2,1)}), bf16[16,64,1024]{2,1,0:T(8,128)(2,1)}, u32[]{:S(2)}, u32[]{:S(2)}) async-start(bf16[16,64,1024]{2,1,0:T(8,128)(2,1)} %get-tuple-element.20), calls=%async_computation.3 | async-start | bytes 4194304 | tf_op jit(solution)/shard_map/all_to_all | solution.py:375
  182.9 9.7 %copy-start.4 = (bf16[1024,1024]{1,0:T(8,128)(2,1)S(1)}, bf16[1024,1024]{1,0:T(8,128)(2,1)}, u32[]{:S(2)}) copy-start(bf16[1024,1024]{1,0:T(8,128)(2,1)} %param.18) | copy-start | bytes 6291460
  182.9 9.7 %copy-start.6 = (bf16[512,1024]{1,0:T(8,128)(2,1)S(1)}, bf16[512,1024]{1,0:T(8,128)(2,1)}, u32[]{:S(2)}) copy-start(bf16[512,1024]{1,0:T(8,128)(2,1)} %get-tuple-element.13) | copy-start | bytes 3145732
  186.9 10.4 %collective-permute-start.13 = (bf16[128,1024]{1,0:T(8,128)(2,1)S(1)}, bf16[128,1024]{1,0:T(8,128)(2,1)S(1)}, u32[]{:S(2)}, u32[]{:S(2)}) collective-permute-start(bf16[128,1024]{1,0:T(8,128)(2,1)S(1)} %get-tuple-element.35), channel_id=1, source_target_pairs={{0,2},{1,3},{2,4},{3,5},{4,6},{5,7},{6,0},{7,1},{8,10},{9,11},{10,... | collective-permute-start | bytes 786440 | tf_op jit(solution)/shard_map/ppermute | solution.py:313
  190.2 8.9 %collective-permute-start.14 = (bf16[128,1024]{1,0:T(8,128)(2,1)S(1)}, bf16[128,1024]{1,0:T(8,128)(2,1)S(1)}, u32[]{:S(2)}, u32[]{:S(2)}) collective-permute-start(bf16[128,1024]{1,0:T(8,128)(2,1)S(1)} %get-tuple-element.35), channel_id=1, source_target_pairs={{0,4},{1,5},{2,6},{3,7},{4,0},{5,1},{6,2},{7,3},{8,12},{9,13},{10,... | collective-permute-start | bytes 786440 | tf_op jit(solution)/shard_map/ppermute | solution.py:313
  191.9 7.2 %collective-permute-start.15 = (bf16[128,1024]{1,0:T(8,128)(2,1)S(1)}, bf16[128,1024]{1,0:T(8,128)(2,1)S(1)}, u32[]{:S(2)}, u32[]{:S(2)}) collective-permute-start(bf16[128,1024]{1,0:T(8,128)(2,1)S(1)} %get-tuple-element.35), channel_id=1, source_target_pairs={{0,6},{1,7},{2,0},{3,1},{4,2},{5,3},{6,4},{7,5},{8,14},{9,15},{10,... | collective-permute-start | bytes 786440 | tf_op jit(solution)/shard_map/ppermute | solution.py:313
  207.4 9.8 %collective-permute-start.16 = (bf16[512,1024]{1,0:T(8,128)(2,1)S(1)}, bf16[512,1024]{1,0:T(8,128)(2,1)S(1)}, u32[]{:S(2)}, u32[]{:S(2)}) collective-permute-start(bf16[512,1024]{1,0:T(8,128)(2,1)S(1)} %pad_maximum_fusion.1), channel_id=1, source_target_pairs={{0,1},{1,0},{2,3},{3,2},{4,5},{5,4},{6,7},{7,6},{8,9},{9,8},{10,11... | collective-permute-start | bytes 3145736 | tf_op jit(solution)/shard_map/ppermute | solution.py:322

commit v5 on v4

--- a/solution.py
+++ b/solution.py
@@ -26,7 +26,7 @@
     lists_ref, counts_ref, core_ref, q_hbm, ga_hbm, cot_hbm, x_hbm, wk_hbm, wv_hbm,
     att_hbm, gq_hbm, keep_hbm, give_hbm, ret0_hbm, ret1_hbm,
     att_ref, gq_ref, keep_ref, give_ref, q_ref, ga_ref, cot_ref, att_t_ref, x_ref, wk_ref, wv_ref, k_ref, v_ref, kt_ref, vt_ref, acc_ref,
-    mask_ref, used_ref, order_ref, in_sems, out_sems, result_sems,
+    mask_ref, used_ref, order_ref, in_sems, x_sems, out_sems, result_sems,
 ):
     bf16 = jnp.bfloat16
     slots, quads, rows, wide = k_ref.shape
@@ -37,11 +37,10 @@
     loads = [
         pltpu.make_async_copy(src, dst, in_sems.at[i])
         for i, (src, dst) in enumerate(
-            ((wk_hbm, wk_ref), (x_hbm, x_ref), (wv_hbm, wv_ref), (q_hbm, q_ref), (ga_hbm, ga_ref), (cot_hbm, cot_ref))
+            ((wk_hbm, wk_ref), (wv_hbm, wv_ref), (q_hbm, q_ref), (ga_hbm, ga_ref), (cot_hbm, cot_ref))
         )
     ]
-    for load in loads:
-        load.start()
+    loads[0].start()
 
     for s in range(slots):
         used_ref[s] = 0
@@ -59,14 +58,29 @@
         n = n + 1 - used_ref[s]
     batches = (n_used + BATCH - 1) // BATCH
 
+    def bring(i):
+        s = order_ref[i]
+        return pltpu.make_async_copy(x_hbm.at[s], x_ref.at[s], x_sems.at[i])
+
+    def ask(i, carry):
+        bring(i).start()
+        return carry
+
+    lax.fori_loop(0, batches * BATCH, ask, 0)
+    for load in loads[1:]:
+        load.start()
+
     def clear(s, carry):
         acc_ref[s] = jnp.zeros(acc_ref.shape[1:], acc_ref.dtype)
         return carry
 
     lax.fori_loop(0, slots, clear, 0)
 
-    def project(w_ref, out_ref, out_t_ref):
+    def project(w_ref, out_ref, out_t_ref, first):
         def batch(b, carry):
+            if first:
+                for i in range(BATCH):
+                    bring(b * BATCH + i).wait()
             ids = [order_ref[b * BATCH + i] for i in range(BATCH)]
             x = jnp.concatenate([x_ref[s] for s in ids], axis=0)
             for quad in range(quads):
@@ -79,12 +93,11 @@
 
         lax.fori_loop(0, batches, batch, 0)
 
-    for load in loads[:2]:
-        load.wait()
-    project(wk_ref, k_ref, kt_ref)
-    loads[2].wait()
-    project(wv_ref, v_ref, vt_ref)
-    for load in loads[3:]:
+    loads[0].wait()
+    project(wk_ref, k_ref, kt_ref, True)
+    loads[1].wait()
+    project(wv_ref, v_ref, vt_ref, False)
+    for load in loads[2:]:
         load.wait()
 
     head_of_row = lax.broadcasted_iota(jnp.int32, mask_ref.shape, 0) // per_group
@@ -251,7 +264,8 @@
             pltpu.VMEM((QUAD * (q.shape[0] // lists.shape[0]), wide), bf16),
             pltpu.SMEM((slots + 1,), jnp.int32),
             pltpu.SMEM((slots + 1,), jnp.int32),
-            pltpu.SemaphoreType.DMA((6,)),
+            pltpu.SemaphoreType.DMA((5,)),
+            pltpu.SemaphoreType.DMA((slots,)),
             pltpu.SemaphoreType.DMA((slots, PIECES)),
             pltpu.SemaphoreType.DMA((4,)),
         ],
@@ -302,6 +316,30 @@
     return lax.optimization_barrier((a,) + others)[0]
 
 
+def lay_kernel(half_ref, x_ref, *refs):
+    refs[-1][...] = x_ref[...].astype(refs[-1].dtype)
+
+
+def lay(half, x, earlier=()):
+    rows, width = x.shape
+    cut = 128
+    return pl.pallas_call(
+        lay_kernel,
+        grid_spec=pltpu.PrefetchScalarGridSpec(
+            num_scalar_prefetch=1,
+            grid=(rows // cut,),
+            in_specs=[pl.BlockSpec((cut, width), lambda i, half_ref: (i, 0))]
+            + [pl.BlockSpec(memory_space=pl.ANY)] * len(earlier),
+            out_specs=pl.BlockSpec((cut, width), lambda i, half_ref: (half_ref[0] * (rows // cut) + i, 0)),
+        ),
+        out_shape=jax.ShapeDtypeStruct((2 * rows, width), jnp.float32),
+        input_output_aliases={2: 0} if earlier else {},
+        compiler_params=pltpu.CompilerParams(vmem_limit_bytes=16 * MIB),
+        cost_estimate=pl.CostEstimate(flops=rows * width, bytes_accessed=6 * rows * width, transcendentals=0),
+        name="lay",
+    )(half, x, *earlier)
+
+
 def sum_over_devices(keep, give, first_piece, send_second, others):
     f32, bf16 = jnp.float32, jnp.bfloat16
     region, slab = (lax.axis_index(axis).astype(jnp.uint32) for axis in ("region", "slab"))
@@ -340,10 +378,10 @@
     part = gather(part, along_x, x)
     second_piece = send_second(part)
     part = gather(part, along_z, z)
-    part = after(part, second_piece, *others)
-    other = swap(part)
-    first, second = jnp.where(core == 0, part, other), jnp.where(core == 0, other, part)
-    return jnp.concatenate([first, second], axis=0).astype(f32), second_piece
+    mine = core.astype(jnp.int32).reshape(1)
+    laid = lay(mine, part)
+    other = swap(after(part, second_piece, laid, *others))
+    return lay(1 - mine, other, (laid,)), second_piece
 
 
 def per_device(

time: 222 us -> 218 us (0.982)
  waiting for transfers between devices: 87.2 us -> 82.6 us
  Pallas kernels: 42.5 us -> 45.1 us
  other arithmetic: 6.73 us -> 4.14 us
  starting transfers between devices: 50.8 us -> 53.1 us
    pallas_call x0 -> x2, Pallas kernels: none -> 3.69 us  [lay(): pl.pallas_call(lay_kernel, grid_spec=pltpu.PrefetchScalarGridSpec(num_sca...]
    all_to_all x1, starting transfers between devices: 9.12 us -> 5.53 us  [per_device(): lax.all_to_all(pieces[0], 'region', split_axis=0, concat_axis=0, tiled=True)]
    ppermute x6, starting transfers between devices: 11.2 us -> 14.7 us  [along_z(): lax.ppermute(a, 'slab', [(p * 2 + c, (p + by) % SIDE * 2 + c) for p in ra...]
    ppermute x2, starting transfers between devices: 7.61 us -> 10.1 us  [swap(): lax.ppermute(a, 'slab', [(p * 2 + c, p * 2 + 1 - c) for p in range(SIDE)...]
    convert_element_type x1 -> x0, other arithmetic: 2.45 us -> none  [sum_over_devices(): return (jnp.concatenate([first, second], axis=0).astype(f32), second_piece)]
  transfers between devices with their start and end apart: 20 -> 20, of which waited for: 10 -> 11; matrix products, arithmetic and copies ran while one was open for 8% -> 8% of each run, Pallas kernels for 2% -> 3%
where the time goes in v5:
time: 218 us; the launch traced here: 217 us
  waiting for transfers between devices  82.6 us (38%)
  starting transfers between devices  53.1 us (24%)
  Pallas kernels  45.1 us (21%)
  blocking collectives  13.8 us (6%)
  matrix products  12.1 us (6%)
  local copies, waits for them, and re-layouts  5.71 us (3%)
  other arithmetic  4.14 us (2%)
    all_to_all x1, waiting for transfers between devices, per_device(): lax.all_to_all(outgoing, 'region', split_axis=0, concat_axis=0, tiled=True)  53.2 us
    pallas_call x1, Pallas kernels, attention(): pl.pallas_call(attention_kernel, in_specs=[smem] * 3 + [hbm] * 6, out_spe...  36.4 us
    ppermute x6, starting transfers between devices, along_z(): lax.ppermute(a, 'slab', [(p * 2 + c, (p + by) % SIDE * 2 + c) for p in ra...  14.7 us
    all_to_all x1, blocking collectives, per_device(): lax.all_to_all(requests.reshape(-1), 'region', split_axis=0, concat_axis=...  13.8 us
    ppermute x6, waiting for transfers between devices, along_z(): lax.ppermute(a, 'slab', [(p * 2 + c, (p + by) % SIDE * 2 + c) for p in ra...  11.3 us
    ppermute x6, waiting for transfers between devices, along_x(): lax.ppermute(a, 'region', [(p * SIDE + i, p * SIDE + (i + by) % SIDE) for...  10.2 us
    ppermute x2, starting transfers between devices, swap(): lax.ppermute(a, 'slab', [(p * 2 + c, p * 2 + 1 - c) for p in range(SIDE)...  10.1 us
    dot_general x2, matrix products, nt(): lax.dot_general(a, b, (((1,), (1,)), ((), ())), preferred_element_type=jn...  7.65 us
  transfers between devices with their start and end apart: 20, of which 11 were waited for; matrix products, arithmetic and copies ran while one was open for 8% of the time, Pallas kernels for 3%

profile of v5, /device:TPU:1, one launch (start us, length us, event | category | flops | bytes accessed | tf_op | source)
XLA Modules:
  0.0 217.5 jit_solution(4337928545510921154)
XLA Ops:
  0.6 0.8 copy.17
  1.5 13.8 %all_to_all.29 = s32[16,1,1]{2,1,0:T(1,128)S(1)} all-to-all(s32[16,1,1]{2,1,0:T(1,128)S(1)} %copy.17), channel_id=1, replica_groups=mesh['region'=16,'slab'=8] {'region'}, dimensions={0} | all-to-all | bytes 128 | tf_op jit(solution)/shard_map/all_to_all | solution.py:395
  15.2 0.4 reduce.asked_ref
  15.7 2.8 %gather_fusion = bf16[16,128,1024]{2,1,0:T(8,128)(2,1)} fusion(bf16[4,128,1024]{2,1,0:T(8,128)(2,1)S(1)} %bitcast.62, s32[1024]{0:T(1024)S(1)} %pad_clamp_fusion), kind=kCustom, calls=%fused_computation | custom fusion | bytes 8388672 | tf_op jit(solution)/shard_map/gather | solution.py:396
  18.5 4.7 %all-to-all-start.1 = ((bf16[16,128,1024]{2,1,0:T(8,128)(2,1)}), bf16[16,128,1024]{2,1,0:T(8,128)(2,1)}, u32[]{:S(2)}, u32[]{:S(2)}) async-start(bf16[16,128,1024]{2,1,0:T(8,128)(2,1)} %gather_fusion), calls=%async_computation.1 | async-start | bytes 8388608 | tf_op jit(solution)/shard_map/all_to_all | solution.py:397
  23.2 3.6 %convolution_convert_fusion.2.ga_hbm = bf16[512,1024]{1,0:T(8,128)(2,1)} fusion(bf16[512,1024]{1,0:T(8,128)(2,1)} %cot_hbm.1, bf16[1024,1024]{1,0:T(8,128)(2,1)S(1)} %copy-done.3), kind=kOutput, calls=%fused_computation.4 | convolution fusion | flops 1074266112 | bytes 4194304 | tf_op jit(solution)/shard_map/dot_general | solution.py:18
  26.9 2.2 %fusion.q_hbm = bf16[512,1024]{1,0:T(8,128)(2,1)} fusion(bf16[512,1024]{1,0:T(8,128)(2,1)S(1)} %copy-done.5, bf16[1024,1024]{1,0:T(8,128)(2,1)S(1)} %copy-done.2), kind=kOutput, calls=%fused_computation.6 | convolution fusion | flops 1074790400 | bytes 4194304 | tf_op jit(solution)/shard_map/dot_general | solution.py:22
  29.1 53.2 %all-to-all-done.1.x_hbm = bf16[16,128,1024]{2,1,0:T(8,128)(2,1)} async-done(((bf16[16,128,1024]{2,1,0:T(8,128)(2,1)}), bf16[16,128,1024]{2,1,0:T(8,128)(2,1)}, u32[]{:S(2)}, u32[]{:S(2)}) %all-to-all-start.1) | async-done | bytes 4194336 | tf_op jit(solution)/shard_map/all_to_all | solution.py:397
  82.3 36.4 %attention.1 = (bf16[512,1024]{1,0:T(8,128)(2,1)}, bf16[512,1024]{1,0:T(8,128)(2,1)}, f32[512,1024]{1,0:T(8,128)}, bf16[512,1024]{1,0:T(8,128)(2,1)}, bf16[16,64...) custom-call(s32[4,4]{1,0:T(4,128)} %lists_ref.1, s32[4]{0:T(128)} %counts_ref.1, s32[1]{0:T(128)} %bitcast.core_ref, ...), custom_call_target="tpu_custom_call" | custom-call | flops 30064771072 | bytes 20971520 | tf_op jit(solution)/shard_map/attention/pallas_call | solution.py:246
  118.7 3.2 %collective-permute-start = (bf16[512,1024]{1,0:T(8,128)(2,1)}, bf16[512,1024]{1,0:T(8,128)(2,1)S(1)}, u32[]{:S(2)}, u32[]{:S(2)}) collective-permute-start(bf16[512,1024]{1,0:T(8,128)(2,1)} %get-tuple-element.17), channel_id=1, source_target_pairs={{0,1},{1,0},{2,3},{3,2},{4,5},{5,4},{6,7},{7,6},{8,9},{9,8},{10,11... | collective-permute-start | bytes 3145736 | tf_op jit(solution)/shard_map/ppermute | solution.py:360
  121.9 5.5 %all-to-all-start.2 = ((bf16[16,64,1024]{2,1,0:T(8,128)(2,1)}), bf16[16,64,1024]{2,1,0:T(8,128)(2,1)}, u32[]{:S(2)}, u32[]{:S(2)}) async-start(bf16[16,64,1024]{2,1,0:T(8,128)(2,1)} %get-tuple-element.18), calls=%async_computation.2 | async-start | bytes 4194304 | tf_op jit(solution)/shard_map/all_to_all | solution.py:406
  127.5 1.0 copy-done.1
  128.4 2.1 convert_add_fusion
  130.6 0.9 fusion.1
  131.5 3.5 %collective-permute-start.1 = (bf16[128,1024]{1,0:T(8,128)(2,1)}, bf16[128,1024]{1,0:T(8,128)(2,1)}, u32[]{:S(2)}, u32[]{:S(2)}) collective-permute-start(bf16[128,1024]{1,0:T(8,128)(2,1)} %get-tuple-element.22), channel_id=1, source_target_pairs={{0,2},{1,3},{2,4},{3,5},{4,6},{5,7},{6,0},{7,1},{8,10},{9,11},{10,... | collective-permute-start | bytes 786440 | tf_op jit(solution)/shard_map/ppermute | solution.py:351
  135.0 2.4 %collective-permute-start.2 = (bf16[128,1024]{1,0:T(8,128)(2,1)}, bf16[128,1024]{1,0:T(8,128)(2,1)}, u32[]{:S(2)}, u32[]{:S(2)}) collective-permute-start(bf16[128,1024]{1,0:T(8,128)(2,1)} %get-tuple-element.24), channel_id=1, source_target_pairs={{0,4},{1,5},{2,6},{3,7},{4,0},{5,1},{6,2},{7,3},{8,12},{9,13},{10,... | collective-permute-start | bytes 786440 | tf_op jit(solution)/shard_map/ppermute | solution.py:351
  137.4 1.7 collective-permute-start.3
  139.0 3.9 %collective-permute-done.1 = bf16[128,1024]{1,0:T(8,128)(2,1)} collective-permute-done((bf16[128,1024]{1,0:T(8,128)(2,1)}, bf16[128,1024]{1,0:T(8,128)(2,1)}, u32[]{:S(2)}, u32[]{:S(2)}) %collective-permute-start.1) | collective-permute-done | bytes 262176 | tf_op jit(solution)/shard_map/ppermute | solution.py:351
  142.9 6.5 %collective-permute-done.2 = bf16[128,1024]{1,0:T(8,128)(2,1)} collective-permute-done((bf16[128,1024]{1,0:T(8,128)(2,1)}, bf16[128,1024]{1,0:T(8,128)(2,1)}, u32[]{:S(2)}, u32[]{:S(2)}) %collective-permute-start.2) | collective-permute-done | bytes 262176 | tf_op jit(solution)/shard_map/ppermute | solution.py:351
  149.4 1.3 bitcast_add_fusion
  150.7 1.0 collective-permute-start.4
  151.8 2.4 %collective-permute-start.5 = (bf16[32,1024]{1,0:T(8,128)(2,1)S(1)}, bf16[32,1024]{1,0:T(8,128)(2,1)S(1)}, u32[]{:S(2)}, u32[]{:S(2)}) collective-permute-start(bf16[32,1024]{1,0:T(8,128)(2,1)S(1)} %get-tuple-element.31), channel_id=1, source_target_pairs={{0,16},{8,24},{16,0},{24,8},{32,48},{40,56},{48,32},{56,40},{64,80... | collective-permute-start | bytes 196616 | tf_op jit(solution)/shard_map/ppermute | solution.py:354
  154.2 1.2 collective-permute-start.6
  155.3 1.5 collective-permute-done.4
  156.8 5.6 %collective-permute-done.5 = bf16[32,1024]{1,0:T(8,128)(2,1)S(1)} collective-permute-done((bf16[32,1024]{1,0:T(8,128)(2,1)S(1)}, bf16[32,1024]{1,0:T(8,128)(2,1)S(1)}, u32[]{:S(2)}, u32[]{:S(2)}) %collective-permute-start.5) | collective-permute-done | bytes 65568 | tf_op jit(solution)/shard_map/ppermute | solution.py:354
  162.5 2.1 collective-permute-start.7
  164.6 2.7 %collective-permute-start.9 = (bf16[32,1024]{1,0:T(8,128)(2,1)S(1)}, bf16[32,1024]{1,0:T(8,128)(2,1)S(1)}, u32[]{:S(2)}, u32[]{:S(2)}) collective-permute-start(bf16[32,1024]{1,0:T(8,128)(2,1)S(1)} %fusion.4), channel_id=1, source_target_pairs={{0,96},{32,0},{64,32},{96,64},{8,104},{40,8},{72,40},{104,72},{16,... | collective-permute-start | bytes 196616 | tf_op jit(solution)/shard_map/ppermute | solution.py:357
  167.3 2.1 collective-permute-done.8
  169.4 0.1 collective-permute-start.10
  169.5 2.6 %collective-permute-start.11 = (bf16[32,1024]{1,0:T(8,128)(2,1)S(1)}, bf16[32,1024]{1,0:T(8,128)(2,1)S(1)}, u32[]{:S(2)}, u32[]{:S(2)}) collective-permute-start(bf16[32,1024]{1,0:T(8,128)(2,1)S(1)} %add_convert_fusion), channel_id=1, source_target_pairs={{0,16},{8,24},{16,0},{24,8},{32,48},{40,56},{48,32},{56,40},{64,80... | collective-permute-start | bytes 196616 | tf_op jit(solution)/shard_map/ppermute | solution.py:354
  172.2 1.7 collective-permute-done.10
  173.8 0.7 collective-permute-done.11
  174.5 0.7 collective-permute-done.12
  175.4 5.9 %all-to-all-start.3 = ((bf16[16,64,1024]{2,1,0:T(8,128)(2,1)}), bf16[16,64,1024]{2,1,0:T(8,128)(2,1)}, u32[]{:S(2)}, u32[]{:S(2)}) async-start(bf16[16,64,1024]{2,1,0:T(8,128)(2,1)} %get-tuple-element.20), calls=%async_computation.3 | async-start | bytes 4194304 | tf_op jit(solution)/shard_map/all_to_all | solution.py:413
  181.4 4.0 %convolution_convert_fusion = bf16[512,1024]{1,0:T(8,128)(2,1)} fusion(bf16[512,1024]{1,0:T(8,128)(2,1)S(1)} %copy-done.7, bf16[1024,1024]{1,0:T(8,128)(2,1)} %param.15), kind=kOutput, calls=%fused_computation.2 | convolution fusion | flops 1074266112 | bytes 4194304 | tf_op jit(solution)/shard_map/dot_general | solution.py:18
  185.4 3.9 %collective-permute-start.13 = (bf16[128,1024]{1,0:T(8,128)(2,1)S(1)}, bf16[128,1024]{1,0:T(8,128)(2,1)S(1)}, u32[]{:S(2)}, u32[]{:S(2)}) collective-permute-start(bf16[128,1024]{1,0:T(8,128)(2,1)S(1)} %get-tuple-element.33), channel_id=1, source_target_pairs={{0,2},{1,3},{2,4},{3,5},{4,6},{5,7},{6,0},{7,1},{8,10},{9,11},{10,... | collective-permute-start | bytes 786440 | tf_op jit(solution)/shard_map/ppermute | solution.py:351
  189.2 1.7 collective-permute-start.14
  191.0 1.6 collective-permute-start.15
  192.6 2.2 %convolution_convert_fusion.1 = bf16[512,1024]{1,0:T(8,128)(2,1)} fusion(bf16[512,1024]{1,0:T(8,128)(2,1)S(1)} %copy-done.6, bf16[1024,1024]{1,0:T(8,128)(2,1)S(1)} %copy-done.4), kind=kOutput, calls=%fused_computation.3 | convolution fusion | flops 1074266112 | bytes 4194304 | tf_op jit(solution)/shard_map/dot_general | solution.py:22
  194.8 2.5 %settle.2.refs_0_ = bf16[4,128,1024]{2,1,0:T(8,128)(2,1)} custom-call(s32[16]{0:T(128)S(1)} %reduce.asked_ref, bf16[16,64,1024]{2,1,0:T(8,128)(2,1)} %all-to-all-done.2.x_ref), custom_call_target="tpu_custom_call" | custom-call | flops 1048576 | bytes 3145728 | tf_op jit(solution)/shard_map/settle/pallas_call | solution.py:293
  197.3 0.9 collective-permute-done.14
  198.2 0.1 pad_maximum_fusion
  198.3 0.1 dynamic-slice_bitcast_fusion.3
  198.5 1.9 lay.2.refs_0_
  200.3 5.8 %all-to-all-done.3.x_ref = bf16[16,64,1024]{2,1,0:T(8,128)(2,1)} async-done(((bf16[16,64,1024]{2,1,0:T(8,128)(2,1)}), bf16[16,64,1024]{2,1,0:T(8,128)(2,1)}, u32[]{:S(2)}, u32[]{:S(2)}) %all-to-all-start.3) | async-done | bytes 2097184 | tf_op jit(solution)/shard_map/all_to_all | solution.py:413
  206.2 7.0 %collective-permute-start.16 = (bf16[512,1024]{1,0:T(8,128)(2,1)S(1)}, bf16[512,1024]{1,0:T(8,128)(2,1)S(1)}, u32[]{:S(2)}, u32[]{:S(2)}) collective-permute-start(bf16[512,1024]{1,0:T(8,128)(2,1)S(1)} %pad_maximum_fusion.1.x_ref), channel_id=1, source_target_pairs={{0,1},{1,0},{2,3},{3,2},{4,5},{5,4},{6,7},{7,6},{8,9},{9,8},{10,11... | collective-permute-start | bytes 3145736 | tf_op jit(solution)/shard_map/ppermute | solution.py:360
  213.1 2.5 %settle.3 = bf16[4,128,1024]{2,1,0:T(8,128)(2,1)} custom-call(s32[16]{0:T(128)S(1)} %reduce.asked_ref, bf16[16,64,1024]{2,1,0:T(8,128)(2,1)} %all-to-all-done.3.x_ref, bf16[4,128,1024]{2,1,0:T(8,128)(2,1)} %settle.2.refs_0_), custom_call_target="tpu_custom_call", output_to_operand_aliasing={{}: (2, {})} | custom-call | flops 1048576 | bytes 3145728 | tf_op jit(solution)/shard_map/settle/pallas_call | solution.py:293
  215.7 1.8 lay.3
  (35 shorter events, 0.4 us)
Async XLA Ops:
  0.6 15.0 %copy-start = (bf16[512,1024]{1,0:T(8,128)(2,1)S(1)}, bf16[512,1024]{1,0:T(8,128)(2,1)}, u32[]{:S(2)}) copy-start(bf16[512,1024]{1,0:T(8,128)(2,1)} %param.11) | copy-start | bytes 3145732
  18.5 4.7 %copy-start.3 = (bf16[1024,1024]{1,0:T(8,128)(2,1)S(1)}, bf16[1024,1024]{1,0:T(8,128)(2,1)}, u32[]{:S(2)}) copy-start(bf16[1024,1024]{1,0:T(8,128)(2,1)} %param.18) | copy-start | bytes 6291460
  18.5 63.8 %all-to-all-start.1 = ((bf16[16,128,1024]{2,1,0:T(8,128)(2,1)}), bf16[16,128,1024]{2,1,0:T(8,128)(2,1)}, u32[]{:S(2)}, u32[]{:S(2)}) async-start(bf16[16,128,1024]{2,1,0:T(8,128)(2,1)} %gather_fusion), calls=%async_computation.1 | async-start | bytes 8388608 | tf_op jit(solution)/shard_map/all_to_all | solution.py:397
  23.2 3.7 %copy-start.2 = (bf16[1024,1024]{1,0:T(8,128)(2,1)S(1)}, bf16[1024,1024]{1,0:T(8,128)(2,1)}, u32[]{:S(2)}) copy-start(bf16[1024,1024]{1,0:T(8,128)(2,1)} %param.15) | copy-start | bytes 6291460
  23.2 3.7 %copy-start.5 = (bf16[512,1024]{1,0:T(8,128)(2,1)S(1)}, bf16[512,1024]{1,0:T(8,128)(2,1)}, u32[]{:S(2)}) copy-start(bf16[512,1024]{1,0:T(8,128)(2,1)} %param.10) | copy-start | bytes 3145732
  118.7 8.7 %collective-permute-start = (bf16[512,1024]{1,0:T(8,128)(2,1)}, bf16[512,1024]{1,0:T(8,128)(2,1)S(1)}, u32[]{:S(2)}, u32[]{:S(2)}) collective-permute-start(bf16[512,1024]{1,0:T(8,128)(2,1)} %get-tuple-element.17), channel_id=1, source_target_pairs={{0,1},{1,0},{2,3},{3,2},{4,5},{5,4},{6,7},{7,6},{8,9},{9,8},{10,11... | collective-permute-start | bytes 3145736 | tf_op jit(solution)/shard_map/ppermute | solution.py:360
  121.9 40.6 %all-to-all-start.2 = ((bf16[16,64,1024]{2,1,0:T(8,128)(2,1)}), bf16[16,64,1024]{2,1,0:T(8,128)(2,1)}, u32[]{:S(2)}, u32[]{:S(2)}) async-start(bf16[16,64,1024]{2,1,0:T(8,128)(2,1)} %get-tuple-element.18), calls=%async_computation.2 | async-start | bytes 4194304 | tf_op jit(solution)/shard_map/all_to_all | solution.py:406
  127.5 1.0 copy-start.1
  131.5 11.5 %collective-permute-start.1 = (bf16[128,1024]{1,0:T(8,128)(2,1)}, bf16[128,1024]{1,0:T(8,128)(2,1)}, u32[]{:S(2)}, u32[]{:S(2)}) collective-permute-start(bf16[128,1024]{1,0:T(8,128)(2,1)} %get-tuple-element.22), channel_id=1, source_target_pairs={{0,2},{1,3},{2,4},{3,5},{4,6},{5,7},{6,0},{7,1},{8,10},{9,11},{10,... | collective-permute-start | bytes 786440 | tf_op jit(solution)/shard_map/ppermute | solution.py:351
  135.0 14.5 %collective-permute-start.2 = (bf16[128,1024]{1,0:T(8,128)(2,1)}, bf16[128,1024]{1,0:T(8,128)(2,1)}, u32[]{:S(2)}, u32[]{:S(2)}) collective-permute-start(bf16[128,1024]{1,0:T(8,128)(2,1)} %get-tuple-element.24), channel_id=1, source_target_pairs={{0,4},{1,5},{2,6},{3,7},{4,0},{5,1},{6,2},{7,3},{8,12},{9,13},{10,... | collective-permute-start | bytes 786440 | tf_op jit(solution)/shard_map/ppermute | solution.py:351
  137.4 12.1 %collective-permute-start.3 = (bf16[128,1024]{1,0:T(8,128)(2,1)S(1)}, bf16[128,1024]{1,0:T(8,128)(2,1)}, u32[]{:S(2)}, u32[]{:S(2)}) collective-permute-start(bf16[128,1024]{1,0:T(8,128)(2,1)S(1)} %get-tuple-element.23), channel_id=1, source_target_pairs={{0,6},{1,7},{2,0},{3,1},{4,2},{5,3},{6,4},{7,5},{8,14},{9,15},{10,... | collective-permute-start | bytes 786440 | tf_op jit(solution)/shard_map/ppermute | solution.py:351
  150.7 6.1 %collective-permute-start.4 = (bf16[32,1024]{1,0:T(8,128)(2,1)S(1)}, bf16[32,1024]{1,0:T(8,128)(2,1)S(1)}, u32[]{:S(2)}, u32[]{:S(2)}) collective-permute-start(bf16[32,1024]{1,0:T(8,128)(2,1)S(1)} %get-tuple-element.29), channel_id=1, source_target_pairs={{0,8},{8,16},{16,24},{24,0},{32,40},{40,48},{48,56},{56,32},{64,72... | collective-permute-start | bytes 196616 | tf_op jit(solution)/shard_map/ppermute | solution.py:354
  151.8 10.7 %collective-permute-start.5 = (bf16[32,1024]{1,0:T(8,128)(2,1)S(1)}, bf16[32,1024]{1,0:T(8,128)(2,1)S(1)}, u32[]{:S(2)}, u32[]{:S(2)}) collective-permute-start(bf16[32,1024]{1,0:T(8,128)(2,1)S(1)} %get-tuple-element.31), channel_id=1, source_target_pairs={{0,16},{8,24},{16,0},{24,8},{32,48},{40,56},{48,32},{56,40},{64,80... | collective-permute-start | bytes 196616 | tf_op jit(solution)/shard_map/ppermute | solution.py:354
  154.2 8.3 %collective-permute-start.6 = (bf16[32,1024]{1,0:T(8,128)(2,1)S(1)}, bf16[32,1024]{1,0:T(8,128)(2,1)S(1)}, u32[]{:S(2)}, u32[]{:S(2)}) collective-permute-start(bf16[32,1024]{1,0:T(8,128)(2,1)S(1)} %get-tuple-element.30), channel_id=1, source_target_pairs={{0,24},{8,0},{16,8},{24,16},{32,56},{40,32},{48,40},{56,48},{64,88... | collective-permute-start | bytes 196616 | tf_op jit(solution)/shard_map/ppermute | solution.py:354
  162.5 4.8 %collective-permute-start.7 = (bf16[32,1024]{1,0:T(8,128)(2,1)S(1)}, bf16[32,1024]{1,0:T(8,128)(2,1)S(1)}, u32[]{:S(2)}, u32[]{:S(2)}) collective-permute-start(bf16[32,1024]{1,0:T(8,128)(2,1)S(1)} %fusion.4), channel_id=1, source_target_pairs={{0,64},{32,96},{64,0},{96,32},{8,72},{40,104},{72,8},{104,40},{16,... | collective-permute-start | bytes 196616 | tf_op jit(solution)/shard_map/ppermute | solution.py:357
  164.6 4.8 %collective-permute-start.8 = (bf16[32,1024]{1,0:T(8,128)(2,1)S(1)}, bf16[32,1024]{1,0:T(8,128)(2,1)S(1)}, u32[]{:S(2)}, u32[]{:S(2)}) collective-permute-start(bf16[32,1024]{1,0:T(8,128)(2,1)S(1)} %fusion.4), channel_id=1, source_target_pairs={{0,32},{32,64},{64,96},{96,0},{8,40},{40,72},{72,104},{104,8},{16,... | collective-permute-start | bytes 196616 | tf_op jit(solution)/shard_map/ppermute | solution.py:357
  164.6 4.8 %collective-permute-start.9 = (bf16[32,1024]{1,0:T(8,128)(2,1)S(1)}, bf16[32,1024]{1,0:T(8,128)(2,1)S(1)}, u32[]{:S(2)}, u32[]{:S(2)}) collective-permute-start(bf16[32,1024]{1,0:T(8,128)(2,1)S(1)} %fusion.4), channel_id=1, source_target_pairs={{0,96},{32,0},{64,32},{96,64},{8,104},{40,8},{72,40},{104,72},{16,... | collective-permute-start | bytes 196616 | tf_op jit(solution)/shard_map/ppermute | solution.py:357
  169.4 4.4 %collective-permute-start.10 = (bf16[32,1024]{1,0:T(8,128)(2,1)S(1)}, bf16[32,1024]{1,0:T(8,128)(2,1)S(1)}, u32[]{:S(2)}, u32[]{:S(2)}) collective-permute-start(bf16[32,1024]{1,0:T(8,128)(2,1)S(1)} %add_convert_fusion), channel_id=1, source_target_pairs={{0,8},{8,16},{16,24},{24,0},{32,40},{40,48},{48,56},{56,32},{64,72... | collective-permute-start | bytes 196616 | tf_op jit(solution)/shard_map/ppermute | solution.py:354
  169.5 5.0 %collective-permute-start.11 = (bf16[32,1024]{1,0:T(8,128)(2,1)S(1)}, bf16[32,1024]{1,0:T(8,128)(2,1)S(1)}, u32[]{:S(2)}, u32[]{:S(2)}) collective-permute-start(bf16[32,1024]{1,0:T(8,128)(2,1)S(1)} %add_convert_fusion), channel_id=1, source_target_pairs={{0,16},{8,24},{16,0},{24,8},{32,48},{40,56},{48,32},{56,40},{64,80... | collective-permute-start | bytes 196616 | tf_op jit(solution)/shard_map/ppermute | solution.py:354
  172.1 3.1 %collective-permute-start.12 = (bf16[32,1024]{1,0:T(8,128)(2,1)S(1)}, bf16[32,1024]{1,0:T(8,128)(2,1)S(1)}, u32[]{:S(2)}, u32[]{:S(2)}) collective-permute-start(bf16[32,1024]{1,0:T(8,128)(2,1)S(1)} %add_convert_fusion), channel_id=1, source_target_pairs={{0,24},{8,0},{16,8},{24,16},{32,56},{40,32},{48,40},{56,48},{64,88... | collective-permute-start | bytes 196616 | tf_op jit(solution)/shard_map/ppermute | solution.py:354
  175.4 6.0 %copy-start.7 = (bf16[512,1024]{1,0:T(8,128)(2,1)S(1)}, bf16[512,1024]{1,0:T(8,128)(2,1)}, u32[]{:S(2)}) copy-start(bf16[512,1024]{1,0:T(8,128)(2,1)} %get-tuple-element.14) | copy-start | bytes 3145732
  175.4 30.8 %all-to-all-start.3 = ((bf16[16,64,1024]{2,1,0:T(8,128)(2,1)}), bf16[16,64,1024]{2,1,0:T(8,128)(2,1)}, u32[]{:S(2)}, u32[]{:S(2)}) async-start(bf16[16,64,1024]{2,1,0:T(8,128)(2,1)} %get-tuple-element.20), calls=%async_computation.3 | async-start | bytes 4194304 | tf_op jit(solution)/shard_map/all_to_all | solution.py:413
  181.4 11.2 %copy-start.4 = (bf16[1024,1024]{1,0:T(8,128)(2,1)S(1)}, bf16[1024,1024]{1,0:T(8,128)(2,1)}, u32[]{:S(2)}) copy-start(bf16[1024,1024]{1,0:T(8,128)(2,1)} %param.18) | copy-start | bytes 6291460
  181.4 11.2 %copy-start.6 = (bf16[512,1024]{1,0:T(8,128)(2,1)S(1)}, bf16[512,1024]{1,0:T(8,128)(2,1)}, u32[]{:S(2)}) copy-start(bf16[512,1024]{1,0:T(8,128)(2,1)} %get-tuple-element.13) | copy-start | bytes 3145732
  185.4 11.9 %collective-permute-start.13 = (bf16[128,1024]{1,0:T(8,128)(2,1)S(1)}, bf16[128,1024]{1,0:T(8,128)(2,1)S(1)}, u32[]{:S(2)}, u32[]{:S(2)}) collective-permute-start(bf16[128,1024]{1,0:T(8,128)(2,1)S(1)} %get-tuple-element.33), channel_id=1, source_target_pairs={{0,2},{1,3},{2,4},{3,5},{4,6},{5,7},{6,0},{7,1},{8,10},{9,11},{10,... | collective-permute-start | bytes 786440 | tf_op jit(solution)/shard_map/ppermute | solution.py:351
  189.2 8.9 %collective-permute-start.14 = (bf16[128,1024]{1,0:T(8,128)(2,1)S(1)}, bf16[128,1024]{1,0:T(8,128)(2,1)S(1)}, u32[]{:S(2)}, u32[]{:S(2)}) collective-permute-start(bf16[128,1024]{1,0:T(8,128)(2,1)S(1)} %get-tuple-element.33), channel_id=1, source_target_pairs={{0,4},{1,5},{2,6},{3,7},{4,0},{5,1},{6,2},{7,3},{8,12},{9,13},{10,... | collective-permute-start | bytes 786440 | tf_op jit(solution)/shard_map/ppermute | solution.py:351
  191.0 7.2 %collective-permute-start.15 = (bf16[128,1024]{1,0:T(8,128)(2,1)S(1)}, bf16[128,1024]{1,0:T(8,128)(2,1)S(1)}, u32[]{:S(2)}, u32[]{:S(2)}) collective-permute-start(bf16[128,1024]{1,0:T(8,128)(2,1)S(1)} %get-tuple-element.33), channel_id=1, source_target_pairs={{0,6},{1,7},{2,0},{3,1},{4,2},{5,3},{6,4},{7,5},{8,14},{9,15},{10,... | collective-permute-start | bytes 786440 | tf_op jit(solution)/shard_map/ppermute | solution.py:351
  206.2 9.5 %collective-permute-start.16 = (bf16[512,1024]{1,0:T(8,128)(2,1)S(1)}, bf16[512,1024]{1,0:T(8,128)(2,1)S(1)}, u32[]{:S(2)}, u32[]{:S(2)}) collective-permute-start(bf16[512,1024]{1,0:T(8,128)(2,1)S(1)} %pad_maximum_fusion.1.x_ref), channel_id=1, source_target_pairs={{0,1},{1,0},{2,3},{3,2},{4,5},{5,4},{6,7},{7,6},{8,9},{9,8},{10,11... | collective-permute-start | bytes 3145736 | tf_op jit(solution)/shard_map/ppermute | solution.py:360

commit v6 on v5

--- a/solution.py
+++ b/solution.py
@@ -9,6 +9,7 @@
 BLOCK = 128
 QUAD = 4
 BATCH = 2
+RETURN_BATCH = 4
 SIDE = 4
 PIECES = 2
 MIB = 2**20
@@ -24,8 +25,8 @@
 
 def attention_kernel(
     lists_ref, counts_ref, core_ref, q_hbm, ga_hbm, cot_hbm, x_hbm, wk_hbm, wv_hbm,
-    att_hbm, gq_hbm, keep_hbm, give_hbm, ret0_hbm, ret1_hbm,
-    att_ref, gq_ref, keep_ref, give_ref, q_ref, ga_ref, cot_ref, att_t_ref, x_ref, wk_ref, wv_ref, k_ref, v_ref, kt_ref, vt_ref, acc_ref,
+    att_hbm, gq_hbm, keep_hbm, give_hbm, ret_hbm, late_hbm,
+    att_ref, gq_ref, keep_ref, give_ref, late_ref, q_ref, ga_ref, cot_ref, att_t_ref, x_ref, wk_ref, wv_ref, k_ref, v_ref, kt_ref, vt_ref, acc_ref,
     mask_ref, used_ref, order_ref, in_sems, x_sems, out_sems, result_sems,
 ):
     bf16 = jnp.bfloat16
@@ -183,19 +184,20 @@
     for result in results[2:]:
         result.start()
 
+    cut = rows // PIECES
+
     def send(i, s):
-        cut = rows // PIECES
         return [
-            pltpu.make_async_copy(x_ref.at[s, pl.ds(n * cut, cut)], ret.at[s], out_sems.at[i, n])
-            for n, ret in enumerate((ret0_hbm, ret1_hbm))
+            pltpu.make_async_copy(x_ref.at[s, pl.ds(0, cut)], ret_hbm.at[s], out_sems.at[i, 0]),
+            pltpu.make_async_copy(late_ref.at[s], late_hbm.at[s], out_sems.at[i, 1]),
         ]
 
     def turn_back(b, carry):
-        ids = [order_ref[b * BATCH + i] for i in range(BATCH)]
+        ids = [order_ref[b * RETURN_BATCH + i] for i in range(RETURN_BATCH)]
         grads = [
             jnp.concatenate(
                 [
-                    jnp.concatenate([acc_ref[s, at + c].astype(bf16) for c in range(quads)], axis=1)
+                    jnp.concatenate([acc_ref[s, at + c, :cut].astype(bf16) for c in range(quads)], axis=1)
                     for s in ids
                 ],
                 axis=0,
@@ -206,22 +208,26 @@
             out_rows = slice(c * wide, (c + 1) * wide)
             y = (nt(grads[0], wk_ref[out_rows]) + nt(grads[1], wv_ref[out_rows])).astype(bf16)
             for i, s in enumerate(ids):
-                x_ref[s, :, out_rows] = y[i * rows:(i + 1) * rows]
+                x_ref[s, :cut, out_rows] = y[i * cut:(i + 1) * cut]
         for i, s in enumerate(ids):
-            for copy in send(b * BATCH + i, s):
+            for c in range(2 * quads):
+                late_ref[s, :, c * wide:(c + 1) * wide] = acc_ref[s, c, cut:].astype(bf16)
+            for copy in send(b * RETURN_BATCH + i, s):
                 copy.start()
         return carry
 
+    batches = (n_used + RETURN_BATCH - 1) // RETURN_BATCH
     lax.fori_loop(0, batches, turn_back, 0)
 
     def nothing(i, carry):
         s = order_ref[i]
-        x_ref[s] = jnp.zeros(x_ref.shape[1:], x_ref.dtype)
+        x_ref[s, :cut] = jnp.zeros((cut,) + x_ref.shape[2:], x_ref.dtype)
+        late_ref[s] = jnp.zeros(late_ref.shape[1:], late_ref.dtype)
         for copy in send(i, s):
             copy.start()
         return carry
 
-    lax.fori_loop(batches * BATCH, slots, nothing, 0)
+    lax.fori_loop(batches * RETURN_BATCH, slots, nothing, 0)
 
     def arrive(i, carry):
         for copy in send(i, order_ref[i]):
@@ -246,16 +252,19 @@
     return pl.pallas_call(
         attention_kernel,
         in_specs=[smem] * 3 + [hbm] * 6,
-        out_specs=[hbm] * (4 + PIECES),
+        out_specs=[hbm] * 6,
         out_shape=[
             jax.ShapeDtypeStruct(q.shape, bf16),
             jax.ShapeDtypeStruct(q.shape, bf16),
             jax.ShapeDtypeStruct((width // 2, width), jnp.float32),
             jax.ShapeDtypeStruct((width // 2, width), bf16),
-        ] + [jax.ShapeDtypeStruct((slots, rows // PIECES, width), bf16)] * PIECES,
+            jax.ShapeDtypeStruct((slots, rows // PIECES, width), bf16),
+            jax.ShapeDtypeStruct((slots, rows // PIECES, 2 * width), bf16),
+        ],
         scratch_shapes=[
             pltpu.VMEM(q.shape, bf16), pltpu.VMEM(q.shape, bf16),
             pltpu.VMEM((width // 2, width), jnp.float32), pltpu.VMEM((width // 2, width), bf16),
+            pltpu.VMEM((slots, rows // PIECES, 2 * width), bf16),
             pltpu.VMEM(q.shape, bf16), pltpu.VMEM(q.shape, bf16), pltpu.VMEM(q.shape, bf16),
             pltpu.VMEM(q.shape[::-1], bf16), pltpu.VMEM(x.shape, bf16),
             pltpu.VMEM(wk.shape, bf16), pltpu.VMEM(wv.shape, bf16),
@@ -340,7 +349,7 @@
     )(half, x, *earlier)
 
 
-def sum_over_devices(keep, give, first_piece, send_second, others):
+def sum_over_devices(keep, give, first_piece, second, send_second, others):
     f32, bf16 = jnp.float32, jnp.bfloat16
     region, slab = (lax.axis_index(axis).astype(jnp.uint32) for axis in ("region", "slab"))
     x = region & (SIDE - 1)
@@ -372,7 +381,7 @@
 
     part = keep + swap(give).astype(f32)
     part = scatter(part, along_z, z)
-    part = after(scatter(part, along_x, x).astype(bf16), first_piece)
+    part = after(scatter(after(part, second), along_x, x).astype(bf16), first_piece)
     ring = [part.astype(f32)] + [along_y(part, by).astype(f32) for by in range(1, SIDE)]
     part = ((ring[0] + ring[2]) + (ring[1] + ring[3])).astype(bf16)
     part = gather(part, along_x, x)
@@ -400,20 +409,22 @@
     grad_att = nt(cotangent, w_out).astype(bf16)
 
     core = (lax.axis_index("slab") & 1).reshape(1)
-    attended, grad_query, keep, give, *pieces = attention(
+    w_both = jnp.concatenate([key_weight, value_weight], axis=1)
+    attended, grad_query, keep, give, first, late = attention(
         lists, counts, core, query, grad_att, cotangent, blocks, key_weight, value_weight
     )
-    returned = lax.all_to_all(pieces[0], "region", split_axis=0, concat_axis=0, tiled=True)
-
+    returned = lax.all_to_all(first, "region", split_axis=0, concat_axis=0, tiled=True)
+
+    second = nt(late.reshape(-1, late.shape[2]), w_both).astype(bf16).reshape(first.shape)
     mixed = nn(attended, w_out).astype(bf16)
     grad_volume = nt(grad_query, w_query).astype(bf16)
     patches_piece = settle(asked, returned, owned, 0)
 
     def send_second(summed):
-        return lax.all_to_all(after(pieces[1], summed), "region", split_axis=0, concat_axis=0, tiled=True)
+        return lax.all_to_all(after(second, summed), "region", split_axis=0, concat_axis=0, tiled=True)
 
     grad_out_weight, later = sum_over_devices(
-        keep, give, returned, send_second, (mixed, grad_volume, patches_piece)
+        keep, give, returned, second, send_second, (mixed, grad_volume, patches_piece)
     )
     grad_patches = settle(asked, later, owned, 1, (patches_piece,))
     return mixed, grad_volume, grad_patches.reshape(owned * BLOCK, width), grad_out_weight

time: 218 us -> 217 us (level)
  matrix products: 12.1 us -> 20.1 us
  waiting for transfers between devices: 82.6 us -> 75.9 us
    ppermute x6, waiting for transfers between devices: 11.3 us -> 2.79 us  [along_z(): lax.ppermute(a, 'slab', [(p * 2 + c, (p + by) % SIDE * 2 + c) for p in ra...]
    dot_general x2 -> x3, matrix products: 7.65 us -> 15.7 us  [nt(): lax.dot_general(a, b, (((1,), (1,)), ((), ())), preferred_element_type=jn...]
    ppermute x6, waiting for transfers between devices: 10.2 us -> 13.1 us  [along_x(): lax.ppermute(a, 'region', [(p * SIDE + i, p * SIDE + (i + by) % SIDE) for...]
    ppermute x2, starting transfers between devices: 10.1 us -> 7.42 us  [swap(): lax.ppermute(a, 'slab', [(p * 2 + c, p * 2 + 1 - c) for p in range(SIDE)...]
  transfers between devices with their start and end apart: 20 -> 20, of which waited for: 11 -> 9; matrix products, arithmetic and copies ran while one was open for 8% -> 10% of each run, Pallas kernels for 3% -> 3%
where the time goes in v6:
time: 217 us; the launch traced here: 215 us
  waiting for transfers between devices  75.9 us (35%)
  starting transfers between devices  52 us (24%)
  Pallas kernels  45.8 us (21%)
  matrix products  20.1 us (9%)
  blocking collectives  13.8 us (6%)
  local copies, waits for them, and re-layouts  3.96 us (2%)
  other arithmetic  2.6 us (1%)
    all_to_all x1, waiting for transfers between devices, per_device(): lax.all_to_all(outgoing, 'region', split_axis=0, concat_axis=0, tiled=True)  53.2 us
    pallas_call x1, Pallas kernels, attention(): pl.pallas_call(attention_kernel, in_specs=[smem] * 3 + [hbm] * 6, out_spe...  37.1 us
    ppermute x6, starting transfers between devices, along_z(): lax.ppermute(a, 'slab', [(p * 2 + c, (p + by) % SIDE * 2 + c) for p in ra...  16.4 us
    dot_general x3, matrix products, nt(): lax.dot_general(a, b, (((1,), (1,)), ((), ())), preferred_element_type=jn...  15.7 us
    all_to_all x1, blocking collectives, per_device(): lax.all_to_all(requests.reshape(-1), 'region', split_axis=0, concat_axis=...  13.8 us
    ppermute x6, waiting for transfers between devices, along_x(): lax.ppermute(a, 'region', [(p * SIDE + i, p * SIDE + (i + by) % SIDE) for...  13.1 us
    ppermute x2, starting transfers between devices, swap(): lax.ppermute(a, 'slab', [(p * 2 + c, p * 2 + 1 - c) for p in range(SIDE)...  7.42 us
    ppermute x6, starting transfers between devices, along_x(): lax.ppermute(a, 'region', [(p * SIDE + i, p * SIDE + (i + by) % SIDE) for...  7.37 us
  transfers between devices with their start and end apart: 20, of which 9 were waited for; matrix products, arithmetic and copies ran while one was open for 10% of the time, Pallas kernels for 3%

profile of v6, /device:TPU:1, one launch (start us, length us, event | category | flops | bytes accessed | tf_op | source)
XLA Modules:
  0.0 215.0 jit_solution(15879227419970790308)
XLA Ops:
  0.6 0.8 copy.17
  1.5 13.8 %all_to_all.29 = s32[16,1,1]{2,1,0:T(1,128)S(1)} all-to-all(s32[16,1,1]{2,1,0:T(1,128)S(1)} %copy.17), channel_id=1, replica_groups=mesh['region'=16,'slab'=8] {'region'}, dimensions={0} | all-to-all | bytes 128 | tf_op jit(solution)/shard_map/all_to_all | solution.py:404
  15.2 0.4 reduce.asked_ref
  15.7 2.8 %gather_fusion = bf16[16,128,1024]{2,1,0:T(8,128)(2,1)} fusion(bf16[4,128,1024]{2,1,0:T(8,128)(2,1)S(1)} %bitcast.65, s32[1024]{0:T(1024)S(1)} %pad_clamp_fusion), kind=kCustom, calls=%fused_computation | custom fusion | bytes 8388672 | tf_op jit(solution)/shard_map/gather | solution.py:405
  18.5 4.7 %all-to-all-start.1 = ((bf16[16,128,1024]{2,1,0:T(8,128)(2,1)}), bf16[16,128,1024]{2,1,0:T(8,128)(2,1)}, u32[]{:S(2)}, u32[]{:S(2)}) async-start(bf16[16,128,1024]{2,1,0:T(8,128)(2,1)} %gather_fusion), calls=%async_computation.1 | async-start | bytes 8388608 | tf_op jit(solution)/shard_map/all_to_all | solution.py:406
  23.2 3.6 %convolution_convert_fusion.2.ga_hbm = bf16[512,1024]{1,0:T(8,128)(2,1)} fusion(bf16[512,1024]{1,0:T(8,128)(2,1)} %cot_hbm.1, bf16[1024,1024]{1,0:T(8,128)(2,1)S(1)} %copy-done.5), kind=kOutput, calls=%fused_computation.9 | convolution fusion | flops 1074266112 | bytes 4194304 | tf_op jit(solution)/shard_map/dot_general | solution.py:19
  26.9 2.2 %fusion.7.q_hbm = bf16[512,1024]{1,0:T(8,128)(2,1)} fusion(bf16[512,1024]{1,0:T(8,128)(2,1)S(1)} %copy-done.7, bf16[1024,1024]{1,0:T(8,128)(2,1)S(1)} %copy-done.4), kind=kOutput, calls=%fused_computation.11 | convolution fusion | flops 1074790400 | bytes 4194304 | tf_op jit(solution)/shard_map/dot_general | solution.py:23
  29.1 53.2 %all-to-all-done.1.x_hbm = bf16[16,128,1024]{2,1,0:T(8,128)(2,1)} async-done(((bf16[16,128,1024]{2,1,0:T(8,128)(2,1)}), bf16[16,128,1024]{2,1,0:T(8,128)(2,1)}, u32[]{:S(2)}, u32[]{:S(2)}) %all-to-all-start.1) | async-done | bytes 4194336 | tf_op jit(solution)/shard_map/all_to_all | solution.py:406
  82.3 37.1 %attention.1 = (bf16[512,1024]{1,0:T(8,128)(2,1)}, bf16[512,1024]{1,0:T(8,128)(2,1)}, f32[512,1024]{1,0:T(8,128)}, bf16[512,1024]{1,0:T(8,128)(2,1)}, bf16[16,64...) custom-call(s32[4,4]{1,0:T(4,128)} %lists_ref.1, s32[4]{0:T(128)} %counts_ref.1, s32[1]{0:T(128)} %bitcast.core_ref, ...), custom_call_target="tpu_custom_call" | custom-call | flops 30064771072 | bytes 20971520 | tf_op jit(solution)/shard_map/attention/pallas_call | solution.py:252
  119.4 0.6 collective-permute-start
  120.0 4.7 %all-to-all-start.2 = ((bf16[16,64,1024]{2,1,0:T(8,128)(2,1)}), bf16[16,64,1024]{2,1,0:T(8,128)(2,1)}, u32[]{:S(2)}, u32[]{:S(2)}) async-start(bf16[16,64,1024]{2,1,0:T(8,128)(2,1)} %get-tuple-element.20), calls=%async_computation.2 | async-start | bytes 4194304 | tf_op jit(solution)/shard_map/all_to_all | solution.py:416
  124.8 1.7 convert_add_fusion
  126.5 0.1 fusion.8
  126.6 2.2 %collective-permute-start.1 = (bf16[128,1024]{1,0:T(8,128)(2,1)S(1)}, bf16[128,1024]{1,0:T(8,128)(2,1)S(1)}, u32[]{:S(2)}, u32[]{:S(2)}) collective-permute-start(bf16[128,1024]{1,0:T(8,128)(2,1)S(1)} %get-tuple-element.24), channel_id=1, source_target_pairs={{0,2},{1,3},{2,4},{3,5},{4,6},{5,7},{6,0},{7,1},{8,10},{9,11},{10,... | collective-permute-start | bytes 786440 | tf_op jit(solution)/shard_map/ppermute | solution.py:360
  128.9 4.3 %collective-permute-start.2 = (bf16[128,1024]{1,0:T(8,128)(2,1)S(1)}, bf16[128,1024]{1,0:T(8,128)(2,1)S(1)}, u32[]{:S(2)}, u32[]{:S(2)}) collective-permute-start(bf16[128,1024]{1,0:T(8,128)(2,1)S(1)} %get-tuple-element.26), channel_id=1, source_target_pairs={{0,4},{1,5},{2,6},{3,7},{4,0},{5,1},{6,2},{7,3},{8,12},{9,13},{10,... | collective-permute-start | bytes 786440 | tf_op jit(solution)/shard_map/ppermute | solution.py:360
  133.2 1.7 collective-permute-start.3
  134.8 8.0 %fusion.4 = bf16[1024,1024]{1,0:T(8,128)(2,1)} fusion(bf16[1024,2048]{1,0:T(8,128)(2,1)} %bitcast.79, bf16[1024,1024]{1,0:T(8,128)(2,1)S(1)} %copy-done.3, bf16[1024,1024]{1,0:T(8,128)(2,1)S(1)} %copy-done.2), kind=kOutput, calls=%fused_computation.6 | convolution fusion | flops 4304404480 | bytes 10485760 | tf_op jit(solution)/shard_map/dot_general | solution.py:19
  142.9 2.1 collective-permute-done.2
  145.0 0.1 bitcast_add_fusion
  145.2 1.0 collective-permute-start.4
  146.2 2.4 %collective-permute-start.5 = (bf16[32,1024]{1,0:T(8,128)(2,1)S(1)}, bf16[32,1024]{1,0:T(8,128)(2,1)S(1)}, u32[]{:S(2)}, u32[]{:S(2)}) collective-permute-start(bf16[32,1024]{1,0:T(8,128)(2,1)S(1)} %get-tuple-element.33), channel_id=1, source_target_pairs={{0,16},{8,24},{16,0},{24,8},{32,48},{40,56},{48,32},{56,40},{64,80... | collective-permute-start | bytes 196616 | tf_op jit(solution)/shard_map/ppermute | solution.py:363
  148.6 1.2 collective-permute-start.6
  149.8 3.9 %collective-permute-done.4 = bf16[32,1024]{1,0:T(8,128)(2,1)S(1)} collective-permute-done((bf16[32,1024]{1,0:T(8,128)(2,1)S(1)}, bf16[32,1024]{1,0:T(8,128)(2,1)S(1)}, u32[]{:S(2)}, u32[]{:S(2)}) %collective-permute-start.4) | collective-permute-done | bytes 65568 | tf_op jit(solution)/shard_map/ppermute | solution.py:363
  153.7 6.2 %collective-permute-done.5 = bf16[32,1024]{1,0:T(8,128)(2,1)S(1)} collective-permute-done((bf16[32,1024]{1,0:T(8,128)(2,1)S(1)}, bf16[32,1024]{1,0:T(8,128)(2,1)S(1)}, u32[]{:S(2)}, u32[]{:S(2)}) %collective-permute-start.5) | collective-permute-done | bytes 65568 | tf_op jit(solution)/shard_map/ppermute | solution.py:363
  160.0 2.6 %collective-permute-start.7 = (bf16[32,1024]{1,0:T(8,128)(2,1)S(1)}, bf16[32,1024]{1,0:T(8,128)(2,1)S(1)}, u32[]{:S(2)}, u32[]{:S(2)}) collective-permute-start(bf16[32,1024]{1,0:T(8,128)(2,1)S(1)} %fusion.11), channel_id=1, source_target_pairs={{0,64},{32,96},{64,0},{96,32},{8,72},{40,104},{72,8},{104,40},{16,... | collective-permute-start | bytes 196616 | tf_op jit(solution)/shard_map/ppermute | solution.py:366
  162.6 2.7 %collective-permute-start.9 = (bf16[32,1024]{1,0:T(8,128)(2,1)S(1)}, bf16[32,1024]{1,0:T(8,128)(2,1)S(1)}, u32[]{:S(2)}, u32[]{:S(2)}) collective-permute-start(bf16[32,1024]{1,0:T(8,128)(2,1)S(1)} %fusion.11), channel_id=1, source_target_pairs={{0,96},{32,0},{64,32},{96,64},{8,104},{40,8},{72,40},{104,72},{16,... | collective-permute-start | bytes 196616 | tf_op jit(solution)/shard_map/ppermute | solution.py:366
  165.3 1.6 collective-permute-done.8
  167.0 0.1 collective-permute-start.10
  167.1 1.0 collective-permute-start.11
  168.1 1.6 collective-permute-start.12
  169.7 2.3 %collective-permute-done.10 = bf16[32,1024]{1,0:T(8,128)(2,1)S(1)} collective-permute-done((bf16[32,1024]{1,0:T(8,128)(2,1)S(1)}, bf16[32,1024]{1,0:T(8,128)(2,1)S(1)}, u32[]{:S(2)}, u32[]{:S(2)}) %collective-permute-start.10) | collective-permute-done | bytes 65568 | tf_op jit(solution)/shard_map/ppermute | solution.py:363
  172.1 0.6 collective-permute-done.12
  172.8 6.1 %all-to-all-start.3 = ((bf16[16,64,1024]{2,1,0:T(8,128)(2,1)}), bf16[16,64,1024]{2,1,0:T(8,128)(2,1)}, u32[]{:S(2)}, u32[]{:S(2)}) async-start(bf16[16,64,1024]{2,1,0:T(8,128)(2,1)} %bitcast.5), calls=%async_computation.3 | async-start | bytes 4194304 | tf_op jit(solution)/shard_map/all_to_all | solution.py:424
  178.9 4.0 %convolution_convert_fusion = bf16[512,1024]{1,0:T(8,128)(2,1)} fusion(bf16[512,1024]{1,0:T(8,128)(2,1)S(1)} %copy-done.9, bf16[1024,1024]{1,0:T(8,128)(2,1)} %param.15), kind=kOutput, calls=%fused_computation.7 | convolution fusion | flops 1074266112 | bytes 4194304 | tf_op jit(solution)/shard_map/dot_general | solution.py:19
  182.9 1.5 collective-permute-start.13
  184.4 4.6 %collective-permute-start.14 = (bf16[128,1024]{1,0:T(8,128)(2,1)S(1)}, bf16[128,1024]{1,0:T(8,128)(2,1)S(1)}, u32[]{:S(2)}, u32[]{:S(2)}) collective-permute-start(bf16[128,1024]{1,0:T(8,128)(2,1)S(1)} %get-tuple-element.35), channel_id=1, source_target_pairs={{0,4},{1,5},{2,6},{3,7},{4,0},{5,1},{6,2},{7,3},{8,12},{9,13},{10,... | collective-permute-start | bytes 786440 | tf_op jit(solution)/shard_map/ppermute | solution.py:360
  189.0 2.1 collective-permute-start.15
  191.1 2.2 %convolution_convert_fusion.1 = bf16[512,1024]{1,0:T(8,128)(2,1)} fusion(bf16[512,1024]{1,0:T(8,128)(2,1)S(1)} %copy-done.8, bf16[1024,1024]{1,0:T(8,128)(2,1)S(1)} %copy-done.6), kind=kOutput, calls=%fused_computation.8 | convolution fusion | flops 1074266112 | bytes 4194304 | tf_op jit(solution)/shard_map/dot_general | solution.py:23
  193.4 2.5 %settle.2.refs_0_ = bf16[4,128,1024]{2,1,0:T(8,128)(2,1)} custom-call(s32[16]{0:T(128)S(1)} %reduce.asked_ref, bf16[16,64,1024]{2,1,0:T(8,128)(2,1)} %all-to-all-done.2.x_ref), custom_call_target="tpu_custom_call" | custom-call | flops 1048576 | bytes 3145728 | tf_op jit(solution)/shard_map/settle/pallas_call | solution.py:302
  195.9 0.6 collective-permute-done.14
  196.5 0.1 pad_maximum_fusion
  196.6 0.1 dynamic-slice_bitcast_fusion.3
  196.7 0.1 pad_maximum_fusion.1.x_ref
  196.8 1.9 lay.2.refs_0_
  198.7 5.1 %all-to-all-done.3.x_ref = bf16[16,64,1024]{2,1,0:T(8,128)(2,1)} async-done(((bf16[16,64,1024]{2,1,0:T(8,128)(2,1)}), bf16[16,64,1024]{2,1,0:T(8,128)(2,1)}, u32[]{:S(2)}, u32[]{:S(2)}) %all-to-all-start.3) | async-done | bytes 2097184 | tf_op jit(solution)/shard_map/all_to_all | solution.py:424
  203.8 6.9 %collective-permute-start.16 = (bf16[512,1024]{1,0:T(8,128)(2,1)S(1)}, bf16[512,1024]{1,0:T(8,128)(2,1)S(1)}, u32[]{:S(2)}, u32[]{:S(2)}) collective-permute-start(bf16[512,1024]{1,0:T(8,128)(2,1)S(1)} %pad_maximum_fusion.1.x_ref), channel_id=1, source_target_pairs={{0,1},{1,0},{2,3},{3,2},{4,5},{5,4},{6,7},{7,6},{8,9},{9,8},{10,11... | collective-permute-start | bytes 3145736 | tf_op jit(solution)/shard_map/ppermute | solution.py:369
  210.6 2.5 %settle.3 = bf16[4,128,1024]{2,1,0:T(8,128)(2,1)} custom-call(s32[16]{0:T(128)S(1)} %reduce.asked_ref, bf16[16,64,1024]{2,1,0:T(8,128)(2,1)} %all-to-all-done.3.x_ref, bf16[4,128,1024]{2,1,0:T(8,128)(2,1)} %settle.2.refs_0_), custom_call_target="tpu_custom_call", output_to_operand_aliasing={{}: (2, {})} | custom-call | flops 1048576 | bytes 3145728 | tf_op jit(solution)/shard_map/settle/pallas_call | solution.py:302
  213.2 1.8 lay.3
  (40 shorter events, 0.3 us)
Async XLA Ops:
  0.6 15.0 %copy-start = (bf16[512,1024]{1,0:T(8,128)(2,1)S(1)}, bf16[512,1024]{1,0:T(8,128)(2,1)}, u32[]{:S(2)}) copy-start(bf16[512,1024]{1,0:T(8,128)(2,1)} %param.11) | copy-start | bytes 3145732
  18.5 4.7 %copy-start.5 = (bf16[1024,1024]{1,0:T(8,128)(2,1)S(1)}, bf16[1024,1024]{1,0:T(8,128)(2,1)}, u32[]{:S(2)}) copy-start(bf16[1024,1024]{1,0:T(8,128)(2,1)} %param.18) | copy-start | bytes 6291460
  18.5 63.8 %all-to-all-start.1 = ((bf16[16,128,1024]{2,1,0:T(8,128)(2,1)}), bf16[16,128,1024]{2,1,0:T(8,128)(2,1)}, u32[]{:S(2)}, u32[]{:S(2)}) async-start(bf16[16,128,1024]{2,1,0:T(8,128)(2,1)} %gather_fusion), calls=%async_computation.1 | async-start | bytes 8388608 | tf_op jit(solution)/shard_map/all_to_all | solution.py:406
  23.2 3.7 %copy-start.4 = (bf16[1024,1024]{1,0:T(8,128)(2,1)S(1)}, bf16[1024,1024]{1,0:T(8,128)(2,1)}, u32[]{:S(2)}) copy-start(bf16[1024,1024]{1,0:T(8,128)(2,1)} %param.15) | copy-start | bytes 6291460
  23.2 3.7 %copy-start.7 = (bf16[512,1024]{1,0:T(8,128)(2,1)S(1)}, bf16[512,1024]{1,0:T(8,128)(2,1)}, u32[]{:S(2)}) copy-start(bf16[512,1024]{1,0:T(8,128)(2,1)} %param.10) | copy-start | bytes 3145732
  119.4 5.3 %collective-permute-start = (bf16[512,1024]{1,0:T(8,128)(2,1)}, bf16[512,1024]{1,0:T(8,128)(2,1)}, u32[]{:S(2)}, u32[]{:S(2)}) collective-permute-start(bf16[512,1024]{1,0:T(8,128)(2,1)} %get-tuple-element.18), channel_id=1, source_target_pairs={{0,1},{1,0},{2,3},{3,2},{4,5},{5,4},{6,7},{7,6},{8,9},{9,8},{10,11... | collective-permute-start | bytes 3145736 | tf_op jit(solution)/shard_map/ppermute | solution.py:369
  120.0 4.8 %copy-start.1 = (f32[512,1024]{1,0:T(8,128)S(1)}, f32[512,1024]{1,0:T(8,128)}, u32[]{:S(2)}) copy-start(f32[512,1024]{1,0:T(8,128)} %get-tuple-element.17) | copy-start | bytes 6291460
  120.0 40.0 %all-to-all-start.2 = ((bf16[16,64,1024]{2,1,0:T(8,128)(2,1)}), bf16[16,64,1024]{2,1,0:T(8,128)(2,1)}, u32[]{:S(2)}, u32[]{:S(2)}) async-start(bf16[16,64,1024]{2,1,0:T(8,128)(2,1)} %get-tuple-element.20), calls=%async_computation.2 | async-start | bytes 4194304 | tf_op jit(solution)/shard_map/all_to_all | solution.py:416
  124.7 10.1 %copy-start.2 = (bf16[1024,1024]{1,0:T(8,128)(2,1)S(1)}, bf16[1024,1024]{1,0:T(8,128)(2,1)}, u32[]{:S(2)}) copy-start(bf16[1024,1024]{1,0:T(8,128)(2,1)} %wk_hbm.1) | copy-start | bytes 6291460
  124.7 10.1 %copy-start.3 = (bf16[1024,1024]{1,0:T(8,128)(2,1)S(1)}, bf16[1024,1024]{1,0:T(8,128)(2,1)}, u32[]{:S(2)}) copy-start(bf16[1024,1024]{1,0:T(8,128)(2,1)} %wv_hbm.1) | copy-start | bytes 6291460
  126.6 16.3 %collective-permute-start.1 = (bf16[128,1024]{1,0:T(8,128)(2,1)S(1)}, bf16[128,1024]{1,0:T(8,128)(2,1)S(1)}, u32[]{:S(2)}, u32[]{:S(2)}) collective-permute-start(bf16[128,1024]{1,0:T(8,128)(2,1)S(1)} %get-tuple-element.24), channel_id=1, source_target_pairs={{0,2},{1,3},{2,4},{3,5},{4,6},{5,7},{6,0},{7,1},{8,10},{9,11},{10,... | collective-permute-start | bytes 786440 | tf_op jit(solution)/shard_map/ppermute | solution.py:360
  128.9 16.1 %collective-permute-start.2 = (bf16[128,1024]{1,0:T(8,128)(2,1)S(1)}, bf16[128,1024]{1,0:T(8,128)(2,1)S(1)}, u32[]{:S(2)}, u32[]{:S(2)}) collective-permute-start(bf16[128,1024]{1,0:T(8,128)(2,1)S(1)} %get-tuple-element.26), channel_id=1, source_target_pairs={{0,4},{1,5},{2,6},{3,7},{4,0},{5,1},{6,2},{7,3},{8,12},{9,13},{10,... | collective-permute-start | bytes 786440 | tf_op jit(solution)/shard_map/ppermute | solution.py:360
  133.2 11.8 %collective-permute-start.3 = (bf16[128,1024]{1,0:T(8,128)(2,1)S(1)}, bf16[128,1024]{1,0:T(8,128)(2,1)S(1)}, u32[]{:S(2)}, u32[]{:S(2)}) collective-permute-start(bf16[128,1024]{1,0:T(8,128)(2,1)S(1)} %get-tuple-element.25), channel_id=1, source_target_pairs={{0,6},{1,7},{2,0},{3,1},{4,2},{5,3},{6,4},{7,5},{8,14},{9,15},{10,... | collective-permute-start | bytes 786440 | tf_op jit(solution)/shard_map/ppermute | solution.py:360
  145.2 8.5 %collective-permute-start.4 = (bf16[32,1024]{1,0:T(8,128)(2,1)S(1)}, bf16[32,1024]{1,0:T(8,128)(2,1)S(1)}, u32[]{:S(2)}, u32[]{:S(2)}) collective-permute-start(bf16[32,1024]{1,0:T(8,128)(2,1)S(1)} %get-tuple-element.31), channel_id=1, source_target_pairs={{0,8},{8,16},{16,24},{24,0},{32,40},{40,48},{48,56},{56,32},{64,72... | collective-permute-start | bytes 196616 | tf_op jit(solution)/shard_map/ppermute | solution.py:363
  146.2 13.7 %collective-permute-start.5 = (bf16[32,1024]{1,0:T(8,128)(2,1)S(1)}, bf16[32,1024]{1,0:T(8,128)(2,1)S(1)}, u32[]{:S(2)}, u32[]{:S(2)}) collective-permute-start(bf16[32,1024]{1,0:T(8,128)(2,1)S(1)} %get-tuple-element.33), channel_id=1, source_target_pairs={{0,16},{8,24},{16,0},{24,8},{32,48},{40,56},{48,32},{56,40},{64,80... | collective-permute-start | bytes 196616 | tf_op jit(solution)/shard_map/ppermute | solution.py:363
  148.6 11.3 %collective-permute-start.6 = (bf16[32,1024]{1,0:T(8,128)(2,1)S(1)}, bf16[32,1024]{1,0:T(8,128)(2,1)S(1)}, u32[]{:S(2)}, u32[]{:S(2)}) collective-permute-start(bf16[32,1024]{1,0:T(8,128)(2,1)S(1)} %get-tuple-element.32), channel_id=1, source_target_pairs={{0,24},{8,0},{16,8},{24,16},{32,56},{40,32},{48,40},{56,48},{64,88... | collective-permute-start | bytes 196616 | tf_op jit(solution)/shard_map/ppermute | solution.py:363
  160.0 5.3 %collective-permute-start.7 = (bf16[32,1024]{1,0:T(8,128)(2,1)S(1)}, bf16[32,1024]{1,0:T(8,128)(2,1)S(1)}, u32[]{:S(2)}, u32[]{:S(2)}) collective-permute-start(bf16[32,1024]{1,0:T(8,128)(2,1)S(1)} %fusion.11), channel_id=1, source_target_pairs={{0,64},{32,96},{64,0},{96,32},{8,72},{40,104},{72,8},{104,40},{16,... | collective-permute-start | bytes 196616 | tf_op jit(solution)/shard_map/ppermute | solution.py:366
  162.6 4.3 %collective-permute-start.8 = (bf16[32,1024]{1,0:T(8,128)(2,1)S(1)}, bf16[32,1024]{1,0:T(8,128)(2,1)S(1)}, u32[]{:S(2)}, u32[]{:S(2)}) collective-permute-start(bf16[32,1024]{1,0:T(8,128)(2,1)S(1)} %fusion.11), channel_id=1, source_target_pairs={{0,32},{32,64},{64,96},{96,0},{8,40},{40,72},{72,104},{104,8},{16,... | collective-permute-start | bytes 196616 | tf_op jit(solution)/shard_map/ppermute | solution.py:366
  162.6 4.3 %collective-permute-start.9 = (bf16[32,1024]{1,0:T(8,128)(2,1)S(1)}, bf16[32,1024]{1,0:T(8,128)(2,1)S(1)}, u32[]{:S(2)}, u32[]{:S(2)}) collective-permute-start(bf16[32,1024]{1,0:T(8,128)(2,1)S(1)} %fusion.11), channel_id=1, source_target_pairs={{0,96},{32,0},{64,32},{96,64},{8,104},{40,8},{72,40},{104,72},{16,... | collective-permute-start | bytes 196616 | tf_op jit(solution)/shard_map/ppermute | solution.py:366
  167.0 5.1 %collective-permute-start.10 = (bf16[32,1024]{1,0:T(8,128)(2,1)S(1)}, bf16[32,1024]{1,0:T(8,128)(2,1)S(1)}, u32[]{:S(2)}, u32[]{:S(2)}) collective-permute-start(bf16[32,1024]{1,0:T(8,128)(2,1)S(1)} %add_convert_fusion), channel_id=1, source_target_pairs={{0,8},{8,16},{16,24},{24,0},{32,40},{40,48},{48,56},{56,32},{64,72... | collective-permute-start | bytes 196616 | tf_op jit(solution)/shard_map/ppermute | solution.py:363
  167.1 5.0 %collective-permute-start.11 = (bf16[32,1024]{1,0:T(8,128)(2,1)S(1)}, bf16[32,1024]{1,0:T(8,128)(2,1)S(1)}, u32[]{:S(2)}, u32[]{:S(2)}) collective-permute-start(bf16[32,1024]{1,0:T(8,128)(2,1)S(1)} %add_convert_fusion), channel_id=1, source_target_pairs={{0,16},{8,24},{16,0},{24,8},{32,48},{40,56},{48,32},{56,40},{64,80... | collective-permute-start | bytes 196616 | tf_op jit(solution)/shard_map/ppermute | solution.py:363
  168.1 4.6 %collective-permute-start.12 = (bf16[32,1024]{1,0:T(8,128)(2,1)S(1)}, bf16[32,1024]{1,0:T(8,128)(2,1)S(1)}, u32[]{:S(2)}, u32[]{:S(2)}) collective-permute-start(bf16[32,1024]{1,0:T(8,128)(2,1)S(1)} %add_convert_fusion), channel_id=1, source_target_pairs={{0,24},{8,0},{16,8},{24,16},{32,56},{40,32},{48,40},{56,48},{64,88... | collective-permute-start | bytes 196616 | tf_op jit(solution)/shard_map/ppermute | solution.py:363
  172.8 6.1 %copy-start.9 = (bf16[512,1024]{1,0:T(8,128)(2,1)S(1)}, bf16[512,1024]{1,0:T(8,128)(2,1)}, u32[]{:S(2)}) copy-start(bf16[512,1024]{1,0:T(8,128)(2,1)} %get-tuple-element.15) | copy-start | bytes 3145732
  172.8 31.0 %all-to-all-start.3 = ((bf16[16,64,1024]{2,1,0:T(8,128)(2,1)}), bf16[16,64,1024]{2,1,0:T(8,128)(2,1)}, u32[]{:S(2)}, u32[]{:S(2)}) async-start(bf16[16,64,1024]{2,1,0:T(8,128)(2,1)} %bitcast.5), calls=%async_computation.3 | async-start | bytes 4194304 | tf_op jit(solution)/shard_map/all_to_all | solution.py:424
  178.9 12.2 %copy-start.6 = (bf16[1024,1024]{1,0:T(8,128)(2,1)S(1)}, bf16[1024,1024]{1,0:T(8,128)(2,1)}, u32[]{:S(2)}) copy-start(bf16[1024,1024]{1,0:T(8,128)(2,1)} %param.18) | copy-start | bytes 6291460
  178.9 12.2 %copy-start.8 = (bf16[512,1024]{1,0:T(8,128)(2,1)S(1)}, bf16[512,1024]{1,0:T(8,128)(2,1)}, u32[]{:S(2)}) copy-start(bf16[512,1024]{1,0:T(8,128)(2,1)} %get-tuple-element.14) | copy-start | bytes 3145732
  182.9 12.9 %collective-permute-start.13 = (bf16[128,1024]{1,0:T(8,128)(2,1)S(1)}, bf16[128,1024]{1,0:T(8,128)(2,1)S(1)}, u32[]{:S(2)}, u32[]{:S(2)}) collective-permute-start(bf16[128,1024]{1,0:T(8,128)(2,1)S(1)} %get-tuple-element.35), channel_id=1, source_target_pairs={{0,2},{1,3},{2,4},{3,5},{4,6},{5,7},{6,0},{7,1},{8,10},{9,11},{10,... | collective-permute-start | bytes 786440 | tf_op jit(solution)/shard_map/ppermute | solution.py:360
  184.4 12.1 %collective-permute-start.14 = (bf16[128,1024]{1,0:T(8,128)(2,1)S(1)}, bf16[128,1024]{1,0:T(8,128)(2,1)S(1)}, u32[]{:S(2)}, u32[]{:S(2)}) collective-permute-start(bf16[128,1024]{1,0:T(8,128)(2,1)S(1)} %get-tuple-element.35), channel_id=1, source_target_pairs={{0,4},{1,5},{2,6},{3,7},{4,0},{5,1},{6,2},{7,3},{8,12},{9,13},{10,... | collective-permute-start | bytes 786440 | tf_op jit(solution)/shard_map/ppermute | solution.py:360
  189.0 7.5 %collective-permute-start.15 = (bf16[128,1024]{1,0:T(8,128)(2,1)S(1)}, bf16[128,1024]{1,0:T(8,128)(2,1)S(1)}, u32[]{:S(2)}, u32[]{:S(2)}) collective-permute-start(bf16[128,1024]{1,0:T(8,128)(2,1)S(1)} %get-tuple-element.35), channel_id=1, source_target_pairs={{0,6},{1,7},{2,0},{3,1},{4,2},{5,3},{6,4},{7,5},{8,14},{9,15},{10,... | collective-permute-start | bytes 786440 | tf_op jit(solution)/shard_map/ppermute | solution.py:360
  203.8 9.4 %collective-permute-start.16 = (bf16[512,1024]{1,0:T(8,128)(2,1)S(1)}, bf16[512,1024]{1,0:T(8,128)(2,1)S(1)}, u32[]{:S(2)}, u32[]{:S(2)}) collective-permute-start(bf16[512,1024]{1,0:T(8,128)(2,1)S(1)} %pad_maximum_fusion.1.x_ref), channel_id=1, source_target_pairs={{0,1},{1,0},{2,3},{3,2},{4,5},{5,4},{6,7},{7,6},{8,9},{9,8},{10,11... | collective-permute-start | bytes 3145736 | tf_op jit(solution)/shard_map/ppermute | solution.py:369

commit v7 on v6

--- a/solution.py
+++ b/solution.py
@@ -164,7 +164,7 @@
             acc_ref[s, quads + c] += grad_value[j * rows:(j + 1) * rows]
         return carry
 
-    lax.fori_loop(0, groups * quads, step, 0, unroll=4)
+    lax.fori_loop(0, groups * quads, step, 0, unroll=8)
 
     results = [
         pltpu.make_async_copy(src, dst, result_sems.at[i])
@@ -297,7 +297,7 @@
 
 def settle(asked, x, owned, piece, earlier=()):
     slots, rows, width = x.shape
-    cut = 32
+    cut = 16
     first = piece * (rows // cut)
     return pl.pallas_call(
         settle_kernel,
@@ -329,9 +329,10 @@
     refs[-1][...] = x_ref[...].astype(refs[-1].dtype)
 
 
-def lay(half, x, earlier=()):
+def lay(half, x, total, at=0, earlier=()):
     rows, width = x.shape
     cut = 128
+    per_half, first = total // 2 // cut, at // cut
     return pl.pallas_call(
         lay_kernel,
         grid_spec=pltpu.PrefetchScalarGridSpec(
@@ -339,9 +340,9 @@
             grid=(rows // cut,),
             in_specs=[pl.BlockSpec((cut, width), lambda i, half_ref: (i, 0))]
             + [pl.BlockSpec(memory_space=pl.ANY)] * len(earlier),
-            out_specs=pl.BlockSpec((cut, width), lambda i, half_ref: (half_ref[0] * (rows // cut) + i, 0)),
+            out_specs=pl.BlockSpec((cut, width), lambda i, half_ref: (half_ref[0] * per_half + first + i, 0)),
         ),
-        out_shape=jax.ShapeDtypeStruct((2 * rows, width), jnp.float32),
+        out_shape=jax.ShapeDtypeStruct((total, width), jnp.float32),
         input_output_aliases={2: 0} if earlier else {},
         compiler_params=pltpu.CompilerParams(vmem_limit_bytes=16 * MIB),
         cost_estimate=pl.CostEstimate(flops=rows * width, bytes_accessed=6 * rows * width, transcendentals=0),
@@ -388,9 +389,11 @@
     second_piece = send_second(part)
     part = gather(part, along_z, z)
     mine = core.astype(jnp.int32).reshape(1)
-    laid = lay(mine, part)
-    other = swap(after(part, second_piece, laid, *others))
-    return lay(1 - mine, other, (laid,)), second_piece
+    total, most = 2 * part.shape[0], part.shape[0] * 3 // 4
+    laid = lay(mine, part, total)
+    laid = lay(1 - mine, swap(part[:most]), total, 0, (laid,))
+    other = swap(after(part[most:], second_piece, laid, *others))
+    return lay(1 - mine, other, total, most, (laid,)), second_piece
 
 
 def per_device(

time: 217 us -> 218 us (level)
  waiting for transfers between devices: 75.9 us -> 80.2 us
  starting transfers between devices: 52 us -> 48.9 us
  Pallas kernels: 45.8 us -> 48.7 us
    ppermute x6, waiting for transfers between devices: 2.79 us -> 12 us  [along_z(): lax.ppermute(a, 'slab', [(p * 2 + c, (p + by) % SIDE * 2 + c) for p in ra...]
    all_to_all x1, waiting for transfers between devices: 5.1 us -> 0.01 us  [send_second(): lax.all_to_all(after(second, summed), 'region', split_axis=0, concat_axis...]
    ppermute x6, starting transfers between devices: 16.4 us -> 12.7 us  [along_z(): lax.ppermute(a, 'slab', [(p * 2 + c, (p + by) % SIDE * 2 + c) for p in ra...]
    pallas_call x2, Pallas kernels: 5.02 us -> 7.49 us  [settle(): pl.pallas_call(settle_kernel, grid=(rows // cut,), in_specs=[pl.BlockSpec...]
    ppermute x2 -> x3, starting transfers between devices: 7.42 us -> 7.32 us  [swap(): lax.ppermute(a, 'slab', [(p * 2 + c, p * 2 + 1 - c) for p in range(SIDE)...]
  transfers between devices with their start and end apart: 20 -> 21, of which waited for: 9 -> 9; matrix products, arithmetic and copies ran while one was open for 10% -> 10% of each run, Pallas kernels for 3% -> 5%
where the time goes in v7:
time: 218 us; the launch traced here: 217 us
  waiting for transfers between devices  80.2 us (37%)
  starting transfers between devices  48.9 us (22%)
  Pallas kernels  48.7 us (22%)
  matrix products  18.3 us (8%)
  blocking collectives  13.8 us (6%)
  local copies, waits for them, and re-layouts  3.97 us (2%)
  other arithmetic  2.65 us (1%)
    all_to_all x1, waiting for transfers between devices, per_device(): lax.all_to_all(outgoing, 'region', split_axis=0, concat_axis=0, tiled=True)  53.2 us
    pallas_call x1, Pallas kernels, attention(): pl.pallas_call(attention_kernel, in_specs=[smem] * 3 + [hbm] * 6, out_spe...  36.8 us
    dot_general x3, matrix products, nt(): lax.dot_general(a, b, (((1,), (1,)), ((), ())), preferred_element_type=jn...  13.8 us
    all_to_all x1, blocking collectives, per_device(): lax.all_to_all(requests.reshape(-1), 'region', split_axis=0, concat_axis=...  13.8 us
    ppermute x6, waiting for transfers between devices, along_x(): lax.ppermute(a, 'region', [(p * SIDE + i, p * SIDE + (i + by) % SIDE) for...  13 us
    ppermute x6, starting transfers between devices, along_z(): lax.ppermute(a, 'slab', [(p * 2 + c, (p + by) % SIDE * 2 + c) for p in ra...  12.7 us
    ppermute x6, waiting for transfers between devices, along_z(): lax.ppermute(a, 'slab', [(p * 2 + c, (p + by) % SIDE * 2 + c) for p in ra...  12 us
    pallas_call x2, Pallas kernels, settle(): pl.pallas_call(settle_kernel, grid=(rows // cut,), in_specs=[pl.BlockSpec...  7.49 us
  transfers between devices with their start and end apart: 21, of which 9 were waited for; matrix products, arithmetic and copies ran while one was open for 10% of the time, Pallas kernels for 5%

profile of v7, /device:TPU:1, one launch (start us, length us, event | category | flops | bytes accessed | tf_op | source)
XLA Modules:
  0.0 217.4 jit_solution(4537775874942568411)
XLA Ops:
  0.6 0.8 copy.18
  1.5 13.8 %all_to_all.29 = s32[16,1,1]{2,1,0:T(1,128)S(1)} all-to-all(s32[16,1,1]{2,1,0:T(1,128)S(1)} %copy.18), channel_id=1, replica_groups=mesh['region'=16,'slab'=8] {'region'}, dimensions={0} | all-to-all | bytes 128 | tf_op jit(solution)/shard_map/all_to_all | solution.py:407
  15.2 0.4 reduce.asked_ref
  15.7 2.8 %gather_fusion = bf16[16,128,1024]{2,1,0:T(8,128)(2,1)} fusion(bf16[4,128,1024]{2,1,0:T(8,128)(2,1)S(1)} %bitcast.65, s32[1024]{0:T(1024)S(1)} %pad_clamp_fusion), kind=kCustom, calls=%fused_computation | custom fusion | bytes 8388672 | tf_op jit(solution)/shard_map/gather | solution.py:408
  18.5 4.7 %all-to-all-start.1 = ((bf16[16,128,1024]{2,1,0:T(8,128)(2,1)}), bf16[16,128,1024]{2,1,0:T(8,128)(2,1)}, u32[]{:S(2)}, u32[]{:S(2)}) async-start(bf16[16,128,1024]{2,1,0:T(8,128)(2,1)} %gather_fusion), calls=%async_computation.1 | async-start | bytes 8388608 | tf_op jit(solution)/shard_map/all_to_all | solution.py:409
  23.2 3.6 %convolution_convert_fusion.2.ga_hbm = bf16[512,1024]{1,0:T(8,128)(2,1)} fusion(bf16[512,1024]{1,0:T(8,128)(2,1)} %cot_hbm.1, bf16[1024,1024]{1,0:T(8,128)(2,1)S(1)} %copy-done.6), kind=kOutput, calls=%fused_computation.9 | convolution fusion | flops 1074266112 | bytes 4194304 | tf_op jit(solution)/shard_map/dot_general | solution.py:19
  26.9 2.2 %fusion.7.q_hbm = bf16[512,1024]{1,0:T(8,128)(2,1)} fusion(bf16[512,1024]{1,0:T(8,128)(2,1)S(1)} %copy-done.8, bf16[1024,1024]{1,0:T(8,128)(2,1)S(1)} %copy-done.4), kind=kOutput, calls=%fused_computation.11 | convolution fusion | flops 1074790400 | bytes 4194304 | tf_op jit(solution)/shard_map/dot_general | solution.py:23
  29.1 53.2 %all-to-all-done.1.x_hbm = bf16[16,128,1024]{2,1,0:T(8,128)(2,1)} async-done(((bf16[16,128,1024]{2,1,0:T(8,128)(2,1)}), bf16[16,128,1024]{2,1,0:T(8,128)(2,1)}, u32[]{:S(2)}, u32[]{:S(2)}) %all-to-all-start.1) | async-done | bytes 4194336 | tf_op jit(solution)/shard_map/all_to_all | solution.py:409
  82.3 36.8 %attention.1 = (bf16[512,1024]{1,0:T(8,128)(2,1)}, bf16[512,1024]{1,0:T(8,128)(2,1)}, f32[512,1024]{1,0:T(8,128)}, bf16[512,1024]{1,0:T(8,128)(2,1)}, bf16[16,64...) custom-call(s32[4,4]{1,0:T(4,128)} %lists_ref.1, s32[4]{0:T(128)} %counts_ref.1, s32[1]{0:T(128)} %bitcast.core_ref, ...), custom_call_target="tpu_custom_call" | custom-call | flops 30064771072 | bytes 20971520 | tf_op jit(solution)/shard_map/attention/pallas_call | solution.py:252
  119.2 0.6 collective-permute-start
  119.7 6.3 %all-to-all-start.2 = ((bf16[16,64,1024]{2,1,0:T(8,128)(2,1)}), bf16[16,64,1024]{2,1,0:T(8,128)(2,1)}, u32[]{:S(2)}, u32[]{:S(2)}) async-start(bf16[16,64,1024]{2,1,0:T(8,128)(2,1)} %get-tuple-element.20), calls=%async_computation.2 | async-start | bytes 4194304 | tf_op jit(solution)/shard_map/all_to_all | solution.py:419
  126.1 1.7 convert_add_fusion
  127.8 0.1 fusion.8
  128.0 3.5 %collective-permute-start.1 = (bf16[128,1024]{1,0:T(8,128)(2,1)S(1)}, bf16[128,1024]{1,0:T(8,128)(2,1)S(1)}, u32[]{:S(2)}, u32[]{:S(2)}) collective-permute-start(bf16[128,1024]{1,0:T(8,128)(2,1)S(1)} %get-tuple-element.24), channel_id=1, source_target_pairs={{0,2},{1,3},{2,4},{3,5},{4,6},{5,7},{6,0},{7,1},{8,10},{9,11},{10,... | collective-permute-start | bytes 786440 | tf_op jit(solution)/shard_map/ppermute | solution.py:361
  131.5 2.4 %collective-permute-start.2 = (bf16[128,1024]{1,0:T(8,128)(2,1)S(1)}, bf16[128,1024]{1,0:T(8,128)(2,1)S(1)}, u32[]{:S(2)}, u32[]{:S(2)}) collective-permute-start(bf16[128,1024]{1,0:T(8,128)(2,1)S(1)} %get-tuple-element.26), channel_id=1, source_target_pairs={{0,4},{1,5},{2,6},{3,7},{4,0},{5,1},{6,2},{7,3},{8,12},{9,13},{10,... | collective-permute-start | bytes 786440 | tf_op jit(solution)/shard_map/ppermute | solution.py:361
  134.0 7.9 %fusion.4 = bf16[1024,1024]{1,0:T(8,128)(2,1)} fusion(bf16[1024,2048]{1,0:T(8,128)(2,1)} %bitcast.79, bf16[1024,1024]{1,0:T(8,128)(2,1)S(1)} %copy-done.3, bf16[1024,1024]{1,0:T(8,128)(2,1)S(1)} %copy-done.2), kind=kOutput, calls=%fused_computation.6 | convolution fusion | flops 4304404480 | bytes 10485760 | tf_op jit(solution)/shard_map/dot_general | solution.py:19
  141.9 4.2 %collective-permute-done.2 = bf16[128,1024]{1,0:T(8,128)(2,1)S(1)} collective-permute-done((bf16[128,1024]{1,0:T(8,128)(2,1)S(1)}, bf16[128,1024]{1,0:T(8,128)(2,1)S(1)}, u32[]{:S(2)}, u32[]{:S(2)}) %collective-permute-start.2) | collective-permute-done | bytes 262176 | tf_op jit(solution)/shard_map/ppermute | solution.py:361
  146.1 0.1 bitcast_add_fusion
  146.2 0.9 collective-permute-start.4
  147.2 2.4 %collective-permute-start.5 = (bf16[32,1024]{1,0:T(8,128)(2,1)S(1)}, bf16[32,1024]{1,0:T(8,128)(2,1)S(1)}, u32[]{:S(2)}, u32[]{:S(2)}) collective-permute-start(bf16[32,1024]{1,0:T(8,128)(2,1)S(1)} %get-tuple-element.33), channel_id=1, source_target_pairs={{0,16},{8,24},{16,0},{24,8},{32,48},{40,56},{48,32},{56,40},{64,80... | collective-permute-start | bytes 196616 | tf_op jit(solution)/shard_map/ppermute | solution.py:364
  149.6 1.2 collective-permute-start.6
  150.8 4.4 %collective-permute-done.4 = bf16[32,1024]{1,0:T(8,128)(2,1)S(1)} collective-permute-done((bf16[32,1024]{1,0:T(8,128)(2,1)S(1)}, bf16[32,1024]{1,0:T(8,128)(2,1)S(1)}, u32[]{:S(2)}, u32[]{:S(2)}) %collective-permute-start.4) | collective-permute-done | bytes 65568 | tf_op jit(solution)/shard_map/ppermute | solution.py:364
  155.2 5.7 %collective-permute-done.5 = bf16[32,1024]{1,0:T(8,128)(2,1)S(1)} collective-permute-done((bf16[32,1024]{1,0:T(8,128)(2,1)S(1)}, bf16[32,1024]{1,0:T(8,128)(2,1)S(1)}, u32[]{:S(2)}, u32[]{:S(2)}) %collective-permute-start.5) | collective-permute-done | bytes 65568 | tf_op jit(solution)/shard_map/ppermute | solution.py:364
  160.9 2.3 %collective-permute-start.7 = (bf16[32,1024]{1,0:T(8,128)(2,1)S(1)}, bf16[32,1024]{1,0:T(8,128)(2,1)S(1)}, u32[]{:S(2)}, u32[]{:S(2)}) collective-permute-start(bf16[32,1024]{1,0:T(8,128)(2,1)S(1)} %fusion.11), channel_id=1, source_target_pairs={{0,64},{32,96},{64,0},{96,32},{8,72},{40,104},{72,8},{104,40},{16,... | collective-permute-start | bytes 196616 | tf_op jit(solution)/shard_map/ppermute | solution.py:367
  163.3 2.7 %collective-permute-start.9 = (bf16[32,1024]{1,0:T(8,128)(2,1)S(1)}, bf16[32,1024]{1,0:T(8,128)(2,1)S(1)}, u32[]{:S(2)}, u32[]{:S(2)}) collective-permute-start(bf16[32,1024]{1,0:T(8,128)(2,1)S(1)} %fusion.11), channel_id=1, source_target_pairs={{0,96},{32,0},{64,32},{96,64},{8,104},{40,8},{72,40},{104,72},{16,... | collective-permute-start | bytes 196616 | tf_op jit(solution)/shard_map/ppermute | solution.py:367
  165.9 1.9 collective-permute-done.8
  167.9 0.1 collective-permute-start.10
  168.0 1.5 collective-permute-start.11
  169.5 1.1 collective-permute-start.12
  170.6 2.3 %collective-permute-done.10 = bf16[32,1024]{1,0:T(8,128)(2,1)S(1)} collective-permute-done((bf16[32,1024]{1,0:T(8,128)(2,1)S(1)}, bf16[32,1024]{1,0:T(8,128)(2,1)S(1)}, u32[]{:S(2)}, u32[]{:S(2)}) %collective-permute-start.10) | collective-permute-done | bytes 65568 | tf_op jit(solution)/shard_map/ppermute | solution.py:364
  173.0 0.6 collective-permute-done.12
  173.7 5.7 %all-to-all-start.3 = ((bf16[16,64,1024]{2,1,0:T(8,128)(2,1)}), bf16[16,64,1024]{2,1,0:T(8,128)(2,1)}, u32[]{:S(2)}, u32[]{:S(2)}) async-start(bf16[16,64,1024]{2,1,0:T(8,128)(2,1)} %bitcast.5), calls=%async_computation.3 | async-start | bytes 4194304 | tf_op jit(solution)/shard_map/all_to_all | solution.py:427
  179.4 3.3 %collective-permute-start.13 = (bf16[128,1024]{1,0:T(8,128)(2,1)S(1)}, bf16[128,1024]{1,0:T(8,128)(2,1)S(1)}, u32[]{:S(2)}, u32[]{:S(2)}) collective-permute-start(bf16[128,1024]{1,0:T(8,128)(2,1)S(1)} %get-tuple-element.35), channel_id=1, source_target_pairs={{0,2},{1,3},{2,4},{3,5},{4,6},{5,7},{6,0},{7,1},{8,10},{9,11},{10,... | collective-permute-start | bytes 786440 | tf_op jit(solution)/shard_map/ppermute | solution.py:361
  182.7 3.3 %collective-permute-start.14 = (bf16[128,1024]{1,0:T(8,128)(2,1)S(1)}, bf16[128,1024]{1,0:T(8,128)(2,1)S(1)}, u32[]{:S(2)}, u32[]{:S(2)}) collective-permute-start(bf16[128,1024]{1,0:T(8,128)(2,1)S(1)} %get-tuple-element.35), channel_id=1, source_target_pairs={{0,4},{1,5},{2,6},{3,7},{4,0},{5,1},{6,2},{7,3},{8,12},{9,13},{10,... | collective-permute-start | bytes 786440 | tf_op jit(solution)/shard_map/ppermute | solution.py:361
  186.0 3.0 %collective-permute-done.13 = bf16[128,1024]{1,0:T(8,128)(2,1)S(1)} collective-permute-done((bf16[128,1024]{1,0:T(8,128)(2,1)S(1)}, bf16[128,1024]{1,0:T(8,128)(2,1)S(1)}, u32[]{:S(2)}, u32[]{:S(2)}) %collective-permute-start.13) | collective-permute-done | bytes 262176 | tf_op jit(solution)/shard_map/ppermute | solution.py:361
  189.0 4.8 %collective-permute-done.14 = bf16[128,1024]{1,0:T(8,128)(2,1)S(1)} collective-permute-done((bf16[128,1024]{1,0:T(8,128)(2,1)S(1)}, bf16[128,1024]{1,0:T(8,128)(2,1)S(1)}, u32[]{:S(2)}, u32[]{:S(2)}) %collective-permute-start.14) | collective-permute-done | bytes 262176 | tf_op jit(solution)/shard_map/ppermute | solution.py:361
  193.9 0.1 pad_maximum_fusion
  194.0 0.1 dynamic-slice_bitcast_fusion.2
  194.2 5.2 %collective-permute-start.16 = (bf16[384,1024]{1,0:T(8,128)(2,1)S(1)}, bf16[384,1024]{1,0:T(8,128)(2,1)S(1)}, u32[]{:S(2)}, u32[]{:S(2)}) collective-permute-start(bf16[384,1024]{1,0:T(8,128)(2,1)S(1)} %pad_maximum_fusion.2), channel_id=1, source_target_pairs={{0,1},{1,0},{2,3},{3,2},{4,5},{5,4},{6,7},{7,6},{8,9},{9,8},{10,11... | collective-permute-start | bytes 2359304 | tf_op jit(solution)/shard_map/ppermute | solution.py:370
  199.3 2.3 %convolution_convert_fusion = bf16[512,1024]{1,0:T(8,128)(2,1)} fusion(bf16[512,1024]{1,0:T(8,128)(2,1)S(1)} %copy-done.10, bf16[1024,1024]{1,0:T(8,128)(2,1)S(1)} %copy-done.5), kind=kOutput, calls=%fused_computation.7 | convolution fusion | flops 1074266112 | bytes 4194304 | tf_op jit(solution)/shard_map/dot_general | solution.py:19
  201.6 2.2 %convolution_convert_fusion.1 = bf16[512,1024]{1,0:T(8,128)(2,1)} fusion(bf16[512,1024]{1,0:T(8,128)(2,1)S(1)} %copy-done.9, bf16[1024,1024]{1,0:T(8,128)(2,1)S(1)} %copy-done.7), kind=kOutput, calls=%fused_computation.8 | convolution fusion | flops 1074266112 | bytes 4194304 | tf_op jit(solution)/shard_map/dot_general | solution.py:23
  203.8 3.7 %settle.2.refs_0_ = bf16[4,128,1024]{2,1,0:T(8,128)(2,1)} custom-call(s32[16]{0:T(128)S(1)} %reduce.asked_ref, bf16[16,64,1024]{2,1,0:T(8,128)(2,1)} %all-to-all-done.2.x_ref), custom_call_target="tpu_custom_call" | custom-call | flops 1048576 | bytes 3145728 | tf_op jit(solution)/shard_map/settle/pallas_call | solution.py:302
  207.6 0.1 pad_maximum_fusion.1.x_ref
  207.6 1.9 lay.3.refs_0_
  209.5 1.7 lay.4.refs_0_
  211.2 1.6 collective-permute-start.17
  212.8 3.8 %settle.3 = bf16[4,128,1024]{2,1,0:T(8,128)(2,1)} custom-call(s32[16]{0:T(128)S(1)} %reduce.asked_ref, bf16[16,64,1024]{2,1,0:T(8,128)(2,1)} %all-to-all-done.3.x_ref, bf16[4,128,1024]{2,1,0:T(8,128)(2,1)} %settle.2.refs_0_), custom_call_target="tpu_custom_call", output_to_operand_aliasing={{}: (2, {})} | custom-call | flops 1048576 | bytes 3145728 | tf_op jit(solution)/shard_map/settle/pallas_call | solution.py:302
  216.5 0.8 lay.5
  (46 shorter events, 0.4 us)
Async XLA Ops:
  0.6 15.0 %copy-start = (bf16[512,1024]{1,0:T(8,128)(2,1)S(1)}, bf16[512,1024]{1,0:T(8,128)(2,1)}, u32[]{:S(2)}) copy-start(bf16[512,1024]{1,0:T(8,128)(2,1)} %param.11) | copy-start | bytes 3145732
  18.5 4.7 %copy-start.6 = (bf16[1024,1024]{1,0:T(8,128)(2,1)S(1)}, bf16[1024,1024]{1,0:T(8,128)(2,1)}, u32[]{:S(2)}) copy-start(bf16[1024,1024]{1,0:T(8,128)(2,1)} %param.18) | copy-start | bytes 6291460
  18.5 63.8 %all-to-all-start.1 = ((bf16[16,128,1024]{2,1,0:T(8,128)(2,1)}), bf16[16,128,1024]{2,1,0:T(8,128)(2,1)}, u32[]{:S(2)}, u32[]{:S(2)}) async-start(bf16[16,128,1024]{2,1,0:T(8,128)(2,1)} %gather_fusion), calls=%async_computation.1 | async-start | bytes 8388608 | tf_op jit(solution)/shard_map/all_to_all | solution.py:409
  23.2 3.7 %copy-start.4 = (bf16[1024,1024]{1,0:T(8,128)(2,1)S(1)}, bf16[1024,1024]{1,0:T(8,128)(2,1)}, u32[]{:S(2)}) copy-start(bf16[1024,1024]{1,0:T(8,128)(2,1)} %param.15) | copy-start | bytes 6291460
  23.2 3.7 %copy-start.8 = (bf16[512,1024]{1,0:T(8,128)(2,1)S(1)}, bf16[512,1024]{1,0:T(8,128)(2,1)}, u32[]{:S(2)}) copy-start(bf16[512,1024]{1,0:T(8,128)(2,1)} %param.10) | copy-start | bytes 3145732
  119.2 6.9 %collective-permute-start = (bf16[512,1024]{1,0:T(8,128)(2,1)}, bf16[512,1024]{1,0:T(8,128)(2,1)}, u32[]{:S(2)}, u32[]{:S(2)}) collective-permute-start(bf16[512,1024]{1,0:T(8,128)(2,1)} %get-tuple-element.18), channel_id=1, source_target_pairs={{0,1},{1,0},{2,3},{3,2},{4,5},{5,4},{6,7},{7,6},{8,9},{9,8},{10,11... | collective-permute-start | bytes 3145736 | tf_op jit(solution)/shard_map/ppermute | solution.py:370
  119.7 6.3 %copy-start.1 = (f32[512,1024]{1,0:T(8,128)S(1)}, f32[512,1024]{1,0:T(8,128)}, u32[]{:S(2)}) copy-start(f32[512,1024]{1,0:T(8,128)} %get-tuple-element.17) | copy-start | bytes 6291460
  119.7 41.2 %all-to-all-start.2 = ((bf16[16,64,1024]{2,1,0:T(8,128)(2,1)}), bf16[16,64,1024]{2,1,0:T(8,128)(2,1)}, u32[]{:S(2)}, u32[]{:S(2)}) async-start(bf16[16,64,1024]{2,1,0:T(8,128)(2,1)} %get-tuple-element.20), calls=%async_computation.2 | async-start | bytes 4194304 | tf_op jit(solution)/shard_map/all_to_all | solution.py:419
  126.1 7.9 %copy-start.2 = (bf16[1024,1024]{1,0:T(8,128)(2,1)S(1)}, bf16[1024,1024]{1,0:T(8,128)(2,1)}, u32[]{:S(2)}) copy-start(bf16[1024,1024]{1,0:T(8,128)(2,1)} %wk_hbm.1) | copy-start | bytes 6291460
  126.1 7.9 %copy-start.3 = (bf16[1024,1024]{1,0:T(8,128)(2,1)S(1)}, bf16[1024,1024]{1,0:T(8,128)(2,1)}, u32[]{:S(2)}) copy-start(bf16[1024,1024]{1,0:T(8,128)(2,1)} %wv_hbm.1) | copy-start | bytes 6291460
  128.0 14.0 %collective-permute-start.1 = (bf16[128,1024]{1,0:T(8,128)(2,1)S(1)}, bf16[128,1024]{1,0:T(8,128)(2,1)S(1)}, u32[]{:S(2)}, u32[]{:S(2)}) collective-permute-start(bf16[128,1024]{1,0:T(8,128)(2,1)S(1)} %get-tuple-element.24), channel_id=1, source_target_pairs={{0,2},{1,3},{2,4},{3,5},{4,6},{5,7},{6,0},{7,1},{8,10},{9,11},{10,... | collective-permute-start | bytes 786440 | tf_op jit(solution)/shard_map/ppermute | solution.py:361
  131.5 14.6 %collective-permute-start.2 = (bf16[128,1024]{1,0:T(8,128)(2,1)S(1)}, bf16[128,1024]{1,0:T(8,128)(2,1)S(1)}, u32[]{:S(2)}, u32[]{:S(2)}) collective-permute-start(bf16[128,1024]{1,0:T(8,128)(2,1)S(1)} %get-tuple-element.26), channel_id=1, source_target_pairs={{0,4},{1,5},{2,6},{3,7},{4,0},{5,1},{6,2},{7,3},{8,12},{9,13},{10,... | collective-permute-start | bytes 786440 | tf_op jit(solution)/shard_map/ppermute | solution.py:361
  133.9 12.1 %collective-permute-start.3 = (bf16[128,1024]{1,0:T(8,128)(2,1)S(1)}, bf16[128,1024]{1,0:T(8,128)(2,1)S(1)}, u32[]{:S(2)}, u32[]{:S(2)}) collective-permute-start(bf16[128,1024]{1,0:T(8,128)(2,1)S(1)} %get-tuple-element.25), channel_id=1, source_target_pairs={{0,6},{1,7},{2,0},{3,1},{4,2},{5,3},{6,4},{7,5},{8,14},{9,15},{10,... | collective-permute-start | bytes 786440 | tf_op jit(solution)/shard_map/ppermute | solution.py:361
  146.2 8.9 %collective-permute-start.4 = (bf16[32,1024]{1,0:T(8,128)(2,1)S(1)}, bf16[32,1024]{1,0:T(8,128)(2,1)S(1)}, u32[]{:S(2)}, u32[]{:S(2)}) collective-permute-start(bf16[32,1024]{1,0:T(8,128)(2,1)S(1)} %get-tuple-element.31), channel_id=1, source_target_pairs={{0,8},{8,16},{16,24},{24,0},{32,40},{40,48},{48,56},{56,32},{64,72... | collective-permute-start | bytes 196616 | tf_op jit(solution)/shard_map/ppermute | solution.py:364
  147.2 13.7 %collective-permute-start.5 = (bf16[32,1024]{1,0:T(8,128)(2,1)S(1)}, bf16[32,1024]{1,0:T(8,128)(2,1)S(1)}, u32[]{:S(2)}, u32[]{:S(2)}) collective-permute-start(bf16[32,1024]{1,0:T(8,128)(2,1)S(1)} %get-tuple-element.33), channel_id=1, source_target_pairs={{0,16},{8,24},{16,0},{24,8},{32,48},{40,56},{48,32},{56,40},{64,80... | collective-permute-start | bytes 196616 | tf_op jit(solution)/shard_map/ppermute | solution.py:364
  149.6 11.3 %collective-permute-start.6 = (bf16[32,1024]{1,0:T(8,128)(2,1)S(1)}, bf16[32,1024]{1,0:T(8,128)(2,1)S(1)}, u32[]{:S(2)}, u32[]{:S(2)}) collective-permute-start(bf16[32,1024]{1,0:T(8,128)(2,1)S(1)} %get-tuple-element.32), channel_id=1, source_target_pairs={{0,24},{8,0},{16,8},{24,16},{32,56},{40,32},{48,40},{56,48},{64,88... | collective-permute-start | bytes 196616 | tf_op jit(solution)/shard_map/ppermute | solution.py:364
  160.9 5.0 %collective-permute-start.7 = (bf16[32,1024]{1,0:T(8,128)(2,1)S(1)}, bf16[32,1024]{1,0:T(8,128)(2,1)S(1)}, u32[]{:S(2)}, u32[]{:S(2)}) collective-permute-start(bf16[32,1024]{1,0:T(8,128)(2,1)S(1)} %fusion.11), channel_id=1, source_target_pairs={{0,64},{32,96},{64,0},{96,32},{8,72},{40,104},{72,8},{104,40},{16,... | collective-permute-start | bytes 196616 | tf_op jit(solution)/shard_map/ppermute | solution.py:367
  163.3 4.6 %collective-permute-start.8 = (bf16[32,1024]{1,0:T(8,128)(2,1)S(1)}, bf16[32,1024]{1,0:T(8,128)(2,1)S(1)}, u32[]{:S(2)}, u32[]{:S(2)}) collective-permute-start(bf16[32,1024]{1,0:T(8,128)(2,1)S(1)} %fusion.11), channel_id=1, source_target_pairs={{0,32},{32,64},{64,96},{96,0},{8,40},{40,72},{72,104},{104,8},{16,... | collective-permute-start | bytes 196616 | tf_op jit(solution)/shard_map/ppermute | solution.py:367
  163.3 4.6 %collective-permute-start.9 = (bf16[32,1024]{1,0:T(8,128)(2,1)S(1)}, bf16[32,1024]{1,0:T(8,128)(2,1)S(1)}, u32[]{:S(2)}, u32[]{:S(2)}) collective-permute-start(bf16[32,1024]{1,0:T(8,128)(2,1)S(1)} %fusion.11), channel_id=1, source_target_pairs={{0,96},{32,0},{64,32},{96,64},{8,104},{40,8},{72,40},{104,72},{16,... | collective-permute-start | bytes 196616 | tf_op jit(solution)/shard_map/ppermute | solution.py:367
  167.9 5.1 %collective-permute-start.10 = (bf16[32,1024]{1,0:T(8,128)(2,1)S(1)}, bf16[32,1024]{1,0:T(8,128)(2,1)S(1)}, u32[]{:S(2)}, u32[]{:S(2)}) collective-permute-start(bf16[32,1024]{1,0:T(8,128)(2,1)S(1)} %add_convert_fusion), channel_id=1, source_target_pairs={{0,8},{8,16},{16,24},{24,0},{32,40},{40,48},{48,56},{56,32},{64,72... | collective-permute-start | bytes 196616 | tf_op jit(solution)/shard_map/ppermute | solution.py:364
  168.0 5.0 %collective-permute-start.11 = (bf16[32,1024]{1,0:T(8,128)(2,1)S(1)}, bf16[32,1024]{1,0:T(8,128)(2,1)S(1)}, u32[]{:S(2)}, u32[]{:S(2)}) collective-permute-start(bf16[32,1024]{1,0:T(8,128)(2,1)S(1)} %add_convert_fusion), channel_id=1, source_target_pairs={{0,16},{8,24},{16,0},{24,8},{32,48},{40,56},{48,32},{56,40},{64,80... | collective-permute-start | bytes 196616 | tf_op jit(solution)/shard_map/ppermute | solution.py:364
  169.5 4.0 %collective-permute-start.12 = (bf16[32,1024]{1,0:T(8,128)(2,1)S(1)}, bf16[32,1024]{1,0:T(8,128)(2,1)S(1)}, u32[]{:S(2)}, u32[]{:S(2)}) collective-permute-start(bf16[32,1024]{1,0:T(8,128)(2,1)S(1)} %add_convert_fusion), channel_id=1, source_target_pairs={{0,24},{8,0},{16,8},{24,16},{32,56},{40,32},{48,40},{56,48},{64,88... | collective-permute-start | bytes 196616 | tf_op jit(solution)/shard_map/ppermute | solution.py:364
  173.7 37.5 %all-to-all-start.3 = ((bf16[16,64,1024]{2,1,0:T(8,128)(2,1)}), bf16[16,64,1024]{2,1,0:T(8,128)(2,1)}, u32[]{:S(2)}, u32[]{:S(2)}) async-start(bf16[16,64,1024]{2,1,0:T(8,128)(2,1)} %bitcast.5), calls=%async_computation.3 | async-start | bytes 4194304 | tf_op jit(solution)/shard_map/all_to_all | solution.py:427
  179.4 9.6 %collective-permute-start.13 = (bf16[128,1024]{1,0:T(8,128)(2,1)S(1)}, bf16[128,1024]{1,0:T(8,128)(2,1)S(1)}, u32[]{:S(2)}, u32[]{:S(2)}) collective-permute-start(bf16[128,1024]{1,0:T(8,128)(2,1)S(1)} %get-tuple-element.35), channel_id=1, source_target_pairs={{0,2},{1,3},{2,4},{3,5},{4,6},{5,7},{6,0},{7,1},{8,10},{9,11},{10,... | collective-permute-start | bytes 786440 | tf_op jit(solution)/shard_map/ppermute | solution.py:361
  182.7 11.1 %collective-permute-start.14 = (bf16[128,1024]{1,0:T(8,128)(2,1)S(1)}, bf16[128,1024]{1,0:T(8,128)(2,1)S(1)}, u32[]{:S(2)}, u32[]{:S(2)}) collective-permute-start(bf16[128,1024]{1,0:T(8,128)(2,1)S(1)} %get-tuple-element.35), channel_id=1, source_target_pairs={{0,4},{1,5},{2,6},{3,7},{4,0},{5,1},{6,2},{7,3},{8,12},{9,13},{10,... | collective-permute-start | bytes 786440 | tf_op jit(solution)/shard_map/ppermute | solution.py:361
  186.0 7.8 %collective-permute-start.15 = (bf16[128,1024]{1,0:T(8,128)(2,1)S(1)}, bf16[128,1024]{1,0:T(8,128)(2,1)S(1)}, u32[]{:S(2)}, u32[]{:S(2)}) collective-permute-start(bf16[128,1024]{1,0:T(8,128)(2,1)S(1)} %get-tuple-element.35), channel_id=1, source_target_pairs={{0,6},{1,7},{2,0},{3,1},{4,2},{5,3},{6,4},{7,5},{8,14},{9,15},{10,... | collective-permute-start | bytes 786440 | tf_op jit(solution)/shard_map/ppermute | solution.py:361
  194.0 5.3 %copy-start.5 = (bf16[1024,1024]{1,0:T(8,128)(2,1)S(1)}, bf16[1024,1024]{1,0:T(8,128)(2,1)}, u32[]{:S(2)}) copy-start(bf16[1024,1024]{1,0:T(8,128)(2,1)} %param.15) | copy-start | bytes 6291460
  194.0 5.3 %copy-start.10 = (bf16[512,1024]{1,0:T(8,128)(2,1)S(1)}, bf16[512,1024]{1,0:T(8,128)(2,1)}, u32[]{:S(2)}) copy-start(bf16[512,1024]{1,0:T(8,128)(2,1)} %get-tuple-element.15) | copy-start | bytes 3145732
  194.2 15.3 %collective-permute-start.16 = (bf16[384,1024]{1,0:T(8,128)(2,1)S(1)}, bf16[384,1024]{1,0:T(8,128)(2,1)S(1)}, u32[]{:S(2)}, u32[]{:S(2)}) collective-permute-start(bf16[384,1024]{1,0:T(8,128)(2,1)S(1)} %pad_maximum_fusion.2), channel_id=1, source_target_pairs={{0,1},{1,0},{2,3},{3,2},{4,5},{5,4},{6,7},{7,6},{8,9},{9,8},{10,11... | collective-permute-start | bytes 2359304 | tf_op jit(solution)/shard_map/ppermute | solution.py:370
  199.3 2.3 %copy-start.7 = (bf16[1024,1024]{1,0:T(8,128)(2,1)S(1)}, bf16[1024,1024]{1,0:T(8,128)(2,1)}, u32[]{:S(2)}) copy-start(bf16[1024,1024]{1,0:T(8,128)(2,1)} %param.18) | copy-start | bytes 6291460
  199.3 2.3 %copy-start.9 = (bf16[512,1024]{1,0:T(8,128)(2,1)S(1)}, bf16[512,1024]{1,0:T(8,128)(2,1)}, u32[]{:S(2)}) copy-start(bf16[512,1024]{1,0:T(8,128)(2,1)} %get-tuple-element.14) | copy-start | bytes 3145732
  211.2 5.4 %collective-permute-start.17 = (bf16[128,1024]{1,0:T(8,128)(2,1)S(1)}, bf16[128,1024]{1,0:T(8,128)(2,1)S(1)}, u32[]{:S(2)}, u32[]{:S(2)}) collective-permute-start(bf16[128,1024]{1,0:T(8,128)(2,1)S(1)} %get-tuple-element.23), channel_id=1, source_target_pairs={{0,1},{1,0},{2,3},{3,2},{4,5},{5,4},{6,7},{7,6},{8,9},{9,8},{10,11... | collective-permute-start | bytes 786440 | tf_op jit(solution)/shard_map/ppermute | solution.py:370
